TPU v7x, 32 devices: a whole 2x2x4 slice. The times are simulated.
32 devices in a mesh: groups: 2 (over x), blk: 16 (over z, y, core).
Axes of the slice: x: 2, y: 2, z: 4, core: 2. Of those that a mesh axis runs over, the one named last changes fastest.
Arguments:
- spectrum: float32 [3, 36, 65536], P(None, None, ('groups', 'blk')), parts along dimension 2, may hold values from 0.1 to 2
- wind_vector: float32 [2, 65536], P(None, ('groups', 'blk')), parts along dimension 1, may hold values from -4 to 4
- dest_cell: int32 [65536], P(('groups', 'blk')), parts along dimension 0, may hold values from 0 to 32767, as said below
- counts: int32 [32], P(('groups', 'blk')), parts along dimension 0, may hold values from 1024 to 2048, as said below
- sea_mask: int32 [65536], P(('groups', 'blk')), parts along dimension 0, may hold values from 0 to 1, as said below
- dia_shift: int32 [2], replicated, may hold values from 1 to 9
Outputs:
- spectrum_next: float32 [3, 36, 65536], P(None, None, ('groups', 'blk')), parts along dimension 2
There are 2 independent parts, one for each index of `groups`. A program takes and returns all parts, laid end to end along the dimension named above; an argument that names none is the same for every part. Nothing has to cross between parts.
Inputs may be any that keep to these rules, and one draw needn't show every extreme that they name: Slots of block d below counts[d] hold sea points, the others are unused; some block has all 2048 slots live. `dest_cell`: distinct over all slots; cell c lies in band c // 2048. Of one block's live slots at most 128 name cells of one band, exactly 128 for some block and band, and some band receives 128 live points from every block. `sea_mask`: 1 exactly at the cells that live slots name.
All inputs are finite; a program needn't handle non-finite values.
Results may differ from a plain program's by a relative error of at most 0.0003.
Values sent between devices are 32-bit elements; how exact they have to be, the bound alone decides.
No kernel may reach another device: no remote copies, remote signals or barrier semaphores. Data moves between devices by JAX's collectives and lax.ppermute only.
A program may use at most 64 MiB of HBM per device.

v0:
```python
import math

import jax
import jax.numpy as jnp
from jax import lax
from jax.sharding import PartitionSpec as P

NLON = 512
SUBSTEPS = 2


def with_halo(block, sides, width):
    for axis, dim in sides:
        count = lax.axis_size(axis)
        forward = [(i, i + 1) for i in range(count - 1)]
        backward = [(target, source) for source, target in forward]
        low = lax.ppermute(
            lax.slice_in_dim(block, block.shape[dim] - width, None, axis=dim), axis, forward
        )
        high = lax.ppermute(lax.slice_in_dim(block, 0, width, axis=dim), axis, backward)
        block = jnp.concatenate([low, block, high], axis=dim)
    return block


def source_terms(spectra, wind_field, dia_shift, energy_mean, frequency):
    count_dirs = spectra.shape[1]
    angles = (
        2.0 * math.pi * jnp.arange(count_dirs, dtype=jnp.int32).astype(jnp.float32) / count_dirs
    )
    along_wind = (
        wind_field[0][None, :] * jnp.cos(angles)[:, None]
        + wind_field[1][None, :] * jnp.sin(angles)[:, None]
    )
    growth = (0.15 + 0.05 * frequency)[:, None, None] * jnp.maximum(along_wind - 0.3, 0.0)[None]
    decay_rate = (0.2 + 0.1 * frequency)[:, None, None] * energy_mean[None, None, :]
    quadruplet = 0.1 * (
        jnp.roll(spectra, -dia_shift[0], axis=1) * jnp.roll(spectra, dia_shift[1], axis=1)
        - spectra * spectra
    )
    return spectra * jnp.exp(growth - decay_rate) + quadruplet


def advance(wave_field, south_rows, north_rows, latitude, frequency, sea_field):
    count_dirs = wave_field.shape[1]
    angles = (
        2.0 * math.pi * jnp.arange(count_dirs, dtype=jnp.int32).astype(jnp.float32) / count_dirs
    )
    group_speed = 1.0 / (1.0 + 0.25 * frequency)
    lat_courant = (0.5 * group_speed[:, None] * jnp.sin(angles)[None, :])[:, :, None, None]
    lon_courant = (
        0.25
        * group_speed[:, None, None]
        * jnp.cos(angles)[None, :, None]
        / jnp.cos(latitude)[None, None, :]
    )[:, :, :, None]
    turn_courant = (
        -0.3
        * group_speed[:, None, None]
        * jnp.cos(angles)[None, :, None]
        * jnp.tan(latitude)[None, None, :]
    )[:, :, :, None]
    west_side = jnp.roll(wave_field, 1, axis=3)
    east_side = jnp.roll(wave_field, -1, axis=3)
    advected = wave_field - (
        jnp.maximum(lat_courant, 0.0) * (wave_field - south_rows)
        + jnp.minimum(lat_courant, 0.0) * (north_rows - wave_field)
    )
    advected = advected - (
        jnp.maximum(lon_courant, 0.0) * (wave_field - west_side)
        + jnp.minimum(lon_courant, 0.0) * (east_side - wave_field)
    )
    advected = advected * sea_field
    lower_dir = jnp.roll(advected, 1, axis=1)
    upper_dir = jnp.roll(advected, -1, axis=1)
    turned = advected - (
        jnp.maximum(turn_courant, 0.0) * (advected - lower_dir)
        + jnp.minimum(turn_courant, 0.0) * (upper_dir - advected)
    )
    return turned * sea_field


def block_width(total):
    return math.gcd(total, 256)


def place_columns(data, index, width):
    step = block_width(width)
    block_count = width // step

    def place_one_block(block_id):
        columns = block_id * step + jnp.arange(step, dtype=jnp.int32)
        table = (index[:, None] == columns[None, :]).astype(jnp.float32)
        return jnp.dot(data, table, precision=lax.Precision.HIGHEST)

    pieces = lax.map(place_one_block, jnp.arange(block_count, dtype=jnp.int32))
    return jnp.moveaxis(pieces, 0, 1).reshape(data.shape[0], width)


def pick_columns(data, index):
    total = index.shape[0]
    width = data.shape[1]
    step = block_width(total)
    block_count = total // step
    columns = jnp.arange(width, dtype=jnp.int32)

    def pick_one_block(block_id):
        wanted = lax.dynamic_slice_in_dim(index, block_id * step, step)
        table = (wanted[:, None] == columns[None, :]).astype(jnp.float32)
        return lax.dot_general(
            data, table, (((1,), (1,)), ((), ())), precision=lax.Precision.HIGHEST
        )

    pieces = lax.map(pick_one_block, jnp.arange(block_count, dtype=jnp.int32))
    return jnp.moveaxis(pieces, 0, 1).reshape(data.shape[0], total)


def earlier_counts(hits):
    total = hits.shape[0]
    step = block_width(total)
    block_count = total // step
    slot_ids = jnp.arange(total, dtype=jnp.int32)

    def earlier_one_block(block_id):
        rows = block_id * step + jnp.arange(step, dtype=jnp.int32)
        lower = (rows[:, None] >= slot_ids[None, :]).astype(jnp.bfloat16)
        return jnp.dot(lower, hits, preferred_element_type=jnp.float32)

    pieces = lax.map(earlier_one_block, jnp.arange(block_count, dtype=jnp.int32))
    return pieces.reshape(total, hits.shape[1])


def per_device(spectrum, wind_vector, dest_cell, counts, sea_mask, dia_shift):
    blocks = lax.axis_size("blk")
    band_index = lax.axis_index("blk")
    count_freq = spectrum.shape[0]
    count_dirs = spectrum.shape[1]
    points = spectrum.shape[2]
    slot_cap = points // blocks
    row_count = points // NLON
    live_slot = jnp.arange(points, dtype=jnp.int32) < counts[0]
    frequencies = jnp.arange(count_freq, dtype=jnp.int32).astype(jnp.float32)
    sourced = source_terms(
        spectrum, wind_vector, dia_shift, jnp.mean(spectrum, axis=(0, 1)), frequencies
    )
    target_band = dest_cell // points
    local_cell = dest_cell % points
    hit_table = (target_band[:, None] == jnp.arange(blocks, dtype=jnp.int32)[None, :]) & live_slot[
        :, None
    ]
    running = earlier_counts(hit_table.astype(jnp.bfloat16))
    ranking = jnp.sum(running * hit_table.astype(jnp.float32), axis=1).astype(jnp.int32) - 1
    position = jnp.where(live_slot, target_band * slot_cap + ranking, blocks * slot_cap)
    stacked = jnp.concatenate(
        [
            sourced.reshape(count_freq * count_dirs, points),
            (local_cell.astype(jnp.float32) + 1.0)[None, :],
        ],
        axis=0,
    )
    placed_rows = place_columns(stacked, position, blocks * slot_cap)
    outgoing = placed_rows[:-1].reshape(count_freq, count_dirs, blocks, slot_cap)
    cell_slots = (placed_rows[-1] - 1.0).reshape(1, 1, blocks, slot_cap)
    labels = jnp.concatenate(
        [
            jnp.broadcast_to(cell_slots, (count_freq, 1, blocks, slot_cap)),
            jnp.broadcast_to(frequencies[:, None, None, None], (count_freq, 1, blocks, slot_cap)),
        ],
        axis=1,
    )
    rows_all = row_count * blocks
    row_ids = band_index * row_count + jnp.arange(row_count, dtype=jnp.int32)
    latitude = (row_ids.astype(jnp.float32) + 0.5) / rows_all * (
        2.0 * math.pi / 3.0
    ) - math.pi / 3.0
    sea_field = sea_mask.astype(jnp.float32).reshape(row_count, NLON)
    arrived, tag_rows = (
        lax.all_to_all(outgoing, "blk", split_axis=2, concat_axis=2, tiled=True),
        lax.all_to_all(labels, "blk", split_axis=2, concat_axis=2, tiled=True),
    )
    item_count = arrived.shape[0]
    cell_ids = tag_rows[0, 0].astype(jnp.int32).reshape(-1)
    item_freq = tag_rows[:, 1, 0, 0]
    flat_arrived = arrived.reshape(item_count * count_dirs, blocks * slot_cap)
    wave_field = place_columns(flat_arrived, cell_ids, points)
    wave_field = wave_field.reshape(item_count, count_dirs, row_count, NLON)
    for substep in range(SUBSTEPS):
        padded = with_halo(wave_field, (("blk", 2),), 1)
        wave_field = advance(
            wave_field, padded[:, :, :-2], padded[:, :, 2:], latitude, item_freq, sea_field
        )
    picked = pick_columns(wave_field.reshape(item_count * count_dirs, points), cell_ids)
    returned = lax.all_to_all(
        picked.reshape(item_count, count_dirs, blocks, slot_cap),
        "blk",
        split_axis=2,
        concat_axis=2,
        tiled=True,
    )
    merged_back = returned.reshape(count_freq * count_dirs, blocks * slot_cap)
    result = pick_columns(merged_back, position)
    return result.reshape(count_freq, count_dirs, points)


def solution(mesh):
    placed = (
        P(None, None, ("groups", "blk")),
        P(None, ("groups", "blk")),
        P(("groups", "blk")),
        P(("groups", "blk")),
        P(("groups", "blk")),
        P(),
    )
    return jax.shard_map(
        per_device,
        mesh=mesh,
        in_specs=placed,
        out_specs=P(None, None, ("groups", "blk")),
        check_vma=False,
    )
```

profile of v0, /device:TPU:1, one launch (start us, length us, event | category | flops | bytes accessed | tf_op | source)
XLA Modules:
  0.0 210.0 jit_solution(16062555036161799481)
XLA Ops:
  0.0 1.3 fusion.105
  8.3 18.9 %while.60 = (s32[]{:T(128)}, f32[8,256,16]{1,2,0:T(8,128)S(1)}, s32[8]{0:T(128)S(1)}, s32[2048]{0:T(1024)S(1)}, pred[2048]{0:T(1024)(128)(4,1)S(1)}, /*index=5*/s32[1]{0:T(128)}) while((s32[]{:T(128)}, f32[8,256,16]{1,2,0:T(8,128)S(1)}, s32[8]{0:T(128)S(1)}, s32[2048]{0:T(1024)S(1)}, pred[2048]{0:T(1024)(128)(4,1)S(1)}, ...), condition=%wide.region_1.2_spmd.clone.clone, body=%wide.region_0.0_spmd.clone.sunk.clone | while | flops 17400068 | bytes 28773 | solution.py:128
  27.9 16.8 %while.58 = (s32[]{:T(128)}, f32[8,109,256]{2,1,0:T(8,128)S(1)}, s32[2048]{0:T(1024)S(1)}, s32[8]{0:T(128)S(1)}, f32[109,2048]{1,0:T(8,128)S(1)}, /*index=5*/s32[1]{0:T(128)}) while((s32[]{:T(128)}, f32[8,109,256]{2,1,0:T(8,128)S(1)}, s32[2048]{0:T(1024)S(1)}, s32[8]{0:T(128)S(1)}, f32[109,2048]{1,0:T(8,128)S(1)}, ...), condition=%wide.region_5.7_spmd.clone, body=%wide.region_4.6_spmd.sunk.clone | while | flops 686293248 | bytes 1042533 | solution.py:95
  45.5 7.3 %all-to-all-start = ((f32[3,2,16,128]{3,1,0,2:T(2,128)}), f32[3,2,16,128]{3,1,0,2:T(2,128)S(1)}, u32[]{:S(2)}, u32[]{:S(2)}) async-start(f32[3,2,16,128]{3,1,0,2:T(2,128)} %pad_maximum_fusion.5), calls=%async_computation | async-start | bytes 98304 | tf_op jit(solution)/shard_map/all_to_all | solution.py:178
  54.7 4.2 %all-to-all-done = f32[3,2,16,128]{3,1,0,2:T(2,128)S(1)} async-done(((f32[3,2,16,128]{3,1,0,2:T(2,128)}), f32[3,2,16,128]{3,1,0,2:T(2,128)S(1)}, u32[]{:S(2)}, u32[]{:S(2)}) %all-to-all-start) | async-done | bytes 49184 | tf_op jit(solution)/shard_map/all_to_all | solution.py:178
  58.9 4.3 %all-to-all-start.1 = ((f32[3,36,16,128]{3,1,0,2:T(8,128)}), f32[3,36,16,128]{3,1,0,2:T(8,128)S(1)}, u32[]{:S(2)}, u32[]{:S(2)}) async-start(f32[3,36,16,128]{3,1,0,2:T(8,128)} %copy.19), calls=%async_computation.1 | async-start | bytes 1966080 | tf_op jit(solution)/shard_map/all_to_all | solution.py:177
  63.7 21.5 %all-to-all-done.1 = f32[3,36,16,128]{3,1,0,2:T(8,128)S(1)} async-done(((f32[3,36,16,128]{3,1,0,2:T(8,128)}), f32[3,36,16,128]{3,1,0,2:T(8,128)S(1)}, u32[]{:S(2)}, u32[]{:S(2)}) %all-to-all-start.1) | async-done | bytes 884768 | tf_op jit(solution)/shard_map/all_to_all | solution.py:177
  85.8 17.5 %while.59 = (s32[]{:T(128)}, f32[8,108,256]{2,1,0:T(8,128)S(1)}, s32[16,128]{1,0:T(8,128)S(1)}, s32[8]{0:T(128)S(1)}, f32[108,2048]{1,0:T(8,128)S(1)}, /*index=5*/s32[1]{0:T(128)}) while((s32[]{:T(128)}, f32[8,108,256]{2,1,0:T(8,128)S(1)}, s32[16,128]{1,0:T(8,128)S(1)}, s32[8]{0:T(128)S(1)}, f32[108,2048]{1,0:T(8,128)S(1)}, ...), condition=%wide.region_7.9_spmd.clone, body=%wide.region_6.8_spmd.sunk.clone | while | flops 680001792 | bytes 1042533 | solution.py:95
  105.2 3.1 %collective-permute-start = (f32[3,36,1,512]{3,2,1,0:T(1,128)S(1)}, f32[3,36,1,512]{3,2,1,0:T(1,128)S(1)}, u32[]{:S(2)}, u32[]{:S(2)}) collective-permute-start(f32[3,36,1,512]{3,2,1,0:T(1,128)S(1)} %get-tuple-element.266), channel_id=1, source_target_pairs={{0,1},{1,2},{2,3},{3,4},{4,5},{5,6},{6,7},{7,8},{8,9},{9,10},{10,1... | collective-permute-start | bytes 663560 | tf_op jit(solution)/shard_map/ppermute | solution.py:17
  108.3 1.9 collective-permute-start.1
  111.2 4.4 %collective-permute-done.1 = f32[3,36,1,512]{3,2,1,0:T(1,128)S(1)} collective-permute-done((f32[3,36,1,512]{3,2,1,0:T(1,128)S(1)}, f32[3,36,1,512]{3,2,1,0:T(1,128)S(1)}, u32[]{:S(2)}, u32[]{:S(2)}) %collective-permute-start.1) | collective-permute-done | bytes 221216 | tf_op jit(solution)/shard_map/ppermute | solution.py:20
  115.6 2.2 %fusion.64 = f32[3,36,4,512]{3,2,1,0:T(4,128)S(1)} fusion(f32[3,36,4,512]{3,2,1,0:T(4,128)S(1)} %reshape_reshape.9, f32[3,36,1,512]{3,2,1,0:T(1,128)S(1)} %collective-permute-done.1, f32[3,36,1,512]{3,2,1,0:T(1,128)S(1)} %collective-permute-done, f32[3,36,4,511]{3,2,1,0:T(4,128)S(1)} %get-tuple-element.263, f32[3,36,4,1]{3,2,1,0:T(4,128)S(1)} %get-tuple-element.265, ...), kind=kLoop, calls=%fused_computation.66 | loop fusion | flops 3760128 | bytes 3993824 | tf_op jit(solution)/shard_map/mul | solution.py:72
  119.5 1.9 collective-permute-start.2
  121.5 2.6 %collective-permute-start.3 = (f32[3,36,1,512]{3,2,1,0:T(1,128)S(1)}, f32[3,36,1,512]{3,2,1,0:T(1,128)S(1)}, u32[]{:S(2)}, u32[]{:S(2)}) collective-permute-start(f32[3,36,1,512]{3,2,1,0:T(1,128)S(1)} %get-tuple-element.257), channel_id=1, source_target_pairs={{1,0},{2,1},{3,2},{4,3},{5,4},{6,5},{7,6},{8,7},{9,8},{10,9},{11,1... | collective-permute-start | bytes 663560 | tf_op jit(solution)/shard_map/ppermute | solution.py:20
  124.3 6.4 %collective-permute-done.3 = f32[3,36,1,512]{3,2,1,0:T(1,128)S(1)} collective-permute-done((f32[3,36,1,512]{3,2,1,0:T(1,128)S(1)}, f32[3,36,1,512]{3,2,1,0:T(1,128)S(1)}, u32[]{:S(2)}, u32[]{:S(2)}) %collective-permute-start.3) | collective-permute-done | bytes 221216 | tf_op jit(solution)/shard_map/ppermute | solution.py:20
  130.8 2.2 %fusion.56 = f32[3,36,4,512]{3,2,1,0:T(4,128)S(1)} fusion(f32[3,36,4,512]{3,2,1,0:T(4,128)S(1)} %fusion.73, f32[3,36,1,512]{3,2,1,0:T(1,128)S(1)} %collective-permute-done.3, f32[3,36,1,512]{3,2,1,0:T(1,128)S(1)} %collective-permute-done.2, f32[3,36,4,511]{3,2,1,0:T(4,128)S(1)} %get-tuple-element.253, f32[3,36,4,1]{3,2,1,0:T(4,128)S(1)} %get-tuple-element.255, ...), kind=kLoop, calls=%fused_computation.56 | loop fusion | flops 3760128 | bytes 3993824 | tf_op jit(solution)/shard_map/mul | solution.py:72
  134.4 21.4 %while.61 = (s32[]{:T(128)}, f32[8,108,256]{2,1,0:T(8,128)S(1)}, s32[8]{0:T(128)S(1)}, s32[2048]{0:T(1024)S(1)}, f32[108,2048]{1,0:T(8,128)S(1)}, /*index=5*/s32[1]{0:T(128)}) while((s32[]{:T(128)}, f32[8,108,256]{2,1,0:T(8,128)S(1)}, s32[8]{0:T(128)S(1)}, s32[2048]{0:T(1024)S(1)}, f32[108,2048]{1,0:T(8,128)S(1)}, ...), condition=%wide.region_9.11_spmd.clone.clone, body=%wide.region_8.10_spmd.clone.sunk.clone | while | flops 680001536 | bytes 1035399 | solution.py:113
  135.8 1.3 fusion.143
  143.8 1.3 fusion.143
  151.9 1.3 fusion.143
  156.8 29.6 %all_to_all.15 = f32[3,36,16,128]{3,1,0,2:T(8,128)S(1)} all-to-all(f32[3,36,16,128]{3,1,0,2:T(8,128)S(1)} %copy.23), channel_id=1, replica_groups=mesh['groups'=2,'blk'=16] {'blk'}, dimensions={2} | all-to-all | bytes 1769472 | tf_op jit(solution)/shard_map/all_to_all | solution.py:192
  187.0 21.4 %while.62 = (s32[]{:T(128)}, f32[8,108,256]{2,1,0:T(8,128)S(1)}, s32[8]{0:T(128)S(1)}, s32[2048]{0:T(1024)S(1)}, f32[108,2048]{1,0:T(8,128)S(1)}, /*index=5*/s32[1]{0:T(128)}) while((s32[]{:T(128)}, f32[8,108,256]{2,1,0:T(8,128)S(1)}, s32[8]{0:T(128)S(1)}, s32[2048]{0:T(1024)S(1)}, f32[108,2048]{1,0:T(8,128)S(1)}, ...), condition=%wide.region_11.13_spmd.clone.clone, body=%wide.region_10.12_spmd.clone.sunk.clone | while | flops 680001536 | bytes 1035399 | solution.py:113
  199.0 1.3 fusion.145
  207.0 1.3 fusion.145
  (197 shorter events, 81.7 us)
Async XLA Ops:
  0.0 6.4 %copy-start = (f32[3,36,2048]{2,1,0:T(8,128)S(1)}, f32[3,36,2048]{2,1,0:T(8,128)}, u32[]{:S(2)}) copy-start(f32[3,36,2048]{2,1,0:T(8,128)} %param.18) | copy-start | bytes 2654212
  27.2 0.7 copy-start.1
  45.5 13.3 %all-to-all-start = ((f32[3,2,16,128]{3,1,0,2:T(2,128)}), f32[3,2,16,128]{3,1,0,2:T(2,128)S(1)}, u32[]{:S(2)}, u32[]{:S(2)}) async-start(f32[3,2,16,128]{3,1,0,2:T(2,128)} %pad_maximum_fusion.5), calls=%async_computation | async-start | bytes 98304 | tf_op jit(solution)/shard_map/all_to_all | solution.py:178
  54.7 8.5 %copy-start.2 = (s32[2048]{0:T(1024)S(1)}, s32[2048]{0:T(1024)}, u32[]{:S(2)}) copy-start(s32[2048]{0:T(1024)} %param.22) | copy-start | bytes 24580
  58.9 26.3 %all-to-all-start.1 = ((f32[3,36,16,128]{3,1,0,2:T(8,128)}), f32[3,36,16,128]{3,1,0,2:T(8,128)S(1)}, u32[]{:S(2)}, u32[]{:S(2)}) async-start(f32[3,36,16,128]{3,1,0,2:T(8,128)} %copy.19), calls=%async_computation.1 | async-start | bytes 1966080 | tf_op jit(solution)/shard_map/all_to_all | solution.py:177
  105.2 6.0 %collective-permute-start = (f32[3,36,1,512]{3,2,1,0:T(1,128)S(1)}, f32[3,36,1,512]{3,2,1,0:T(1,128)S(1)}, u32[]{:S(2)}, u32[]{:S(2)}) collective-permute-start(f32[3,36,1,512]{3,2,1,0:T(1,128)S(1)} %get-tuple-element.266), channel_id=1, source_target_pairs={{0,1},{1,2},{2,3},{3,4},{4,5},{5,6},{6,7},{7,8},{8,9},{9,10},{10,1... | collective-permute-start | bytes 663560 | tf_op jit(solution)/shard_map/ppermute | solution.py:17
  108.3 7.3 %collective-permute-start.1 = (f32[3,36,1,512]{3,2,1,0:T(1,128)S(1)}, f32[3,36,1,512]{3,2,1,0:T(1,128)S(1)}, u32[]{:S(2)}, u32[]{:S(2)}) collective-permute-start(f32[3,36,1,512]{3,2,1,0:T(1,128)S(1)} %get-tuple-element.267), channel_id=1, source_target_pairs={{1,0},{2,1},{3,2},{4,3},{5,4},{6,5},{7,6},{8,7},{9,8},{10,9},{11,1... | collective-permute-start | bytes 663560 | tf_op jit(solution)/shard_map/ppermute | solution.py:20
  119.5 4.8 %collective-permute-start.2 = (f32[3,36,1,512]{3,2,1,0:T(1,128)S(1)}, f32[3,36,1,512]{3,2,1,0:T(1,128)S(1)}, u32[]{:S(2)}, u32[]{:S(2)}) collective-permute-start(f32[3,36,1,512]{3,2,1,0:T(1,128)S(1)} %get-tuple-element.256), channel_id=1, source_target_pairs={{0,1},{1,2},{2,3},{3,4},{4,5},{5,6},{6,7},{7,8},{8,9},{9,10},{10,1... | collective-permute-start | bytes 663560 | tf_op jit(solution)/shard_map/ppermute | solution.py:17
  121.5 9.3 %collective-permute-start.3 = (f32[3,36,1,512]{3,2,1,0:T(1,128)S(1)}, f32[3,36,1,512]{3,2,1,0:T(1,128)S(1)}, u32[]{:S(2)}, u32[]{:S(2)}) collective-permute-start(f32[3,36,1,512]{3,2,1,0:T(1,128)S(1)} %get-tuple-element.257), channel_id=1, source_target_pairs={{1,0},{2,1},{3,2},{4,3},{5,4},{6,5},{7,6},{8,7},{9,8},{10,9},{11,1... | collective-permute-start | bytes 663560 | tf_op jit(solution)/shard_map/ppermute | solution.py:20
where the time goes:
time: 211 us; the launch traced here: 210 us
  matrix products  45 us (21%)
  local copies, waits for them, and re-layouts  37.3 us (18%)
  waiting for transfers between devices  37.3 us (18%)
  blocking collectives  29.6 us (14%)
  loops' own time  26.2 us (12%)
  starting transfers between devices  21.2 us (10%)
  other arithmetic  11 us (5%)
  between operations  2.39 us (1%)
    all_to_all x1, blocking collectives, per_device(): lax.all_to_all(picked.reshape(item_count, count_dirs, blocks, slot_cap),...  29.6 us
    dynamic_slice x40, local copies, waits for them, and re-layouts, earlier_counts(): lax.map(earlier_one_block, jnp.arange(block_count, dtype=jnp.int32))  23.6 us
    all_to_all x1, waiting for transfers between devices, per_device(): lax.all_to_all(outgoing, 'blk', split_axis=2, concat_axis=2, tiled=True)  21.5 us
    dot_general x16, matrix products, pick_one_block(): lax.dot_general(data, table, (((1,), (1,)), ((), ())), precision=lax.Prec...  21.4 us
    dot_general x16, matrix products, place_one_block(): return jnp.dot(data, table, precision=lax.Precision.HIGHEST)  14.7 us
    another operation x2, loops' own time, pick_columns(): pieces = lax.map(pick_one_block, jnp.arange(block_count, dtype=jnp.int32))  10.9 us
    ppermute x2, waiting for transfers between devices, with_halo(): lax.ppermute(lax.slice_in_dim(block, 0, width, axis=dim), axis, backward)  10.8 us
    another operation x2, loops' own time, place_columns(): pieces = lax.map(place_one_block, jnp.arange(block_count, dtype=jnp.int32))  10.2 us
  transfers between devices with their start and end apart: 6, of which 6 were waited for; matrix products, arithmetic and copies ran while one was open for 1% of the time, Pallas kernels for 0%

commit v1 on v0

v1 whole, which is shorter than its diff:
```python
import functools
import math

import jax
import jax.numpy as jnp
from jax import lax
from jax.experimental import pallas as pl
from jax.experimental.pallas import tpu as pltpu
from jax.sharding import PartitionSpec as P

NLON = 512
SUBSTEPS = 2
LANES = 128
TILE = 256
STRIDE = 40
F32 = jnp.float32
BF16 = jnp.bfloat16
VMEM_LIMIT = 48 * 1024 * 1024


def snake_row(blocks):
    chips = max(blocks // 2, 1)
    return 1 << ((chips.bit_length() - 1) // 2)


def snake(index, blocks):
    row = snake_row(blocks)
    if blocks % (2 * row):
        return index
    core = lax.rem(index, 2)
    chip = lax.div(index, 2)
    line = lax.div(chip, row)
    place = lax.rem(chip, row)
    place = jnp.where(lax.rem(line, 2) == 1, row - 1 - place, place)
    return (line * row + place) * 2 + core


def halo_pairs(blocks):
    row = snake_row(blocks)
    order = []
    for band in range(blocks):
        if blocks % (2 * row):
            order.append(band)
            continue
        core, chip = band % 2, band // 2
        line, place = chip // row, chip % row
        if line % 2:
            place = row - 1 - place
        order.append((line * row + place) * 2 + core)
    up = [(order[b], order[b + 1]) for b in range(blocks - 1)]
    return up, [(t, s) for s, t in up]


def column(values):
    return jnp.concatenate([jnp.full((1, 1), float(v), F32) for v in values], axis=0)


def split(x):
    high = x.astype(BF16)
    return high, (x - high.astype(F32)).astype(BF16)


def one_hot(row, start, width):
    ids = lax.broadcasted_iota(jnp.int32, (TILE, width), 0)
    return (ids == (row - start)).astype(F32).astype(BF16)


def matmul_nt(data, table):
    return lax.dot_general(
        data, table, (((1,), (1,)), ((), ())), preferred_element_type=F32
    )


def direction_trig(dirs, rows):
    j = lax.broadcasted_iota(jnp.int32, (rows, LANES), 0)
    angles = (2.0 * math.pi / dirs) * j.astype(F32)
    return jnp.cos(angles), jnp.sin(angles)


def source_kernel(
    blocks, cap, shift_ref, count_ref, spec_ref, wind_ref, dest_ref, send_ref, pos_ref, dbl, lhs
):
    freqs, dirs, points = spec_ref.shape
    rows = lhs.shape[0] // 2
    dest = dest_ref[...]
    slot = lax.broadcasted_iota(jnp.int32, (1, points), 1)
    live = slot < count_ref[0]
    band = lax.shift_right_logical(dest, points.bit_length() - 1)
    band = jnp.where(live, band, -1)
    owner_band = snake(lax.broadcasted_iota(jnp.int32, (blocks, 1), 0), blocks)
    hits = (band == owner_band).astype(F32)
    tri_r = lax.broadcasted_iota(jnp.int32, (LANES, LANES), 0)
    tri_c = lax.broadcasted_iota(jnp.int32, (LANES, LANES), 1)
    upper = (tri_r <= tri_c).astype(F32).astype(BF16)
    ones = jnp.ones((LANES, LANES), BF16)
    base = (lax.broadcasted_iota(jnp.int32, (blocks, LANES), 0) * cap).astype(F32)
    for c in range(points // LANES):
        piece = hits[:, c * LANES : (c + 1) * LANES]
        packed = piece.astype(BF16)
        running = jnp.dot(packed, upper, preferred_element_type=F32) + base
        base = base + jnp.dot(packed, ones, preferred_element_type=F32)
        where_to = jnp.sum(piece * running, axis=0, keepdims=True) - 1.0
        pos_ref[:, c * LANES : (c + 1) * LANES] = where_to.astype(jnp.int32)
    total = jnp.zeros((1, points), F32)
    for f in range(freqs):
        x = spec_ref[f]
        dbl[f, 0:dirs, :] = x
        dbl[f, dirs : 2 * dirs, :] = x
        total = total + jnp.sum(x, axis=0, keepdims=True)
    mean = total * (1.0 / (freqs * dirs))
    cos_a, sin_a = direction_trig(dirs, dirs)
    along = wind_ref[0:1, :] * cos_a[:, 0:1] + wind_ref[1:2, :] * sin_a[:, 0:1]
    drive = jnp.maximum(along - 0.3, 0.0)
    for f in range(freqs):
        x = spec_ref[f]
        twice = dbl[f]
        ahead = pltpu.roll(twice, 2 * dirs - shift_ref[0], 0)[0:dirs]
        behind = pltpu.roll(twice, shift_ref[1], 0)[0:dirs]
        out = x * jnp.exp((0.15 + 0.05 * f) * drive - (0.2 + 0.1 * f) * mean) + 0.1 * (
            ahead * behind - x * x
        )
        dbl[f, 0:dirs, :] = out
    extra = rows - freqs * dirs
    local = (lax.bitwise_and(dest, points - 1) + 1).astype(F32)
    whole = jnp.concatenate(
        [dbl[f, 0:dirs, :] for f in range(freqs)] + [jnp.broadcast_to(local, (extra, points))],
        axis=0,
    )
    high, low = split(whole)
    lhs[0:rows, :] = high
    lhs[rows : 2 * rows, :] = low
    pos = pos_ref[...]

    def body(t, carry):
        table = one_hot(pos, t * TILE, points)
        both = matmul_nt(lhs[...], table)
        out = both[0:rows] + both[rows : 2 * rows]
        for h in range(TILE // LANES):
            send_ref[t * (TILE // LANES) + h] = out[:, h * LANES : (h + 1) * LANES]
        return carry

    lax.fori_loop(0, points // TILE, body, 0)


def spread_rows(get, freqs, dirs, points, lhs):
    rows = lhs.shape[0] // 2
    fill = jnp.ones((STRIDE - dirs - 2, LANES), F32)
    for c in range(points // LANES):
        x = get(c)
        pieces = []
        for f in range(freqs):
            one = x[f * dirs : (f + 1) * dirs]
            pieces += [one, one[0:1], fill, one[dirs - 1 : dirs]]
        high, low = split(jnp.concatenate(pieces, axis=0))
        lhs[0:rows, c * LANES : (c + 1) * LANES] = high
        lhs[rows : 2 * rows, c * LANES : (c + 1) * LANES] = low


def place_kernel(freqs, dirs, recv_ref, field_ref, up_ref, down_ref, cell_ref, lhs):
    points = cell_ref.shape[1]
    rows = freqs * STRIDE
    label = freqs * dirs
    for c in range(points // LANES):
        cell_ref[:, c * LANES : (c + 1) * LANES] = (
            recv_ref[c, label : label + 1, :].astype(jnp.int32) - 1
        )
    spread_rows(lambda c: recv_ref[c], freqs, dirs, points, lhs)
    cells = cell_ref[...]

    def body(t, carry):
        table = one_hot(cells, t * TILE, points)
        both = matmul_nt(lhs[...], table)
        where = pl.ds(pl.multiple_of(t * TILE, TILE), TILE)
        field_ref[:, where] = both[0:rows] + both[rows : 2 * rows]
        return carry

    lax.fori_loop(0, points // TILE, body, 0)
    half = dirs // 2
    width = half + 1
    edge = up_ref.shape[1]
    for f in range(freqs):
        top = field_ref[f * STRIDE : f * STRIDE + width, points - edge : points]
        up_ref[f * width : (f + 1) * width, :] = top
        low = field_ref[f * STRIDE + half : f * STRIDE + half + width, 0:edge]
        down_ref[f * width : (f + 1) * width, :] = low
    left = up_ref.shape[0] - freqs * width
    mask = field_ref[dirs + 1 : dirs + 2, :]
    up_ref[freqs * width :, :] = jnp.broadcast_to(mask[:, points - edge : points], (left, edge))
    down_ref[freqs * width :, :] = jnp.broadcast_to(mask[:, 0:edge], (left, edge))


def roll_lanes(x, shift):
    return pltpu.roll(x, shift % x.shape[1], 1)


def step_kernel(
    freqs, dirs, blocks, field_ref, south_ref, north_ref, cell_ref, back_ref, ext, mid, lhs
):
    points = field_ref.shape[1]
    rows = freqs * STRIDE
    row_count = points // NLON
    half = dirs // 2
    width = half + 1
    ghost = SUBSTEPS
    band = snake(lax.axis_index("blk"), blocks)
    rows_all = row_count * blocks

    def lanes(row):
        return slice(row * NLON, (row + 1) * NLON)

    ext[:, 0 : ghost * NLON] = jnp.zeros((rows, ghost * NLON), F32)
    ext[:, (ghost + row_count) * NLON :] = jnp.zeros((rows, ghost * NLON), F32)
    ext[:, ghost * NLON : (ghost + row_count) * NLON] = field_ref[...]
    for f in range(freqs):
        ext[f * STRIDE : f * STRIDE + width, 0 : ghost * NLON] = south_ref[
            f * width : (f + 1) * width, :
        ]
        ext[f * STRIDE + half : f * STRIDE + half + width, (ghost + row_count) * NLON :] = (
            north_ref[f * width : (f + 1) * width, :]
        )
        spot = f * width + dirs - 1 - half
        ext[(f + 1) * STRIDE - 1 : (f + 1) * STRIDE, (ghost + row_count) * NLON :] = north_ref[
            spot : spot + 1, :
        ]
    at = freqs * width
    masks = []
    for row in range(-ghost, row_count + ghost):
        if row < 0:
            masks.append(south_ref[at : at + 1, lanes(row + ghost)])
        elif row < row_count:
            masks.append(field_ref[dirs + 1 : dirs + 2, lanes(row)])
        else:
            masks.append(north_ref[at : at + 1, lanes(row - row_count)])

    j = lax.broadcasted_iota(jnp.int32, (STRIDE, LANES), 0)
    j = jnp.where(j < dirs, j, jnp.where(j < STRIDE - 1, j - dirs, dirs - 1))
    angles = (2.0 * math.pi / dirs) * j.astype(F32)
    sin_a = jnp.where((j == 0) | (j == half), 0.0, jnp.sin(angles))
    cos_a = jnp.cos(angles)
    from_south = (sin_a > 0.0)[:, 0:1]
    from_west = (cos_a > 0.0)[:, 0:1]
    cy_base = 0.5 * jnp.abs(sin_a)
    cx_base = 0.25 * jnp.abs(cos_a)

    def advance(src, dst, first, last, shift):
        for row in range(first, last):
            spot = (band * row_count + row).astype(F32) + 0.5
            lat = jnp.full((STRIDE, LANES), spot / rows_all * (2.0 * math.pi / 3.0) - math.pi / 3.0)
            sec = 1.0 / jnp.cos(lat)
            tan = jnp.sin(lat) * sec
            turn = -0.3 * cos_a * tan
            from_lower = (turn > 0.0)[:, 0:1]
            sea = masks[row + ghost]
            for f in range(freqs):
                speed = 1.0 / (1.0 + 0.25 * f)
                cy = (speed * cy_base)[:, 0:1]
                cx = (speed * cx_base * sec)[:, 0:1]
                ct = (speed * jnp.abs(turn))[:, 0:1]
                piece = slice(f * STRIDE, (f + 1) * STRIDE)
                x = src[piece, lanes(row + shift)]
                meridional = jnp.where(
                    from_south, src[piece, lanes(row + shift - 1)], src[piece, lanes(row + shift + 1)]
                )
                zonal = jnp.where(from_west, roll_lanes(x, 1), roll_lanes(x, -1))
                adv = (x - cy * (x - meridional) - cx * (x - zonal)) * sea
                lower = pltpu.roll(adv, 1, 0)
                upper = pltpu.roll(adv, STRIDE - 1, 0)
                out = (adv - ct * (adv - jnp.where(from_lower, lower, upper))) * sea
                dst(f, row, out)

    def keep(f, row, out):
        out = jnp.concatenate(
            [out[0:dirs], out[0:1], out[dirs + 1 : STRIDE - 1], out[dirs - 1 : dirs]], axis=0
        )
        mid[f * STRIDE : (f + 1) * STRIDE, lanes(row + 1)] = out

    def last(f, row, out):
        high, low = split(out)
        lhs[f * STRIDE : (f + 1) * STRIDE, lanes(row)] = high
        lhs[rows + f * STRIDE : rows + (f + 1) * STRIDE, lanes(row)] = low

    advance(ext, keep, -1, row_count + 1, ghost)
    advance(mid, last, 0, row_count, 1)

    def body(t, carry):
        where = pl.ds(pl.multiple_of(t * TILE, TILE), TILE)
        cells = cell_ref[:, where]
        table = jnp.concatenate(
            [one_hot(cells, k * TILE, TILE) for k in range(points // TILE)], axis=0
        )
        both = jnp.dot(lhs[...], table, preferred_element_type=F32)
        out = both[0:rows] + both[rows : 2 * rows]
        packed = jnp.concatenate(
            [out[f * STRIDE : f * STRIDE + dirs] for f in range(freqs)], axis=0
        )
        for h in range(TILE // LANES):
            back_ref[t * (TILE // LANES) + h] = packed[:, h * LANES : (h + 1) * LANES]
        return carry

    lax.fori_loop(0, points // TILE, body, 0)


def pick_kernel(freqs, dirs, recv_ref, pos_ref, out_ref, lhs):
    points = pos_ref.shape[1]
    rows = freqs * STRIDE
    spread_rows(lambda c: recv_ref[c], freqs, dirs, points, lhs)

    def body(t, carry):
        where = pl.ds(pl.multiple_of(t * TILE, TILE), TILE)
        wanted = pos_ref[:, where]
        table = jnp.concatenate(
            [one_hot(wanted, k * TILE, TILE) for k in range(points // TILE)], axis=0
        )
        both = jnp.dot(lhs[...], table, preferred_element_type=F32)
        out = both[0:rows] + both[rows : 2 * rows]
        for f in range(freqs):
            out_ref[f, :, where] = out[f * STRIDE : f * STRIDE + dirs]
        return carry

    lax.fori_loop(0, points // TILE, body, 0)


def exchange(x, blocks, cap):
    if cap == LANES:
        return lax.all_to_all(x, "blk", split_axis=0, concat_axis=0, tiled=True)
    pieces, rows, lanes = x.shape
    x = jnp.moveaxis(x, 1, 0).reshape(rows, blocks, cap)
    x = lax.all_to_all(x, "blk", split_axis=1, concat_axis=1, tiled=True)
    return jnp.moveaxis(x.reshape(rows, pieces, lanes), 0, 1)


def per_device(spectrum, wind_vector, dest_cell, counts, sea_mask, dia_shift):
    blocks = lax.axis_size("blk")
    freqs, dirs, points = spectrum.shape
    cap = points // blocks
    pieces = points // LANES
    rows = freqs * STRIDE
    send_rows = -(-(freqs * dirs + 1) // 8) * 8
    edge = SUBSTEPS * NLON
    edge_rows = -(-(freqs * (dirs // 2 + 1) + 1) // 8) * 8
    vmem = pl.BlockSpec(memory_space=pltpu.VMEM)
    smem = pl.BlockSpec(memory_space=pltpu.SMEM)
    params = pltpu.CompilerParams(vmem_limit_bytes=VMEM_LIMIT)

    def arr(shape, dtype=F32):
        return jax.ShapeDtypeStruct(shape, dtype)

    send, position = pl.pallas_call(
        functools.partial(source_kernel, blocks, cap),
        out_shape=(arr((pieces, send_rows, LANES)), arr((1, points), jnp.int32)),
        in_specs=[smem, smem, vmem, vmem, vmem],
        out_specs=(vmem, vmem),
        scratch_shapes=[
            pltpu.VMEM((freqs, 2 * dirs, points), F32),
            pltpu.VMEM((2 * send_rows, points), BF16),
        ],
        compiler_params=params,
        name="source",
    )(dia_shift, counts, spectrum, wind_vector, dest_cell.reshape(1, points))
    arrived = exchange(send, blocks, cap)
    field, up, down, cells = pl.pallas_call(
        functools.partial(place_kernel, freqs, dirs),
        out_shape=(
            arr((rows, points)),
            arr((edge_rows, edge)),
            arr((edge_rows, edge)),
            arr((1, points), jnp.int32),
        ),
        in_specs=[vmem],
        out_specs=(vmem, vmem, vmem, vmem),
        scratch_shapes=[pltpu.VMEM((2 * rows, points), BF16)],
        compiler_params=params,
        name="place",
    )(arrived)
    forward, backward = halo_pairs(blocks)
    south = lax.ppermute(up, "blk", forward)
    north = lax.ppermute(down, "blk", backward)
    row_count = points // NLON
    back = pl.pallas_call(
        functools.partial(step_kernel, freqs, dirs, blocks),
        out_shape=arr((pieces, freqs * dirs, LANES)),
        in_specs=[vmem] * 4,
        out_specs=vmem,
        scratch_shapes=[
            pltpu.VMEM((rows, points + 2 * edge), F32),
            pltpu.VMEM((rows, points + 2 * NLON), F32),
            pltpu.VMEM((2 * rows, points), BF16),
        ],
        compiler_params=params,
        name="step",
    )(field, south, north, cells)
    returned = exchange(back, blocks, cap)
    return pl.pallas_call(
        functools.partial(pick_kernel, freqs, dirs),
        out_shape=arr((freqs, dirs, points)),
        in_specs=[vmem, vmem],
        out_specs=vmem,
        scratch_shapes=[pltpu.VMEM((2 * rows, points), BF16)],
        compiler_params=params,
        name="pick",
    )(returned, position)


def solution(mesh):
    placed = (
        P(None, None, ("groups", "blk")),
        P(None, ("groups", "blk")),
        P(("groups", "blk")),
        P(("groups", "blk")),
        P(("groups", "blk")),
        P(),
    )
    return jax.shard_map(
        per_device,
        mesh=mesh,
        in_specs=placed,
        out_specs=P(None, None, ("groups", "blk")),
        check_vma=False,
    )
```

time: 211 us -> 93.2 us (0.44)
  matrix products: 45 us -> 0 us
  local copies, waits for them, and re-layouts: 37.3 us -> 3.26 us
  waiting for transfers between devices: 37.3 us -> 5.69 us
  blocking collectives: 29.6 us -> 56.8 us
  loops' own time: 26.2 us -> 0 us
  Pallas kernels: 0 us -> 22 us
  starting transfers between devices: 21.2 us -> 4.34 us
  other arithmetic: 11 us -> 0 us
    dot_general x40 -> x0, matrix products: 45 us -> none  [the longest x16 21.4 us: pick_one_block(): lax.dot_general(data, table, (((1,), (1,)), ((), ())), precision=lax.Prec...]
    all_to_all x1 -> x2, blocking collectives: 29.6 us -> 56.8 us  [exchange(): return lax.all_to_all(x, 'blk', split_axis=0, concat_axis=0, tiled=True)]
    another operation x5 -> x0, loops' own time: 26.2 us -> none  [the longest x2 10.9 us: pick_columns(): pieces = lax.map(pick_one_block, jnp.arange(block_count, dtype=jnp.int32))]
    all_to_all x2 -> x0, waiting for transfers between devices: 25.7 us -> none  [the longest x1 21.5 us: per_device(): lax.all_to_all(outgoing, 'blk', split_axis=2, concat_axis=2, tiled=True)]
    dynamic_slice x56 -> x0, local copies, waits for them, and re-layouts: 24.8 us -> none  [the longest x40 23.6 us: earlier_counts(): lax.map(earlier_one_block, jnp.arange(block_count, dtype=jnp.int32))]
    pallas_call x0 -> x4, Pallas kernels: none -> 22 us  [the longest x1 7.14 us: per_device(): pl.pallas_call(functools.partial(source_kernel, blocks, cap), out_shape=(...]
    all_to_all x2 -> x0, starting transfers between devices: 11.7 us -> none  [the longest x1 7.35 us: per_device(): lax.all_to_all(labels, 'blk', split_axis=2, concat_axis=2, tiled=True)]
    ppermute x4 -> x2, waiting for transfers between devices: 11.7 us -> 5.69 us  [the longest x1 4.4 us: per_device(): north = lax.ppermute(down, 'blk', backward)]
  transfers between devices with their start and end apart: 6 -> 2, of which waited for: 6 -> 2; matrix products, arithmetic and copies ran while one was open for 1% -> 0% of each run, Pallas kernels for 0% -> 0%
where the time goes in v1:
time: 93.2 us; the launch traced here: 92.8 us
  blocking collectives  56.8 us (61%)
  Pallas kernels  22 us (24%)
  waiting for transfers between devices  5.69 us (6%)
  starting transfers between devices  4.34 us (5%)
  local copies, waits for them, and re-layouts  3.26 us (3%)
    all_to_all x2, blocking collectives, exchange(): return lax.all_to_all(x, 'blk', split_axis=0, concat_axis=0, tiled=True)  56.8 us
    pallas_call x1, Pallas kernels, per_device(): pl.pallas_call(functools.partial(source_kernel, blocks, cap), out_shape=(...  7.14 us
    pallas_call x1, Pallas kernels, per_device(): pl.pallas_call(functools.partial(step_kernel, freqs, dirs, blocks), out_s...  6.09 us
    pallas_call x1, Pallas kernels, per_device(): pl.pallas_call(functools.partial(pick_kernel, freqs, dirs), out_shape=arr...  4.68 us
    ppermute x1, waiting for transfers between devices, per_device(): north = lax.ppermute(down, 'blk', backward)  4.4 us
    pallas_call x1, Pallas kernels, per_device(): pl.pallas_call(functools.partial(place_kernel, freqs, dirs), out_shape=(a...  4.12 us
    unnamed x8, local copies, waits for them, and re-layouts  3.26 us
    ppermute x1, starting transfers between devices, per_device(): south = lax.ppermute(up, 'blk', forward)  2.35 us
  transfers between devices with their start and end apart: 2, of which 2 were waited for; matrix products, arithmetic and copies ran while one was open for 0% of the time, Pallas kernels for 0%

profile of v1, /device:TPU:1, one launch (start us, length us, event | category | flops | bytes accessed | tf_op | source)
XLA Modules:
  0.0 92.8 jit_solution(1065594427740781658)
XLA Ops:
  0.7 0.0 copy-start.3
  0.7 0.6 copy-done.3
  1.3 0.0 copy-start
  1.3 1.2 %copy-done = f32[3,36,2048]{2,1,0:T(8,128)S(1)} copy-done((f32[3,36,2048]{2,1,0:T(8,128)S(1)}, f32[3,36,2048]{2,1,0:T(8,128)}, u32[]{:S(2)}) %copy-start) | copy-done | bytes 884760
  2.5 0.0 copy-start.1
  2.5 0.7 copy-done.1
  3.2 0.0 copy-start.2
  3.2 0.7 copy-done.2
  3.9 7.1 %source.1 = (f32[16,112,128]{2,1,0:T(8,128)S(1)}, s32[1,2048]{1,0:T(1,128)S(1)}) custom-call(s32[2]{0:T(128)S(1)} %copy-done.3, s32[1]{0:T(128)S(6)} %copy.6.count_ref, f32[3,36,2048]{2,1,0:T(8,128)S(1)} %copy-done, f32[2,2048]{1,0:T(2,128)S(1)} %copy-done.1, s32[1,2048]{1,0:T(1,128)S(1)} %bitcast.1), custom_call_target="tpu_custom_call" | custom-call | tf_op jit(solution)/shard_map/source/pallas_call | solution.py:348
  11.1 30.1 %all_to_all.10.recv_ref = f32[16,112,128]{2,1,0:T(8,128)S(1)} all-to-all(f32[16,112,128]{2,1,0:T(8,128)S(1)} %get-tuple-element.11), channel_id=1, replica_groups=mesh['groups'=2,'blk'=16] {'blk'}, dimensions={0} | all-to-all | bytes 1835008 | tf_op jit(solution)/shard_map/all_to_all | solution.py:325
  41.1 4.1 %place.1 = (f32[120,2048]{1,0:T(8,128)S(1)}, f32[64,1024]{1,0:T(8,128)S(1)}, f32[64,1024]{1,0:T(8,128)S(1)}, s32[1,2048]{1,0:T(1,128)S(1)}) custom-call(f32[16,112,128]{2,1,0:T(8,128)S(1)} %all_to_all.10.recv_ref), custom_call_target="tpu_custom_call" | custom-call | tf_op jit(solution)/shard_map/place/pallas_call | solution.py:361
  45.3 2.4 %collective-permute-start = (f32[64,1024]{1,0:T(8,128)S(1)}, f32[64,1024]{1,0:T(8,128)S(1)}, u32[]{:S(2)}, u32[]{:S(2)}) collective-permute-start(f32[64,1024]{1,0:T(8,128)S(1)} %get-tuple-element.13), channel_id=1, source_target_pairs={{0,1},{1,2},{2,3},{3,6},{6,7},{7,4},{4,5},{5,8},{8,9},{9,10},{10,1... | collective-permute-start | bytes 786440 | tf_op jit(solution)/shard_map/ppermute | solution.py:376
  47.6 2.0 %collective-permute-start.1 = (f32[64,1024]{1,0:T(8,128)S(1)}, f32[64,1024]{1,0:T(8,128)S(1)}, u32[]{:S(2)}, u32[]{:S(2)}) collective-permute-start(f32[64,1024]{1,0:T(8,128)S(1)} %get-tuple-element.14), channel_id=1, source_target_pairs={{1,0},{2,1},{3,2},{6,3},{7,6},{4,7},{5,4},{8,5},{9,8},{10,9},{11,1... | collective-permute-start | bytes 786440 | tf_op jit(solution)/shard_map/ppermute | solution.py:377
  49.6 1.3 %collective-permute-done.south_ref = f32[64,1024]{1,0:T(8,128)S(1)} collective-permute-done((f32[64,1024]{1,0:T(8,128)S(1)}, f32[64,1024]{1,0:T(8,128)S(1)}, u32[]{:S(2)}, u32[]{:S(2)}) %collective-permute-start) | collective-permute-done | bytes 262176 | tf_op jit(solution)/shard_map/ppermute | solution.py:376
  50.9 4.4 %collective-permute-done.1.north_ref = f32[64,1024]{1,0:T(8,128)S(1)} collective-permute-done((f32[64,1024]{1,0:T(8,128)S(1)}, f32[64,1024]{1,0:T(8,128)S(1)}, u32[]{:S(2)}, u32[]{:S(2)}) %collective-permute-start.1) | collective-permute-done | bytes 262176 | tf_op jit(solution)/shard_map/ppermute | solution.py:377
  55.3 6.1 %step.1 = f32[16,108,128]{2,1,0:T(8,128)S(1)} custom-call(f32[120,2048]{1,0:T(8,128)S(1)} %get-tuple-element.12.field_ref, f32[64,1024]{1,0:T(8,128)S(1)} %collective-permute-done.south_ref, f32[64,1024]{1,0:T(8,128)S(1)} %collective-permute-done.1.north_ref, s32[1,2048]{1,0:T(1,128)S(1)} %get-tuple-element.15.cell_ref), custom_call_target="tpu_custom_call" | custom-call | tf_op jit(solution)/shard_map/step/pallas_call | solution.py:379
  61.4 26.7 %all_to_all.11.recv_ref = f32[16,108,128]{2,1,0:T(8,128)S(1)} all-to-all(f32[16,108,128]{2,1,0:T(8,128)S(1)} %step.1), channel_id=1, replica_groups=mesh['groups'=2,'blk'=16] {'blk'}, dimensions={0} | all-to-all | bytes 1769472 | tf_op jit(solution)/shard_map/all_to_all | solution.py:325
  88.1 4.7 %pick.1 = f32[3,36,2048]{2,1,0:T(8,128)} custom-call(f32[16,108,128]{2,1,0:T(8,128)S(1)} %all_to_all.11.recv_ref, s32[1,2048]{1,0:T(1,128)S(1)} %get-tuple-element.16.pos_ref), custom_call_target="tpu_custom_call" | custom-call | tf_op jit(solution)/shard_map/pick/pallas_call | solution.py:393
Async XLA Ops:
  0.7 0.7 copy-start.3
  1.3 1.2 %copy-start = (f32[3,36,2048]{2,1,0:T(8,128)S(1)}, f32[3,36,2048]{2,1,0:T(8,128)}, u32[]{:S(2)}) copy-start(f32[3,36,2048]{2,1,0:T(8,128)} %spec_ref.1) | copy-start | bytes 2654212
  2.5 0.7 copy-start.1
  3.2 0.7 copy-start.2
  45.3 5.7 %collective-permute-start = (f32[64,1024]{1,0:T(8,128)S(1)}, f32[64,1024]{1,0:T(8,128)S(1)}, u32[]{:S(2)}, u32[]{:S(2)}) collective-permute-start(f32[64,1024]{1,0:T(8,128)S(1)} %get-tuple-element.13), channel_id=1, source_target_pairs={{0,1},{1,2},{2,3},{3,6},{6,7},{7,4},{4,5},{5,8},{8,9},{9,10},{10,1... | collective-permute-start | bytes 786440 | tf_op jit(solution)/shard_map/ppermute | solution.py:376
  47.6 7.7 %collective-permute-start.1 = (f32[64,1024]{1,0:T(8,128)S(1)}, f32[64,1024]{1,0:T(8,128)S(1)}, u32[]{:S(2)}, u32[]{:S(2)}) collective-permute-start(f32[64,1024]{1,0:T(8,128)S(1)} %get-tuple-element.14), channel_id=1, source_target_pairs={{1,0},{2,1},{3,2},{6,3},{7,6},{4,7},{5,4},{8,5},{9,8},{10,9},{11,1... | collective-permute-start | bytes 786440 | tf_op jit(solution)/shard_map/ppermute | solution.py:377

commit v2 on v1

--- a/solution.py
+++ b/solution.py
@@ -15,7 +15,8 @@
 STRIDE = 40
 F32 = jnp.float32
 BF16 = jnp.bfloat16
-VMEM_LIMIT = 48 * 1024 * 1024
+VMEM_LIMIT = 40 * 1024 * 1024
+SOURCE_LIMIT = 60 * 1024 * 1024
 
 
 def snake_row(blocks):
@@ -35,7 +36,7 @@
     return (line * row + place) * 2 + core
 
 
-def halo_pairs(blocks):
+def halo_swaps(blocks):
     row = snake_row(blocks)
     order = []
     for band in range(blocks):
@@ -47,12 +48,15 @@
         if line % 2:
             place = row - 1 - place
         order.append((line * row + place) * 2 + core)
-    up = [(order[b], order[b + 1]) for b in range(blocks - 1)]
-    return up, [(t, s) for s, t in up]
-
-
-def column(values):
-    return jnp.concatenate([jnp.full((1, 1), float(v), F32) for v in values], axis=0)
+
+    def swaps(first):
+        pairs = []
+        for band in range(first, blocks - 1, 2):
+            low, high = order[band], order[band + 1]
+            pairs += [(low, high), (high, low)]
+        return pairs
+
+    return swaps(0), swaps(1)
 
 
 def split(x):
@@ -78,10 +82,38 @@
 
 
 def source_kernel(
-    blocks, cap, shift_ref, count_ref, spec_ref, wind_ref, dest_ref, send_ref, pos_ref, dbl, lhs
+    blocks,
+    cap,
+    shift_in,
+    count_in,
+    spec_in,
+    wind_in,
+    dest_in,
+    send_ref,
+    pos_ref,
+    shift_ref,
+    count_ref,
+    spec_ref,
+    wind_ref,
+    dest_ref,
+    dbl,
+    lhs,
+    sems,
 ):
     freqs, dirs, points = spec_ref.shape
     rows = lhs.shape[0] // 2
+    pairs = (
+        (dest_in, dest_ref),
+        (count_in, count_ref),
+        (shift_in, shift_ref),
+        (wind_in, wind_ref),
+        (spec_in, spec_ref),
+    )
+    copies = [pltpu.make_async_copy(a, b, sems.at[i]) for i, (a, b) in enumerate(pairs)]
+    for copy in copies:
+        copy.start()
+    copies[0].wait()
+    copies[1].wait()
     dest = dest_ref[...]
     slot = lax.broadcasted_iota(jnp.int32, (1, points), 1)
     live = slot < count_ref[0]
@@ -101,6 +133,8 @@
         base = base + jnp.dot(packed, ones, preferred_element_type=F32)
         where_to = jnp.sum(piece * running, axis=0, keepdims=True) - 1.0
         pos_ref[:, c * LANES : (c + 1) * LANES] = where_to.astype(jnp.int32)
+    for copy in copies[2:]:
+        copy.wait()
     total = jnp.zeros((1, points), F32)
     for f in range(freqs):
         x = spec_ref[f]
@@ -111,11 +145,12 @@
     cos_a, sin_a = direction_trig(dirs, dirs)
     along = wind_ref[0:1, :] * cos_a[:, 0:1] + wind_ref[1:2, :] * sin_a[:, 0:1]
     drive = jnp.maximum(along - 0.3, 0.0)
+    span = -(-(dirs + dirs // 4) // 8) * 8
     for f in range(freqs):
         x = spec_ref[f]
-        twice = dbl[f]
-        ahead = pltpu.roll(twice, 2 * dirs - shift_ref[0], 0)[0:dirs]
-        behind = pltpu.roll(twice, shift_ref[1], 0)[0:dirs]
+        ahead = pltpu.roll(dbl[f, 0:span, :], span - shift_ref[0], 0)[0:dirs]
+        offset = 2 * dirs - span
+        behind = pltpu.roll(dbl[f, offset:, :], shift_ref[1] + span - (dirs - offset), 0)[0:dirs]
         out = x * jnp.exp((0.15 + 0.05 * f) * drive - (0.2 + 0.1 * f) * mean) + 0.1 * (
             ahead * behind - x * x
         )
@@ -139,7 +174,7 @@
             send_ref[t * (TILE // LANES) + h] = out[:, h * LANES : (h + 1) * LANES]
         return carry
 
-    lax.fori_loop(0, points // TILE, body, 0)
+    lax.fori_loop(0, points // TILE, body, 0, unroll=True)
 
 
 def spread_rows(get, freqs, dirs, points, lhs):
@@ -156,7 +191,7 @@
         lhs[rows : 2 * rows, c * LANES : (c + 1) * LANES] = low
 
 
-def place_kernel(freqs, dirs, recv_ref, field_ref, up_ref, down_ref, cell_ref, lhs):
+def place_kernel(freqs, dirs, blocks, recv_ref, field_ref, first_ref, second_ref, cell_ref, lhs):
     points = cell_ref.shape[1]
     rows = freqs * STRIDE
     label = freqs * dirs
@@ -174,19 +209,33 @@
         field_ref[:, where] = both[0:rows] + both[rows : 2 * rows]
         return carry
 
-    lax.fori_loop(0, points // TILE, body, 0)
+    lax.fori_loop(0, points // TILE, body, 0, unroll=True)
     half = dirs // 2
     width = half + 1
-    edge = up_ref.shape[1]
-    for f in range(freqs):
-        top = field_ref[f * STRIDE : f * STRIDE + width, points - edge : points]
-        up_ref[f * width : (f + 1) * width, :] = top
-        low = field_ref[f * STRIDE + half : f * STRIDE + half + width, 0:edge]
-        down_ref[f * width : (f + 1) * width, :] = low
-    left = up_ref.shape[0] - freqs * width
-    mask = field_ref[dirs + 1 : dirs + 2, :]
-    up_ref[freqs * width :, :] = jnp.broadcast_to(mask[:, points - edge : points], (left, edge))
-    down_ref[freqs * width :, :] = jnp.broadcast_to(mask[:, 0:edge], (left, edge))
+    last = points - NLON
+
+    def edge(out_ref, near, far, skip):
+        at = 0
+        for start, extra in ((near, 0), (far, 1)):
+            for f in range(freqs):
+                low = f * STRIDE + skip + extra
+                high = f * STRIDE + skip + width - extra
+                out_ref[at : at + high - low, :] = field_ref[low:high, start : start + NLON]
+                at += high - low
+        mask = field_ref[dirs + 1 : dirs + 2, near : near + NLON]
+        out_ref[at:, :] = jnp.broadcast_to(mask, (out_ref.shape[0] - at, NLON))
+
+    even = lax.rem(snake(lax.axis_index("blk"), blocks), 2) == 0
+
+    @pl.when(even)
+    def _():
+        edge(first_ref, last, last - NLON, 0)
+        edge(second_ref, 0, NLON, half)
+
+    @pl.when(jnp.logical_not(even))
+    def _():
+        edge(second_ref, last, last - NLON, 0)
+        edge(first_ref, 0, NLON, half)
 
 
 def roll_lanes(x, shift):
@@ -194,7 +243,7 @@
 
 
 def step_kernel(
-    freqs, dirs, blocks, field_ref, south_ref, north_ref, cell_ref, back_ref, ext, mid, lhs
+    freqs, dirs, blocks, field_ref, first_ref, second_ref, cell_ref, back_ref, ext, mid, ends, lhs
 ):
     points = field_ref.shape[1]
     rows = freqs * STRIDE
@@ -211,26 +260,40 @@
     ext[:, 0 : ghost * NLON] = jnp.zeros((rows, ghost * NLON), F32)
     ext[:, (ghost + row_count) * NLON :] = jnp.zeros((rows, ghost * NLON), F32)
     ext[:, ghost * NLON : (ghost + row_count) * NLON] = field_ref[...]
-    for f in range(freqs):
-        ext[f * STRIDE : f * STRIDE + width, 0 : ghost * NLON] = south_ref[
-            f * width : (f + 1) * width, :
-        ]
-        ext[f * STRIDE + half : f * STRIDE + half + width, (ghost + row_count) * NLON :] = (
-            north_ref[f * width : (f + 1) * width, :]
-        )
-        spot = f * width + dirs - 1 - half
-        ext[(f + 1) * STRIDE - 1 : (f + 1) * STRIDE, (ghost + row_count) * NLON :] = north_ref[
-            spot : spot + 1, :
-        ]
-    at = freqs * width
-    masks = []
-    for row in range(-ghost, row_count + ghost):
+
+    def fill(in_ref, near, far, skip, end):
+        at = 0
+        for row, extra in ((near, 0), (far, 1)):
+            for f in range(freqs):
+                low = f * STRIDE + skip + extra
+                high = f * STRIDE + skip + width - extra
+                ext[low:high, lanes(row)] = in_ref[at : at + high - low, :]
+                at += high - low
+        if skip:
+            for f in range(freqs):
+                spot = f * width + dirs - 1 - half
+                top = (f + 1) * STRIDE
+                ext[top - 1 : top, lanes(near)] = in_ref[spot : spot + 1, :]
+        ends[end : end + 1, :] = in_ref[at : at + 1, :]
+
+    even = lax.rem(band, 2) == 0
+
+    @pl.when(even)
+    def _():
+        fill(second_ref, ghost - 1, ghost - 2, 0, 0)
+        fill(first_ref, ghost + row_count, ghost + row_count + 1, half, 1)
+
+    @pl.when(jnp.logical_not(even))
+    def _():
+        fill(first_ref, ghost - 1, ghost - 2, 0, 0)
+        fill(second_ref, ghost + row_count, ghost + row_count + 1, half, 1)
+
+    def sea_of(row):
         if row < 0:
-            masks.append(south_ref[at : at + 1, lanes(row + ghost)])
-        elif row < row_count:
-            masks.append(field_ref[dirs + 1 : dirs + 2, lanes(row)])
-        else:
-            masks.append(north_ref[at : at + 1, lanes(row - row_count)])
+            return ends[0:1, :]
+        if row >= row_count:
+            return ends[1:2, :]
+        return field_ref[dirs + 1 : dirs + 2, lanes(row)]
 
     j = lax.broadcasted_iota(jnp.int32, (STRIDE, LANES), 0)
     j = jnp.where(j < dirs, j, jnp.where(j < STRIDE - 1, j - dirs, dirs - 1))
@@ -250,7 +313,7 @@
             tan = jnp.sin(lat) * sec
             turn = -0.3 * cos_a * tan
             from_lower = (turn > 0.0)[:, 0:1]
-            sea = masks[row + ghost]
+            sea = sea_of(row)
             for f in range(freqs):
                 speed = 1.0 / (1.0 + 0.25 * f)
                 cy = (speed * cy_base)[:, 0:1]
@@ -290,23 +353,31 @@
         )
         both = jnp.dot(lhs[...], table, preferred_element_type=F32)
         out = both[0:rows] + both[rows : 2 * rows]
-        packed = jnp.concatenate(
-            [out[f * STRIDE : f * STRIDE + dirs] for f in range(freqs)], axis=0
-        )
         for h in range(TILE // LANES):
-            back_ref[t * (TILE // LANES) + h] = packed[:, h * LANES : (h + 1) * LANES]
+            for q in range(freqs * dirs // 4):
+                low = q // (dirs // 4) * STRIDE + q % (dirs // 4) * 4
+                back_ref[t * (TILE // LANES) + h, q] = out[
+                    low : low + 4, h * LANES : (h + 1) * LANES
+                ]
         return carry
 
-    lax.fori_loop(0, points // TILE, body, 0)
-
-
-def pick_kernel(freqs, dirs, recv_ref, pos_ref, out_ref, lhs):
+    lax.fori_loop(0, points // TILE, body, 0, unroll=True)
+
+
+def pick_kernel(freqs, dirs, recv_ref, pos_ref, out_ref, result, lhs, sems):
     points = pos_ref.shape[1]
     rows = freqs * STRIDE
-    spread_rows(lambda c: recv_ref[c], freqs, dirs, points, lhs)
-
-    def body(t, carry):
-        where = pl.ds(pl.multiple_of(t * TILE, TILE), TILE)
+    spread_rows(
+        lambda c: jnp.concatenate([recv_ref[c, q] for q in range(freqs * dirs // 4)], axis=0),
+        freqs,
+        dirs,
+        points,
+        lhs,
+    )
+    parts = []
+
+    def body(t):
+        where = slice(t * TILE, (t + 1) * TILE)
         wanted = pos_ref[:, where]
         table = jnp.concatenate(
             [one_hot(wanted, k * TILE, TILE) for k in range(points // TILE)], axis=0
@@ -314,19 +385,28 @@
         both = jnp.dot(lhs[...], table, preferred_element_type=F32)
         out = both[0:rows] + both[rows : 2 * rows]
         for f in range(freqs):
-            out_ref[f, :, where] = out[f * STRIDE : f * STRIDE + dirs]
-        return carry
-
-    lax.fori_loop(0, points // TILE, body, 0)
+            result[f, :, where] = out[f * STRIDE : f * STRIDE + dirs]
+        part = pltpu.make_async_copy(
+            result.at[:, :, where], out_ref.at[:, :, where], sems.at[t]
+        )
+        part.start()
+        parts.append(part)
+
+    for t in range(points // TILE):
+        body(t)
+    for part in parts:
+        part.wait()
 
 
 def exchange(x, blocks, cap):
     if cap == LANES:
         return lax.all_to_all(x, "blk", split_axis=0, concat_axis=0, tiled=True)
-    pieces, rows, lanes = x.shape
-    x = jnp.moveaxis(x, 1, 0).reshape(rows, blocks, cap)
-    x = lax.all_to_all(x, "blk", split_axis=1, concat_axis=1, tiled=True)
-    return jnp.moveaxis(x.reshape(rows, pieces, lanes), 0, 1)
+    pieces, lanes = x.shape[0], x.shape[-1]
+    inner = x.shape[1:-1]
+    x = jnp.moveaxis(x, 0, -2).reshape(*inner, blocks, cap)
+    dim = len(inner)
+    x = lax.all_to_all(x, "blk", split_axis=dim, concat_axis=dim, tiled=True)
+    return jnp.moveaxis(x.reshape(*inner, pieces, lanes), -2, 0)
 
 
 def per_device(spectrum, wind_vector, dest_cell, counts, sea_mask, dia_shift):
@@ -336,10 +416,9 @@
     pieces = points // LANES
     rows = freqs * STRIDE
     send_rows = -(-(freqs * dirs + 1) // 8) * 8
-    edge = SUBSTEPS * NLON
-    edge_rows = -(-(freqs * (dirs // 2 + 1) + 1) // 8) * 8
+    edge_rows = -(-(2 * freqs * (dirs // 2) + 1) // 8) * 8
     vmem = pl.BlockSpec(memory_space=pltpu.VMEM)
-    smem = pl.BlockSpec(memory_space=pltpu.SMEM)
+    hbm = pl.BlockSpec(memory_space=pltpu.HBM)
     params = pltpu.CompilerParams(vmem_limit_bytes=VMEM_LIMIT)
 
     def arr(shape, dtype=F32):
@@ -348,22 +427,28 @@
     send, position = pl.pallas_call(
         functools.partial(source_kernel, blocks, cap),
         out_shape=(arr((pieces, send_rows, LANES)), arr((1, points), jnp.int32)),
-        in_specs=[smem, smem, vmem, vmem, vmem],
+        in_specs=[hbm] * 5,
         out_specs=(vmem, vmem),
         scratch_shapes=[
+            pltpu.SMEM(dia_shift.shape, jnp.int32),
+            pltpu.SMEM(counts.shape, jnp.int32),
+            pltpu.VMEM(spectrum.shape, F32),
+            pltpu.VMEM(wind_vector.shape, F32),
+            pltpu.VMEM((1, points), jnp.int32),
             pltpu.VMEM((freqs, 2 * dirs, points), F32),
             pltpu.VMEM((2 * send_rows, points), BF16),
+            pltpu.SemaphoreType.DMA((5,)),
         ],
-        compiler_params=params,
+        compiler_params=pltpu.CompilerParams(vmem_limit_bytes=SOURCE_LIMIT),
         name="source",
     )(dia_shift, counts, spectrum, wind_vector, dest_cell.reshape(1, points))
     arrived = exchange(send, blocks, cap)
-    field, up, down, cells = pl.pallas_call(
-        functools.partial(place_kernel, freqs, dirs),
+    field, first, second, cells = pl.pallas_call(
+        functools.partial(place_kernel, freqs, dirs, blocks),
         out_shape=(
             arr((rows, points)),
-            arr((edge_rows, edge)),
-            arr((edge_rows, edge)),
+            arr((edge_rows, NLON)),
+            arr((edge_rows, NLON)),
             arr((1, points), jnp.int32),
         ),
         in_specs=[vmem],
@@ -372,30 +457,33 @@
         compiler_params=params,
         name="place",
     )(arrived)
-    forward, backward = halo_pairs(blocks)
-    south = lax.ppermute(up, "blk", forward)
-    north = lax.ppermute(down, "blk", backward)
-    row_count = points // NLON
+    inner, outer = halo_swaps(blocks)
+    mine, theirs = lax.ppermute(first, "blk", inner), lax.ppermute(second, "blk", outer)
     back = pl.pallas_call(
         functools.partial(step_kernel, freqs, dirs, blocks),
-        out_shape=arr((pieces, freqs * dirs, LANES)),
+        out_shape=arr((pieces, freqs * dirs // 4, 4, LANES)),
         in_specs=[vmem] * 4,
         out_specs=vmem,
         scratch_shapes=[
-            pltpu.VMEM((rows, points + 2 * edge), F32),
+            pltpu.VMEM((rows, points + 2 * SUBSTEPS * NLON), F32),
             pltpu.VMEM((rows, points + 2 * NLON), F32),
+            pltpu.VMEM((8, NLON), F32),
             pltpu.VMEM((2 * rows, points), BF16),
         ],
         compiler_params=params,
         name="step",
-    )(field, south, north, cells)
+    )(field, mine, theirs, cells)
     returned = exchange(back, blocks, cap)
     return pl.pallas_call(
         functools.partial(pick_kernel, freqs, dirs),
         out_shape=arr((freqs, dirs, points)),
         in_specs=[vmem, vmem],
-        out_specs=vmem,
-        scratch_shapes=[pltpu.VMEM((2 * rows, points), BF16)],
+        out_specs=hbm,
+        scratch_shapes=[
+            pltpu.VMEM((freqs, dirs, points), F32),
+            pltpu.VMEM((2 * rows, points), BF16),
+            pltpu.SemaphoreType.DMA((points // TILE,)),
+        ],
         compiler_params=params,
         name="pick",
     )(returned, position)

time: 93.2 us -> 82.5 us (0.89)
  Pallas kernels: 22 us -> 17.1 us
  local copies, waits for them, and re-layouts: 3.26 us -> 0.01 us
  waiting for transfers between devices: 5.69 us -> 4.24 us
  starting transfers between devices: 4.34 us -> 3.16 us
    unnamed x8 -> x2, local copies, waits for them, and re-layouts: 3.26 us -> 0.01 us
    pallas_call x1, Pallas kernels: 4.12 us -> 2.43 us  [per_device(): pl.pallas_call(functools.partial(place_kernel, freqs, dirs, blocks), out_...]
    ppermute x2, waiting for transfers between devices: 5.69 us -> 4.24 us  [the longest x1 4.23 us: per_device(): lax.ppermute(second, 'blk', outer)]
    pallas_call x1, Pallas kernels: 6.09 us -> 4.9 us  [per_device(): pl.pallas_call(functools.partial(step_kernel, freqs, dirs, blocks), out_s...]
    ppermute x2, starting transfers between devices: 4.34 us -> 3.16 us  [the longest x1 3.09 us: per_device(): lax.ppermute(second, 'blk', outer)]
    pallas_call x1, Pallas kernels: 4.68 us -> 3.66 us  [per_device(): pl.pallas_call(functools.partial(pick_kernel, freqs, dirs), out_shape=arr...]
    pallas_call x1, Pallas kernels: 7.14 us -> 6.16 us  [per_device(): pl.pallas_call(functools.partial(source_kernel, blocks, cap), out_shape=(...]
  transfers between devices with their start and end apart: 2 -> 2, of which waited for: 2 -> 1; matrix products, arithmetic and copies ran while one was open for 0% -> 0% of each run, Pallas kernels for 0% -> 0%
where the time goes in v2:
time: 82.5 us; the launch traced here: 82.2 us
  blocking collectives  56.8 us (69%)
  Pallas kernels  17.1 us (21%)
  waiting for transfers between devices  4.24 us (5%)
  starting transfers between devices  3.16 us (4%)
  between operations  0.87 us (1%)
    all_to_all x2, blocking collectives, exchange(): return lax.all_to_all(x, 'blk', split_axis=0, concat_axis=0, tiled=True)  56.8 us
    pallas_call x1, Pallas kernels, per_device(): pl.pallas_call(functools.partial(source_kernel, blocks, cap), out_shape=(...  6.16 us
    pallas_call x1, Pallas kernels, per_device(): pl.pallas_call(functools.partial(step_kernel, freqs, dirs, blocks), out_s...  4.9 us
    ppermute x1, waiting for transfers between devices, per_device(): lax.ppermute(second, 'blk', outer)  4.23 us
    pallas_call x1, Pallas kernels, per_device(): pl.pallas_call(functools.partial(pick_kernel, freqs, dirs), out_shape=arr...  3.66 us
    ppermute x1, starting transfers between devices, per_device(): lax.ppermute(second, 'blk', outer)  3.09 us
    pallas_call x1, Pallas kernels, per_device(): pl.pallas_call(functools.partial(place_kernel, freqs, dirs, blocks), out_...  2.43 us
  transfers between devices with their start and end apart: 2, of which 1 were waited for; matrix products, arithmetic and copies ran while one was open for 0% of the time, Pallas kernels for 0%

profile of v2, /device:TPU:1, one launch (start us, length us, event | category | flops | bytes accessed | tf_op | source)
XLA Modules:
  0.0 82.2 jit_solution(14815673053456817324)
XLA Ops:
  0.7 6.2 %source.1 = (f32[16,112,128]{2,1,0:T(8,128)}, s32[1,2048]{1,0:T(1,128)}) custom-call(s32[2]{0:T(128)} %shift_in.1, s32[1]{0:T(128)S(6)} %copy.6.count_in, f32[3,36,2048]{2,1,0:T(8,128)} %spec_in.1, f32[2,2048]{1,0:T(2,128)} %wind_in.1, s32[1,2048]{1,0:T(1,128)} %bitcast.1), custom_call_target="tpu_custom_call" | custom-call | tf_op jit(solution)/shard_map/source/pallas_call | solution.py:427
  6.8 30.3 %all_to_all.10.recv_ref = f32[16,112,128]{2,1,0:T(8,128)S(1)} all-to-all(f32[16,112,128]{2,1,0:T(8,128)} %get-tuple-element.11), channel_id=1, replica_groups=mesh['groups'=2,'blk'=16] {'blk'}, dimensions={0} | all-to-all | bytes 1835008 | tf_op jit(solution)/shard_map/all_to_all | solution.py:403
  37.1 2.4 %place.1 = (f32[120,2048]{1,0:T(8,128)S(1)}, f32[112,512]{1,0:T(8,128)S(1)}, f32[112,512]{1,0:T(8,128)S(1)}, s32[1,2048]{1,0:T(1,128)S(1)}) custom-call(f32[16,112,128]{2,1,0:T(8,128)S(1)} %all_to_all.10.recv_ref), custom_call_target="tpu_custom_call" | custom-call | tf_op jit(solution)/shard_map/place/pallas_call | solution.py:446
  39.5 0.1 collective-permute-start
  39.6 3.1 %collective-permute-start.1 = (f32[112,512]{1,0:T(8,128)S(1)}, f32[112,512]{1,0:T(8,128)S(1)}, u32[]{:S(2)}, u32[]{:S(2)}) collective-permute-start(f32[112,512]{1,0:T(8,128)S(1)} %get-tuple-element.14), channel_id=1, source_target_pairs={{1,2},{2,1},{3,6},{6,3},{7,4},{4,7},{5,8},{8,5},{9,10},{10,9},{11,... | collective-permute-start | bytes 688136 | tf_op jit(solution)/shard_map/ppermute | solution.py:461
  42.7 0.0 collective-permute-done.first_ref
  42.7 4.2 %collective-permute-done.1.second_ref = f32[112,512]{1,0:T(8,128)S(1)} collective-permute-done((f32[112,512]{1,0:T(8,128)S(1)}, f32[112,512]{1,0:T(8,128)S(1)}, u32[]{:S(2)}, u32[]{:S(2)}) %collective-permute-start.1) | collective-permute-done | bytes 229408 | tf_op jit(solution)/shard_map/ppermute | solution.py:461
  46.9 4.9 %step.1 = f32[16,27,4,128]{3,2,1,0:T(4,128)S(1)} custom-call(f32[120,2048]{1,0:T(8,128)S(1)} %get-tuple-element.12.field_ref, f32[112,512]{1,0:T(8,128)S(1)} %collective-permute-done.first_ref, f32[112,512]{1,0:T(8,128)S(1)} %collective-permute-done.1.second_ref, s32[1,2048]{1,0:T(1,128)S(1)} %get-tuple-element.15.cell_ref), custom_call_target="tpu_custom_call" | custom-call | tf_op jit(solution)/shard_map/step/pallas_call | solution.py:462
  51.9 0.0 copy-start
  51.9 26.5 %all_to_all.11.recv_ref = f32[16,27,4,128]{3,2,1,0:T(4,128)S(1)} all-to-all(f32[16,27,4,128]{3,2,1,0:T(4,128)S(1)} %step.1), channel_id=1, replica_groups=mesh['groups'=2,'blk'=16] {'blk'}, dimensions={0} | all-to-all | bytes 1769472 | tf_op jit(solution)/shard_map/all_to_all | solution.py:403
  78.4 0.0 copy-done
  78.4 3.7 %pick.1 = f32[3,36,2048]{2,1,0:T(8,128)} custom-call(f32[16,27,4,128]{3,2,1,0:T(4,128)S(1)} %all_to_all.11.recv_ref, s32[1,2048]{1,0:T(1,128)S(1)} %copy-done), custom_call_target="tpu_custom_call" | custom-call | tf_op jit(solution)/shard_map/pick/pallas_call | solution.py:477
Async XLA Ops:
  39.5 3.2 %collective-permute-start = (f32[112,512]{1,0:T(8,128)S(1)}, f32[112,512]{1,0:T(8,128)S(1)}, u32[]{:S(2)}, u32[]{:S(2)}) collective-permute-start(f32[112,512]{1,0:T(8,128)S(1)} %get-tuple-element.13), channel_id=1, source_target_pairs={{0,1},{1,0},{2,3},{3,2},{6,7},{7,6},{4,5},{5,4},{8,9},{9,8},{10,11... | collective-permute-start | bytes 688136 | tf_op jit(solution)/shard_map/ppermute | solution.py:461
  39.6 7.3 %collective-permute-start.1 = (f32[112,512]{1,0:T(8,128)S(1)}, f32[112,512]{1,0:T(8,128)S(1)}, u32[]{:S(2)}, u32[]{:S(2)}) collective-permute-start(f32[112,512]{1,0:T(8,128)S(1)} %get-tuple-element.14), channel_id=1, source_target_pairs={{1,2},{2,1},{3,6},{6,3},{7,4},{4,7},{5,8},{8,5},{9,10},{10,9},{11,... | collective-permute-start | bytes 688136 | tf_op jit(solution)/shard_map/ppermute | solution.py:461
  51.9 26.5 %copy-start = (s32[1,2048]{1,0:T(1,128)S(1)}, s32[1,2048]{1,0:T(1,128)}, u32[]{:S(2)}) copy-start(s32[1,2048]{1,0:T(1,128)} %get-tuple-element.16.pos_ref) | copy-start | bytes 24580

commit v3 on v2

--- a/solution.py
+++ b/solution.py
@@ -12,6 +12,7 @@
 SUBSTEPS = 2
 LANES = 128
 TILE = 256
+GROUP = 512
 STRIDE = 40
 F32 = jnp.float32
 BF16 = jnp.bfloat16
@@ -65,8 +66,9 @@
 
 
 def one_hot(row, start, width):
-    ids = lax.broadcasted_iota(jnp.int32, (TILE, width), 0)
-    return (ids == (row - start)).astype(F32).astype(BF16)
+    ids = lax.broadcasted_iota(jnp.int32, (TILE, width), 0).astype(F32).astype(BF16)
+    wanted = (row - start).astype(F32).astype(BF16)
+    return jnp.where(ids == wanted, jnp.ones((), BF16), jnp.zeros((), BF16))
 
 
 def matmul_nt(data, table):
@@ -135,46 +137,61 @@
         pos_ref[:, c * LANES : (c + 1) * LANES] = where_to.astype(jnp.int32)
     for copy in copies[2:]:
         copy.wait()
-    total = jnp.zeros((1, points), F32)
-    for f in range(freqs):
-        x = spec_ref[f]
-        dbl[f, 0:dirs, :] = x
-        dbl[f, dirs : 2 * dirs, :] = x
-        total = total + jnp.sum(x, axis=0, keepdims=True)
-    mean = total * (1.0 / (freqs * dirs))
     cos_a, sin_a = direction_trig(dirs, dirs)
-    along = wind_ref[0:1, :] * cos_a[:, 0:1] + wind_ref[1:2, :] * sin_a[:, 0:1]
-    drive = jnp.maximum(along - 0.3, 0.0)
     span = -(-(dirs + dirs // 4) // 8) * 8
-    for f in range(freqs):
-        x = spec_ref[f]
-        ahead = pltpu.roll(dbl[f, 0:span, :], span - shift_ref[0], 0)[0:dirs]
-        offset = 2 * dirs - span
-        behind = pltpu.roll(dbl[f, offset:, :], shift_ref[1] + span - (dirs - offset), 0)[0:dirs]
-        out = x * jnp.exp((0.15 + 0.05 * f) * drive - (0.2 + 0.1 * f) * mean) + 0.1 * (
-            ahead * behind - x * x
-        )
-        dbl[f, 0:dirs, :] = out
+    offset = 2 * dirs - span
     extra = rows - freqs * dirs
-    local = (lax.bitwise_and(dest, points - 1) + 1).astype(F32)
-    whole = jnp.concatenate(
-        [dbl[f, 0:dirs, :] for f in range(freqs)] + [jnp.broadcast_to(local, (extra, points))],
-        axis=0,
-    )
-    high, low = split(whole)
-    lhs[0:rows, :] = high
-    lhs[rows : 2 * rows, :] = low
-    pos = pos_ref[...]
-
-    def body(t, carry):
-        table = one_hot(pos, t * TILE, points)
-        both = matmul_nt(lhs[...], table)
+
+    def terms(c):
+        where = slice(c * LANES, (c + 1) * LANES)
+        total = jnp.zeros((1, LANES), F32)
+        for f in range(freqs):
+            x = spec_ref[f, :, where]
+            dbl[f, 0:dirs, where] = x
+            dbl[f, dirs : 2 * dirs, where] = x
+            total = total + jnp.sum(x, axis=0, keepdims=True)
+        mean = total * (1.0 / (freqs * dirs))
+        along = wind_ref[0:1, where] * cos_a + wind_ref[1:2, where] * sin_a
+        drive = jnp.maximum(along - 0.3, 0.0)
+        pieces = []
+        for f in range(freqs):
+            x = spec_ref[f, :, where]
+            ahead = pltpu.roll(dbl[f, 0:span, where], span - shift_ref[0], 0)[0:dirs]
+            behind = pltpu.roll(
+                dbl[f, offset:, where], shift_ref[1] + span - (dirs - offset), 0
+            )[0:dirs]
+            pieces.append(
+                x * jnp.exp((0.15 + 0.05 * f) * drive - (0.2 + 0.1 * f) * mean)
+                + 0.1 * (ahead * behind - x * x)
+            )
+        local = (lax.bitwise_and(dest_ref[:, where], points - 1) + 1).astype(F32)
+        pieces.append(jnp.broadcast_to(local, (extra, LANES)))
+        high, low = split(jnp.concatenate(pieces, axis=0))
+        lhs[0:rows, where] = high
+        lhs[rows : 2 * rows, where] = low
+
+    per_step = TILE // LANES
+
+    def place(t, g):
+        where = slice(g * GROUP, (g + 1) * GROUP)
+        both = matmul_nt(lhs[:, where], one_hot(pos_ref[:, where], t * TILE, GROUP))
         out = both[0:rows] + both[rows : 2 * rows]
-        for h in range(TILE // LANES):
-            send_ref[t * (TILE // LANES) + h] = out[:, h * LANES : (h + 1) * LANES]
-        return carry
-
-    lax.fori_loop(0, points // TILE, body, 0, unroll=True)
+        for h in range(per_step):
+            piece = out[:, h * LANES : (h + 1) * LANES]
+            if g:
+                piece = send_ref[t * per_step + h] + piece
+            send_ref[t * per_step + h] = piece
+
+    groups = points // GROUP
+    chunks = GROUP // LANES
+    steps = points // TILE
+    for g in range(groups + 1):
+        for c in range(chunks):
+            if g < groups:
+                terms(g * chunks + c)
+            if g > 0:
+                for t in range(c * steps // chunks, (c + 1) * steps // chunks):
+                    place(t, g - 1)
 
 
 def spread_rows(get, freqs, dirs, points, lhs):
@@ -243,7 +260,7 @@
 
 
 def step_kernel(
-    freqs, dirs, blocks, field_ref, first_ref, second_ref, cell_ref, back_ref, ext, mid, ends, lhs
+    freqs, dirs, blocks, field_ref, first_ref, second_ref, cell_ref, back_ref, ext, mid, ends, acc, lhs
 ):
     points = field_ref.shape[1]
     rows = freqs * STRIDE
@@ -305,31 +322,28 @@
     cy_base = 0.5 * jnp.abs(sin_a)
     cx_base = 0.25 * jnp.abs(cos_a)
 
-    def advance(src, dst, first, last, shift):
-        for row in range(first, last):
-            spot = (band * row_count + row).astype(F32) + 0.5
-            lat = jnp.full((STRIDE, LANES), spot / rows_all * (2.0 * math.pi / 3.0) - math.pi / 3.0)
-            sec = 1.0 / jnp.cos(lat)
-            tan = jnp.sin(lat) * sec
-            turn = -0.3 * cos_a * tan
-            from_lower = (turn > 0.0)[:, 0:1]
-            sea = sea_of(row)
-            for f in range(freqs):
-                speed = 1.0 / (1.0 + 0.25 * f)
-                cy = (speed * cy_base)[:, 0:1]
-                cx = (speed * cx_base * sec)[:, 0:1]
-                ct = (speed * jnp.abs(turn))[:, 0:1]
-                piece = slice(f * STRIDE, (f + 1) * STRIDE)
-                x = src[piece, lanes(row + shift)]
-                meridional = jnp.where(
-                    from_south, src[piece, lanes(row + shift - 1)], src[piece, lanes(row + shift + 1)]
-                )
-                zonal = jnp.where(from_west, roll_lanes(x, 1), roll_lanes(x, -1))
-                adv = (x - cy * (x - meridional) - cx * (x - zonal)) * sea
-                lower = pltpu.roll(adv, 1, 0)
-                upper = pltpu.roll(adv, STRIDE - 1, 0)
-                out = (adv - ct * (adv - jnp.where(from_lower, lower, upper))) * sea
-                dst(f, row, out)
+    def advance(src, dst, row, f, shift):
+        spot = (band * row_count + row).astype(F32) + 0.5
+        lat = jnp.full((STRIDE, LANES), spot / rows_all * (2.0 * math.pi / 3.0) - math.pi / 3.0)
+        sec = 1.0 / jnp.cos(lat)
+        tan = jnp.sin(lat) * sec
+        turn = -0.3 * cos_a * tan
+        from_lower = (turn > 0.0)[:, 0:1]
+        sea = sea_of(row)
+        speed = 1.0 / (1.0 + 0.25 * f)
+        cy = (speed * cy_base)[:, 0:1]
+        cx = (speed * cx_base * sec)[:, 0:1]
+        ct = (speed * jnp.abs(turn))[:, 0:1]
+        piece = slice(f * STRIDE, (f + 1) * STRIDE)
+        x = src[piece, lanes(row + shift)]
+        meridional = jnp.where(
+            from_south, src[piece, lanes(row + shift - 1)], src[piece, lanes(row + shift + 1)]
+        )
+        zonal = jnp.where(from_west, roll_lanes(x, 1), roll_lanes(x, -1))
+        adv = (x - cy * (x - meridional) - cx * (x - zonal)) * sea
+        lower = pltpu.roll(adv, 1, 0)
+        upper = pltpu.roll(adv, STRIDE - 1, 0)
+        dst(f, row, (adv - ct * (adv - jnp.where(from_lower, lower, upper))) * sea)
 
     def keep(f, row, out):
         out = jnp.concatenate(
@@ -342,26 +356,38 @@
         lhs[f * STRIDE : (f + 1) * STRIDE, lanes(row)] = high
         lhs[rows + f * STRIDE : rows + (f + 1) * STRIDE, lanes(row)] = low
 
-    advance(ext, keep, -1, row_count + 1, ghost)
-    advance(mid, last, 0, row_count, 1)
-
-    def body(t, carry):
-        where = pl.ds(pl.multiple_of(t * TILE, TILE), TILE)
+    def pick(t, row):
+        where = slice(t * TILE, (t + 1) * TILE)
         cells = cell_ref[:, where]
         table = jnp.concatenate(
-            [one_hot(cells, k * TILE, TILE) for k in range(points // TILE)], axis=0
+            [one_hot(cells, row * NLON + k * TILE, TILE) for k in range(NLON // TILE)], axis=0
         )
-        both = jnp.dot(lhs[...], table, preferred_element_type=F32)
+        both = jnp.dot(lhs[:, lanes(row)], table, preferred_element_type=F32)
         out = both[0:rows] + both[rows : 2 * rows]
+        if row:
+            out = acc[:, where] + out
+        if row < row_count - 1:
+            acc[:, where] = out
+            return
         for h in range(TILE // LANES):
             for q in range(freqs * dirs // 4):
                 low = q // (dirs // 4) * STRIDE + q % (dirs // 4) * 4
                 back_ref[t * (TILE // LANES) + h, q] = out[
                     low : low + 4, h * LANES : (h + 1) * LANES
                 ]
-        return carry
-
-    lax.fori_loop(0, points // TILE, body, 0, unroll=True)
+
+    steps = points // TILE
+    for row in range(-1, 1):
+        for f in range(freqs):
+            advance(ext, keep, row, f, ghost)
+    for row in range(row_count + 1):
+        for f in range(freqs):
+            if row < row_count:
+                advance(ext, keep, row + 1, f, ghost)
+                advance(mid, last, row, f, 1)
+            if row:
+                for t in range(f * steps // freqs, (f + 1) * steps // freqs):
+                    pick(t, row - 1)
 
 
 def pick_kernel(freqs, dirs, recv_ref, pos_ref, out_ref, result, lhs, sems):
@@ -468,6 +494,7 @@
             pltpu.VMEM((rows, points + 2 * SUBSTEPS * NLON), F32),
             pltpu.VMEM((rows, points + 2 * NLON), F32),
             pltpu.VMEM((8, NLON), F32),
+            pltpu.VMEM((rows, points), F32),
             pltpu.VMEM((2 * rows, points), BF16),
         ],
         compiler_params=params,

time: 82.5 us -> 80.9 us (0.981)
  Pallas kernels: 17.1 us -> 15.7 us
where the time goes in v3:
time: 80.9 us; the launch traced here: 80.6 us
  blocking collectives  56.8 us (70%)
  Pallas kernels  15.7 us (19%)
  waiting for transfers between devices  4.24 us (5%)
  starting transfers between devices  3.15 us (4%)
    all_to_all x2, blocking collectives, exchange(): return lax.all_to_all(x, 'blk', split_axis=0, concat_axis=0, tiled=True)  56.8 us
    pallas_call x1, Pallas kernels, per_device(): pl.pallas_call(functools.partial(source_kernel, blocks, cap), out_shape=(...  5.79 us
    pallas_call x1, Pallas kernels, per_device(): pl.pallas_call(functools.partial(step_kernel, freqs, dirs, blocks), out_s...  4.46 us
    ppermute x1, waiting for transfers between devices, per_device(): lax.ppermute(second, 'blk', outer)  4.24 us
    ppermute x1, starting transfers between devices, per_device(): lax.ppermute(second, 'blk', outer)  3.08 us
    pallas_call x1, Pallas kernels, per_device(): pl.pallas_call(functools.partial(pick_kernel, freqs, dirs), out_shape=arr...  3.01 us
    pallas_call x1, Pallas kernels, per_device(): pl.pallas_call(functools.partial(place_kernel, freqs, dirs, blocks), out_...  2.44 us
  transfers between devices with their start and end apart: 2, of which 1 were waited for; matrix products, arithmetic and copies ran while one was open for 0% of the time, Pallas kernels for 0%

profile of v3, /device:TPU:1, one launch (start us, length us, event | category | flops | bytes accessed | tf_op | source)
XLA Modules:
  0.0 80.6 jit_solution(16898436237430140772)
XLA Ops:
  0.7 5.8 %source.1 = (f32[16,112,128]{2,1,0:T(8,128)}, s32[1,2048]{1,0:T(1,128)}) custom-call(s32[2]{0:T(128)} %shift_in.1, s32[1]{0:T(128)S(6)} %copy.6.count_in, f32[3,36,2048]{2,1,0:T(8,128)} %spec_in.1, f32[2,2048]{1,0:T(2,128)} %wind_in.1, s32[1,2048]{1,0:T(1,128)} %bitcast.1), custom_call_target="tpu_custom_call" | custom-call | tf_op jit(solution)/shard_map/source/pallas_call | solution.py:453
  6.5 30.3 %all_to_all.10.recv_ref = f32[16,112,128]{2,1,0:T(8,128)S(1)} all-to-all(f32[16,112,128]{2,1,0:T(8,128)} %get-tuple-element.11), channel_id=1, replica_groups=mesh['groups'=2,'blk'=16] {'blk'}, dimensions={0} | all-to-all | bytes 1835008 | tf_op jit(solution)/shard_map/all_to_all | solution.py:429
  36.7 2.4 %place.1 = (f32[120,2048]{1,0:T(8,128)S(1)}, f32[112,512]{1,0:T(8,128)S(1)}, f32[112,512]{1,0:T(8,128)S(1)}, s32[1,2048]{1,0:T(1,128)S(1)}) custom-call(f32[16,112,128]{2,1,0:T(8,128)S(1)} %all_to_all.10.recv_ref), custom_call_target="tpu_custom_call" | custom-call | tf_op jit(solution)/shard_map/place/pallas_call | solution.py:472
  39.2 0.1 collective-permute-start
  39.3 3.1 %collective-permute-start.1 = (f32[112,512]{1,0:T(8,128)S(1)}, f32[112,512]{1,0:T(8,128)S(1)}, u32[]{:S(2)}, u32[]{:S(2)}) collective-permute-start(f32[112,512]{1,0:T(8,128)S(1)} %get-tuple-element.14), channel_id=1, source_target_pairs={{1,2},{2,1},{3,6},{6,3},{7,4},{4,7},{5,8},{8,5},{9,10},{10,9},{11,... | collective-permute-start | bytes 688136 | tf_op jit(solution)/shard_map/ppermute | solution.py:487
  42.3 0.0 collective-permute-done.first_ref
  42.4 4.2 %collective-permute-done.1.second_ref = f32[112,512]{1,0:T(8,128)S(1)} collective-permute-done((f32[112,512]{1,0:T(8,128)S(1)}, f32[112,512]{1,0:T(8,128)S(1)}, u32[]{:S(2)}, u32[]{:S(2)}) %collective-permute-start.1) | collective-permute-done | bytes 229408 | tf_op jit(solution)/shard_map/ppermute | solution.py:487
  46.6 4.5 %step.1 = f32[16,27,4,128]{3,2,1,0:T(4,128)S(1)} custom-call(f32[120,2048]{1,0:T(8,128)S(1)} %get-tuple-element.12.field_ref, f32[112,512]{1,0:T(8,128)S(1)} %collective-permute-done.first_ref, f32[112,512]{1,0:T(8,128)S(1)} %collective-permute-done.1.second_ref, s32[1,2048]{1,0:T(1,128)S(1)} %get-tuple-element.15.cell_ref), custom_call_target="tpu_custom_call" | custom-call | tf_op jit(solution)/shard_map/step/pallas_call | solution.py:488
  51.1 0.0 copy-start
  51.1 26.5 %all_to_all.11.recv_ref = f32[16,27,4,128]{3,2,1,0:T(4,128)S(1)} all-to-all(f32[16,27,4,128]{3,2,1,0:T(4,128)S(1)} %step.1), channel_id=1, replica_groups=mesh['groups'=2,'blk'=16] {'blk'}, dimensions={0} | all-to-all | bytes 1769472 | tf_op jit(solution)/shard_map/all_to_all | solution.py:429
  77.6 0.0 copy-done
  77.6 3.0 %pick.1 = f32[3,36,2048]{2,1,0:T(8,128)} custom-call(f32[16,27,4,128]{3,2,1,0:T(4,128)S(1)} %all_to_all.11.recv_ref, s32[1,2048]{1,0:T(1,128)S(1)} %copy-done), custom_call_target="tpu_custom_call" | custom-call | tf_op jit(solution)/shard_map/pick/pallas_call | solution.py:504
Async XLA Ops:
  39.2 3.2 %collective-permute-start = (f32[112,512]{1,0:T(8,128)S(1)}, f32[112,512]{1,0:T(8,128)S(1)}, u32[]{:S(2)}, u32[]{:S(2)}) collective-permute-start(f32[112,512]{1,0:T(8,128)S(1)} %get-tuple-element.13), channel_id=1, source_target_pairs={{0,1},{1,0},{2,3},{3,2},{6,7},{7,6},{4,5},{5,4},{8,9},{9,8},{10,11... | collective-permute-start | bytes 688136 | tf_op jit(solution)/shard_map/ppermute | solution.py:487
  39.3 7.3 %collective-permute-start.1 = (f32[112,512]{1,0:T(8,128)S(1)}, f32[112,512]{1,0:T(8,128)S(1)}, u32[]{:S(2)}, u32[]{:S(2)}) collective-permute-start(f32[112,512]{1,0:T(8,128)S(1)} %get-tuple-element.14), channel_id=1, source_target_pairs={{1,2},{2,1},{3,6},{6,3},{7,4},{4,7},{5,8},{8,5},{9,10},{10,9},{11,... | collective-permute-start | bytes 688136 | tf_op jit(solution)/shard_map/ppermute | solution.py:487
  51.1 26.5 %copy-start = (s32[1,2048]{1,0:T(1,128)S(1)}, s32[1,2048]{1,0:T(1,128)}, u32[]{:S(2)}) copy-start(s32[1,2048]{1,0:T(1,128)} %get-tuple-element.16.pos_ref) | copy-start | bytes 24580

commit v4 on v3

--- a/solution.py
+++ b/solution.py
@@ -81,6 +81,17 @@
     j = lax.broadcasted_iota(jnp.int32, (rows, LANES), 0)
     angles = (2.0 * math.pi / dirs) * j.astype(F32)
     return jnp.cos(angles), jnp.sin(angles)
+
+
+def shifted(x, shift, size):
+    count = x.shape[0] // 8
+    fine = lax.rem(shift, 8)
+    back = lax.rem(8 - fine, 8)
+    keep = lax.broadcasted_iota(jnp.int32, (8, LANES), 0) < 8 - fine
+    tiles = [pltpu.roll(x[8 * k : 8 * k + 8], back, 0) for k in range(count)]
+    near = [jnp.where(keep, a, b) for a, b in zip(tiles, tiles[1:] + tiles[-1:])]
+    out = [jnp.where(shift >= 8, b, a) for a, b in zip(near, near[1:] + near[-1:])]
+    return jnp.concatenate(out, axis=0)[0:size]
 
 
 def source_kernel(
@@ -156,10 +167,8 @@
         pieces = []
         for f in range(freqs):
             x = spec_ref[f, :, where]
-            ahead = pltpu.roll(dbl[f, 0:span, where], span - shift_ref[0], 0)[0:dirs]
-            behind = pltpu.roll(
-                dbl[f, offset:, where], shift_ref[1] + span - (dirs - offset), 0
-            )[0:dirs]
+            ahead = shifted(dbl[f, 0:span, where], shift_ref[0], dirs)
+            behind = shifted(dbl[f, offset:, where], dirs - offset - shift_ref[1], dirs)
             pieces.append(
                 x * jnp.exp((0.15 + 0.05 * f) * drive - (0.2 + 0.1 * f) * mean)
                 + 0.1 * (ahead * behind - x * x)
@@ -208,151 +217,264 @@
         lhs[rows : 2 * rows, c * LANES : (c + 1) * LANES] = low
 
 
-def place_kernel(freqs, dirs, blocks, recv_ref, field_ref, first_ref, second_ref, cell_ref, lhs):
+def edge_kernel(
+    freqs, dirs, blocks, recv_ref, first_ref, second_ref, cell_ref, south_lhs, north_lhs, wide
+):
+    points = cell_ref.shape[1]
+    label = freqs * dirs
+    half = dirs // 2
+    rows = south_lhs.shape[0] // 2
+    near_rows = freqs * (half + 1) + 1
+    fill = jnp.ones((rows - freqs * (half + 1), LANES), F32)
+    for c in range(points // LANES):
+        where = slice(c * LANES, (c + 1) * LANES)
+        own = recv_ref[c, label : label + 1, :].astype(jnp.int32) - 1
+        cell_ref[:, where] = own
+        wide[where, :] = jnp.broadcast_to(own, (LANES, LANES)).T.astype(jnp.int16)
+        x = recv_ref[c]
+        for lhs, start, other in ((south_lhs, 0, half), (north_lhs, half, 0)):
+            pieces = []
+            for f in range(freqs):
+                base = f * dirs
+                pieces.append(x[base + start : base + start + half])
+                pieces.append(x[base + other : base + other + 1])
+            high, low = split(jnp.concatenate(pieces + [fill], axis=0))
+            lhs[0:rows, where] = high
+            lhs[rows : 2 * rows, where] = low
+    ids = lax.broadcasted_iota(jnp.int32, (1, LANES), 1)
+
+    def side(out_ref, lhs, row, near):
+        for t in range(NLON // TILE):
+            start = row * NLON + t * TILE
+            table = jnp.concatenate(
+                [
+                    jnp.where(
+                        wide[...] == (ids + (start + h * LANES)).astype(jnp.int16),
+                        jnp.ones((), BF16),
+                        jnp.zeros((), BF16),
+                    )
+                    for h in range(TILE // LANES)
+                ],
+                axis=1,
+            )
+            both = jnp.dot(lhs[...], table, preferred_element_type=F32)
+            out = both[0:rows] + both[rows : 2 * rows]
+            where = slice(t * TILE, (t + 1) * TILE)
+            if near:
+                out_ref[0:near_rows, where] = out[0:near_rows]
+                continue
+            for f in range(freqs):
+                at = near_rows + f * (half - 1)
+                low = f * (half + 1) + 1
+                out_ref[at : at + half - 1, where] = out[low : low + half - 1]
+
+    top = points // NLON - 1
+    even = lax.rem(snake(lax.axis_index("blk"), blocks), 2) == 0
+
+    def sides(up_ref, down_ref):
+        side(up_ref, south_lhs, top, True)
+        side(up_ref, south_lhs, top - 1, False)
+        side(down_ref, north_lhs, 0, True)
+        side(down_ref, north_lhs, 1, False)
+
+    @pl.when(even)
+    def _():
+        sides(first_ref, second_ref)
+
+    @pl.when(jnp.logical_not(even))
+    def _():
+        sides(second_ref, first_ref)
+
+
+def lanes(row):
+    return slice(row * NLON, (row + 1) * NLON)
+
+
+def stepper(freqs, dirs, blocks, row_count):
+    band = snake(lax.axis_index("blk"), blocks)
+    rows_all = row_count * blocks
+    half = dirs // 2
+    at = lax.broadcasted_iota(jnp.int32, (STRIDE, LANES), 0)
+    j = jnp.where(at < dirs, at, jnp.where(at < STRIDE - 1, at - dirs, dirs - 1))
+    angles = (2.0 * math.pi / dirs) * j.astype(F32)
+    sin_a = jnp.where((j == 0) | (j == half), 0.0, jnp.sin(angles))
+    cos_a = jnp.cos(angles)
+    from_south = (at <= half)[:, 0:1]
+    from_west = (cos_a > 0.0)[:, 0:1]
+    cy_base = 0.5 * jnp.abs(sin_a)
+    cx_base = 0.25 * jnp.abs(cos_a)
+
+    index = [k if k < dirs else (k - dirs if k < STRIDE - 1 else dirs - 1) for k in range(STRIDE)]
+    cosines = [math.cos(2.0 * math.pi * k / dirs) for k in index]
+
+    def by_tile(low, high, values, mask, one, other):
+        out = []
+        for k in range(low, high, 8):
+            signs = {v > 0 for v in values[k : k + 8] if abs(v) > 1e-9}
+            if signs == {True}:
+                out.append(one(k - low))
+            elif signs == {False}:
+                out.append(other(k - low))
+            else:
+                out.append(jnp.where(mask[k : k + 8], one(k - low), other(k - low)))
+        return jnp.concatenate(out, axis=0)
+
+    norths = [1 if k <= half else -1 for k in range(STRIDE)]
+    latitudes = {}
+
+    def latitude(row):
+        if row not in latitudes:
+            spot = (band * row_count + row).astype(F32) + 0.5
+            lat = jnp.full((8, LANES), spot / rows_all * (2.0 * math.pi / 3.0) - math.pi / 3.0)
+            sec = 1.0 / jnp.cos(lat)
+            turn = -0.3 * cos_a * (jnp.sin(lat) * sec)[0:1]
+            latitudes[row] = (
+                (cx_base * sec[0:1])[:, 0:1],
+                jnp.abs(turn)[:, 0:1],
+                (turn > 0.0)[:, 0:1],
+            )
+        return latitudes[row]
+
+    def advance(get, row, f, sea, low=0, high=STRIDE):
+        part = slice(low, high)
+        cx, ct, from_lower = latitude(row)
+        speed = 1.0 / (1.0 + 0.25 * f)
+        cy = (speed * cy_base)[part, 0:1]
+        cx = (speed * cx)[part]
+        ct = (speed * ct)[part]
+        base = f * STRIDE + low
+        x = get(row, slice(base, base + high - low))
+
+        def rows_of(r):
+            return lambda k: get(r, slice(base + k, base + k + 8))
+
+        def turned_by(shift):
+            return lambda k: pltpu.roll(x[k : k + 8], shift % NLON, 1)
+
+        meridional = by_tile(low, high, norths, from_south, rows_of(row - 1), rows_of(row + 1))
+        zonal = by_tile(low, high, cosines, from_west, turned_by(1), turned_by(-1))
+        adv = (x - cy * (x - meridional) - cx * (x - zonal)) * sea
+        lower = pltpu.roll(adv, 1, 0)
+        upper = pltpu.roll(adv, high - low - 1, 0)
+        return (adv - ct * (adv - jnp.where(from_lower[part], lower, upper))) * sea
+
+    return advance
+
+
+def repeat_ends(out, dirs):
+    return jnp.concatenate(
+        [out[0:dirs], out[0:1], out[dirs + 1 : STRIDE - 1], out[dirs - 1 : dirs]], axis=0
+    )
+
+
+def place_kernel(freqs, dirs, blocks, recv_ref, cell_ref, field_ref, inner_ref, lhs):
     points = cell_ref.shape[1]
     rows = freqs * STRIDE
-    label = freqs * dirs
-    for c in range(points // LANES):
-        cell_ref[:, c * LANES : (c + 1) * LANES] = (
-            recv_ref[c, label : label + 1, :].astype(jnp.int32) - 1
-        )
+    row_count = points // NLON
     spread_rows(lambda c: recv_ref[c], freqs, dirs, points, lhs)
     cells = cell_ref[...]
-
-    def body(t, carry):
-        table = one_hot(cells, t * TILE, points)
-        both = matmul_nt(lhs[...], table)
-        where = pl.ds(pl.multiple_of(t * TILE, TILE), TILE)
-        field_ref[:, where] = both[0:rows] + both[rows : 2 * rows]
-        return carry
-
-    lax.fori_loop(0, points // TILE, body, 0, unroll=True)
-    half = dirs // 2
-    width = half + 1
-    last = points - NLON
-
-    def edge(out_ref, near, far, skip):
-        at = 0
-        for start, extra in ((near, 0), (far, 1)):
-            for f in range(freqs):
-                low = f * STRIDE + skip + extra
-                high = f * STRIDE + skip + width - extra
-                out_ref[at : at + high - low, :] = field_ref[low:high, start : start + NLON]
-                at += high - low
-        mask = field_ref[dirs + 1 : dirs + 2, near : near + NLON]
-        out_ref[at:, :] = jnp.broadcast_to(mask, (out_ref.shape[0] - at, NLON))
-
-    even = lax.rem(snake(lax.axis_index("blk"), blocks), 2) == 0
-
-    @pl.when(even)
-    def _():
-        edge(first_ref, last, last - NLON, 0)
-        edge(second_ref, 0, NLON, half)
-
-    @pl.when(jnp.logical_not(even))
-    def _():
-        edge(second_ref, last, last - NLON, 0)
-        edge(first_ref, 0, NLON, half)
-
-
-def roll_lanes(x, shift):
-    return pltpu.roll(x, shift % x.shape[1], 1)
+    for t in range(points // TILE):
+        both = matmul_nt(lhs[...], one_hot(cells, t * TILE, points))
+        field_ref[:, t * TILE : (t + 1) * TILE] = both[0:rows] + both[rows : 2 * rows]
+    advance = stepper(freqs, dirs, blocks, row_count)
+    for row in range(1, row_count - 1):
+        sea = field_ref[dirs + 1 : dirs + 2, lanes(row)]
+        for f in range(freqs):
+            out = advance(lambda r, piece: field_ref[piece, lanes(r)], row, f, sea)
+            inner_ref[f * STRIDE : (f + 1) * STRIDE, lanes(row - 1)] = repeat_ends(out, dirs)
 
 
 def step_kernel(
-    freqs, dirs, blocks, field_ref, first_ref, second_ref, cell_ref, back_ref, ext, mid, ends, acc, lhs
+    freqs,
+    dirs,
+    blocks,
+    field_ref,
+    inner_ref,
+    first_ref,
+    second_ref,
+    cell_ref,
+    back_ref,
+    south,
+    north,
+    outer,
+    acc,
+    lhs,
 ):
     points = field_ref.shape[1]
     rows = freqs * STRIDE
     row_count = points // NLON
     half = dirs // 2
-    width = half + 1
-    ghost = SUBSTEPS
-    band = snake(lax.axis_index("blk"), blocks)
-    rows_all = row_count * blocks
-
-    def lanes(row):
-        return slice(row * NLON, (row + 1) * NLON)
-
-    ext[:, 0 : ghost * NLON] = jnp.zeros((rows, ghost * NLON), F32)
-    ext[:, (ghost + row_count) * NLON :] = jnp.zeros((rows, ghost * NLON), F32)
-    ext[:, ghost * NLON : (ghost + row_count) * NLON] = field_ref[...]
-
-    def fill(in_ref, near, far, skip, end):
-        at = 0
-        for row, extra in ((near, 0), (far, 1)):
-            for f in range(freqs):
-                low = f * STRIDE + skip + extra
-                high = f * STRIDE + skip + width - extra
-                ext[low:high, lanes(row)] = in_ref[at : at + high - low, :]
-                at += high - low
-        if skip:
-            for f in range(freqs):
-                spot = f * width + dirs - 1 - half
-                top = (f + 1) * STRIDE
-                ext[top - 1 : top, lanes(near)] = in_ref[spot : spot + 1, :]
-        ends[end : end + 1, :] = in_ref[at : at + 1, :]
-
-    even = lax.rem(band, 2) == 0
+    inside = half - 1
+    near_rows = freqs * (half + 1) + 1
+    top = row_count - 1
+
+    def fill(ghost, in_ref, start):
+        ghost[0:rows, lanes(1)] = jnp.zeros((rows, NLON), F32)
+        for f in range(freqs):
+            base = f * STRIDE + start
+            at = f * (half + 1)
+            ghost[base : base + half + 1, lanes(0)] = in_ref[at : at + half + 1, :]
+            if start:
+                top_row = (f + 1) * STRIDE - 1
+                ghost[top_row : top_row + 1, lanes(0)] = in_ref[at + half - 1 : at + half, :]
+            at = near_rows + f * inside
+            ghost[base + 1 : base + half, lanes(1)] = in_ref[at : at + inside, :]
+        ghost[rows : rows + 1, lanes(0)] = in_ref[near_rows - 1 : near_rows, :]
+
+    even = lax.rem(snake(lax.axis_index("blk"), blocks), 2) == 0
 
     @pl.when(even)
     def _():
-        fill(second_ref, ghost - 1, ghost - 2, 0, 0)
-        fill(first_ref, ghost + row_count, ghost + row_count + 1, half, 1)
+        fill(south, second_ref, 0)
+        fill(north, first_ref, half)
 
     @pl.when(jnp.logical_not(even))
     def _():
-        fill(first_ref, ghost - 1, ghost - 2, 0, 0)
-        fill(second_ref, ghost + row_count, ghost + row_count + 1, half, 1)
+        fill(south, first_ref, 0)
+        fill(north, second_ref, half)
 
     def sea_of(row):
         if row < 0:
-            return ends[0:1, :]
-        if row >= row_count:
-            return ends[1:2, :]
+            return south[rows : rows + 1, lanes(0)]
+        if row > top:
+            return north[rows : rows + 1, lanes(0)]
         return field_ref[dirs + 1 : dirs + 2, lanes(row)]
 
-    j = lax.broadcasted_iota(jnp.int32, (STRIDE, LANES), 0)
-    j = jnp.where(j < dirs, j, jnp.where(j < STRIDE - 1, j - dirs, dirs - 1))
-    angles = (2.0 * math.pi / dirs) * j.astype(F32)
-    sin_a = jnp.where((j == 0) | (j == half), 0.0, jnp.sin(angles))
-    cos_a = jnp.cos(angles)
-    from_south = (sin_a > 0.0)[:, 0:1]
-    from_west = (cos_a > 0.0)[:, 0:1]
-    cy_base = 0.5 * jnp.abs(sin_a)
-    cx_base = 0.25 * jnp.abs(cos_a)
-
-    def advance(src, dst, row, f, shift):
-        spot = (band * row_count + row).astype(F32) + 0.5
-        lat = jnp.full((STRIDE, LANES), spot / rows_all * (2.0 * math.pi / 3.0) - math.pi / 3.0)
-        sec = 1.0 / jnp.cos(lat)
-        tan = jnp.sin(lat) * sec
-        turn = -0.3 * cos_a * tan
-        from_lower = (turn > 0.0)[:, 0:1]
-        sea = sea_of(row)
-        speed = 1.0 / (1.0 + 0.25 * f)
-        cy = (speed * cy_base)[:, 0:1]
-        cx = (speed * cx_base * sec)[:, 0:1]
-        ct = (speed * jnp.abs(turn))[:, 0:1]
-        piece = slice(f * STRIDE, (f + 1) * STRIDE)
-        x = src[piece, lanes(row + shift)]
-        meridional = jnp.where(
-            from_south, src[piece, lanes(row + shift - 1)], src[piece, lanes(row + shift + 1)]
-        )
-        zonal = jnp.where(from_west, roll_lanes(x, 1), roll_lanes(x, -1))
-        adv = (x - cy * (x - meridional) - cx * (x - zonal)) * sea
-        lower = pltpu.roll(adv, 1, 0)
-        upper = pltpu.roll(adv, STRIDE - 1, 0)
-        dst(f, row, (adv - ct * (adv - jnp.where(from_lower, lower, upper))) * sea)
-
-    def keep(f, row, out):
-        out = jnp.concatenate(
-            [out[0:dirs], out[0:1], out[dirs + 1 : STRIDE - 1], out[dirs - 1 : dirs]], axis=0
-        )
-        mid[f * STRIDE : (f + 1) * STRIDE, lanes(row + 1)] = out
-
-    def last(f, row, out):
-        high, low = split(out)
+    def before(row, piece):
+        if row < 0:
+            return south[piece, lanes(-1 - row)]
+        if row > top:
+            return north[piece, lanes(row - top - 1)]
+        return field_ref[piece, lanes(row)]
+
+    places = {-1: 0, 0: 1, top: 2, top + 1: 3}
+
+    def between(row, piece):
+        if row in places:
+            return outer[piece, lanes(places[row])]
+        return inner_ref[piece, lanes(row - 1)]
+
+    advance = stepper(freqs, dirs, blocks, row_count)
+    south_high = -(-(half + 1) // 8) * 8
+    north_low = half // 8 * 8
+
+    def first_step(row, f):
+        base = f * STRIDE
+        where = lanes(places[row])
+        if row < 0:
+            out = advance(before, row, f, sea_of(row), 0, south_high)
+            outer[base : base + south_high, where] = out
+        elif row > top:
+            out = advance(before, row, f, sea_of(row), north_low, STRIDE)
+            outer[base + north_low : base + STRIDE, where] = out
+            spot = dirs - 1 - north_low
+            outer[base + STRIDE - 1 : base + STRIDE, where] = out[spot : spot + 1]
+        else:
+            out = advance(before, row, f, sea_of(row))
+            outer[base : base + STRIDE, where] = repeat_ends(out, dirs)
+
+    def second_step(row, f):
+        high, low = split(advance(between, row, f, sea_of(row)))
         lhs[f * STRIDE : (f + 1) * STRIDE, lanes(row)] = high
         lhs[rows + f * STRIDE : rows + (f + 1) * STRIDE, lanes(row)] = low
 
@@ -366,7 +488,7 @@
         out = both[0:rows] + both[rows : 2 * rows]
         if row:
             out = acc[:, where] + out
-        if row < row_count - 1:
+        if row < top:
             acc[:, where] = out
             return
         for h in range(TILE // LANES):
@@ -377,14 +499,13 @@
                 ]
 
     steps = points // TILE
-    for row in range(-1, 1):
-        for f in range(freqs):
-            advance(ext, keep, row, f, ghost)
+    for row in places:
+        for f in range(freqs):
+            first_step(row, f)
     for row in range(row_count + 1):
         for f in range(freqs):
             if row < row_count:
-                advance(ext, keep, row + 1, f, ghost)
-                advance(mid, last, row, f, 1)
+                second_step(row, f)
             if row:
                 for t in range(f * steps // freqs, (f + 1) * steps // freqs):
                     pick(t, row - 1)
@@ -442,7 +563,10 @@
     pieces = points // LANES
     rows = freqs * STRIDE
     send_rows = -(-(freqs * dirs + 1) // 8) * 8
-    edge_rows = -(-(2 * freqs * (dirs // 2) + 1) // 8) * 8
+    near_rows = freqs * (dirs // 2 + 1) + 1
+    far_rows = freqs * (dirs // 2 - 1)
+    edge_rows = -(-(near_rows + far_rows) // 8) * 8
+    edge_lhs = -(-near_rows // 8) * 8
     vmem = pl.BlockSpec(memory_space=pltpu.VMEM)
     hbm = pl.BlockSpec(memory_space=pltpu.HBM)
     params = pltpu.CompilerParams(vmem_limit_bytes=VMEM_LIMIT)
@@ -469,37 +593,52 @@
         name="source",
     )(dia_shift, counts, spectrum, wind_vector, dest_cell.reshape(1, points))
     arrived = exchange(send, blocks, cap)
-    field, first, second, cells = pl.pallas_call(
-        functools.partial(place_kernel, freqs, dirs, blocks),
+    first, second, cells = pl.pallas_call(
+        functools.partial(edge_kernel, freqs, dirs, blocks),
         out_shape=(
-            arr((rows, points)),
             arr((edge_rows, NLON)),
             arr((edge_rows, NLON)),
             arr((1, points), jnp.int32),
         ),
         in_specs=[vmem],
-        out_specs=(vmem, vmem, vmem, vmem),
-        scratch_shapes=[pltpu.VMEM((2 * rows, points), BF16)],
+        out_specs=(vmem,) * 3,
+        scratch_shapes=[
+            pltpu.VMEM((2 * edge_lhs, points), BF16),
+            pltpu.VMEM((2 * edge_lhs, points), BF16),
+            pltpu.VMEM((points, LANES), jnp.int16),
+        ],
         compiler_params=params,
-        name="place",
+        name="edges",
     )(arrived)
     inner, outer = halo_swaps(blocks)
     mine, theirs = lax.ppermute(first, "blk", inner), lax.ppermute(second, "blk", outer)
+    field, middle = pl.pallas_call(
+        functools.partial(place_kernel, freqs, dirs, blocks),
+        out_shape=(arr((rows, points)), arr((rows, points - 2 * NLON))),
+        in_specs=[vmem] * 2,
+        out_specs=(vmem,) * 2,
+        scratch_shapes=[pltpu.VMEM((2 * rows, points), BF16)],
+        compiler_params=params,
+        cost_estimate=pl.CostEstimate(
+            flops=4 * rows * points * points, bytes_accessed=8 * rows * points, transcendentals=0
+        ),
+        name="place",
+    )(arrived, cells)
     back = pl.pallas_call(
         functools.partial(step_kernel, freqs, dirs, blocks),
         out_shape=arr((pieces, freqs * dirs // 4, 4, LANES)),
-        in_specs=[vmem] * 4,
+        in_specs=[vmem] * 5,
         out_specs=vmem,
         scratch_shapes=[
-            pltpu.VMEM((rows, points + 2 * SUBSTEPS * NLON), F32),
-            pltpu.VMEM((rows, points + 2 * NLON), F32),
-            pltpu.VMEM((8, NLON), F32),
+            pltpu.VMEM((rows + 8, 2 * NLON), F32),
+            pltpu.VMEM((rows + 8, 2 * NLON), F32),
+            pltpu.VMEM((rows, 4 * NLON), F32),
             pltpu.VMEM((rows, points), F32),
             pltpu.VMEM((2 * rows, points), BF16),
         ],
         compiler_params=params,
         name="step",
-    )(field, mine, theirs, cells)
+    )(field, middle, mine, theirs, cells)
     returned = exchange(back, blocks, cap)
     return pl.pallas_call(
         functools.partial(pick_kernel, freqs, dirs),

time: 80.9 us -> 80.1 us (level)
  waiting for transfers between devices: 4.24 us -> 1.57 us
  Pallas kernels: 15.7 us -> 17.3 us
    ppermute x1, waiting for transfers between devices: 4.24 us -> 1.57 us  [per_device(): lax.ppermute(second, 'blk', outer)]
    pallas_call x0 -> x1, Pallas kernels: none -> 2.28 us  [per_device(): pl.pallas_call(functools.partial(edge_kernel, freqs, dirs, blocks), out_s...]
  transfers between devices with their start and end apart: 2 -> 2, of which waited for: 1 -> 1; matrix products, arithmetic and copies ran while one was open for 0% -> 0% of each run, Pallas kernels for 0% -> 3%
where the time goes in v4:
time: 80.1 us; the launch traced here: 79.7 us
  blocking collectives  56.8 us (71%)
  Pallas kernels  17.3 us (22%)
  starting transfers between devices  3.16 us (4%)
  waiting for transfers between devices  1.57 us (2%)
  between operations  0.88 us (1%)
    all_to_all x2, blocking collectives, exchange(): return lax.all_to_all(x, 'blk', split_axis=0, concat_axis=0, tiled=True)  56.8 us
    pallas_call x1, Pallas kernels, per_device(): pl.pallas_call(functools.partial(source_kernel, blocks, cap), out_shape=(...  5.59 us
    pallas_call x1, Pallas kernels, per_device(): pl.pallas_call(functools.partial(step_kernel, freqs, dirs, blocks), out_s...  3.79 us
    ppermute x1, starting transfers between devices, per_device(): lax.ppermute(second, 'blk', outer)  3.09 us
    pallas_call x1, Pallas kernels, per_device(): pl.pallas_call(functools.partial(pick_kernel, freqs, dirs), out_shape=arr...  3.01 us
    pallas_call x1, Pallas kernels, per_device(): pl.pallas_call(functools.partial(place_kernel, freqs, dirs, blocks), out_...  2.66 us
    pallas_call x1, Pallas kernels, per_device(): pl.pallas_call(functools.partial(edge_kernel, freqs, dirs, blocks), out_s...  2.28 us
  transfers between devices with their start and end apart: 2, of which 1 were waited for; matrix products, arithmetic and copies ran while one was open for 0% of the time, Pallas kernels for 3%

profile of v4, /device:TPU:1, one launch (start us, length us, event | category | flops | bytes accessed | tf_op | source)
XLA Modules:
  0.0 79.7 jit_solution(7510502110761827078)
XLA Ops:
  0.7 5.6 %source.1 = (f32[16,112,128]{2,1,0:T(8,128)}, s32[1,2048]{1,0:T(1,128)}) custom-call(s32[2]{0:T(128)} %shift_in.1, s32[1]{0:T(128)S(6)} %copy.6.count_in, f32[3,36,2048]{2,1,0:T(8,128)} %spec_in.1, f32[2,2048]{1,0:T(2,128)} %wind_in.1, s32[1,2048]{1,0:T(1,128)} %bitcast.1), custom_call_target="tpu_custom_call" | custom-call | tf_op jit(solution)/shard_map/source/pallas_call | solution.py:577
  6.2 30.3 %all_to_all.10.recv_ref = f32[16,112,128]{2,1,0:T(8,128)S(1)} all-to-all(f32[16,112,128]{2,1,0:T(8,128)} %get-tuple-element.12), channel_id=1, replica_groups=mesh['groups'=2,'blk'=16] {'blk'}, dimensions={0} | all-to-all | bytes 1835008 | tf_op jit(solution)/shard_map/all_to_all | solution.py:550
  36.5 2.3 %edges.1 = (f32[112,512]{1,0:T(8,128)S(1)}, f32[112,512]{1,0:T(8,128)S(1)}, s32[1,2048]{1,0:T(1,128)S(1)}) custom-call(f32[16,112,128]{2,1,0:T(8,128)S(1)} %all_to_all.10.recv_ref), custom_call_target="tpu_custom_call" | custom-call | tf_op jit(solution)/shard_map/edges/pallas_call | solution.py:596
  38.8 0.1 collective-permute-start
  38.9 3.1 %collective-permute-start.1 = (f32[112,512]{1,0:T(8,128)S(1)}, f32[112,512]{1,0:T(8,128)S(1)}, u32[]{:S(2)}, u32[]{:S(2)}) collective-permute-start(f32[112,512]{1,0:T(8,128)S(1)} %get-tuple-element.17), channel_id=1, source_target_pairs={{1,2},{2,1},{3,6},{6,3},{7,4},{4,7},{5,8},{8,5},{9,10},{10,9},{11,... | collective-permute-start | bytes 688136 | tf_op jit(solution)/shard_map/ppermute | solution.py:614
  42.0 2.7 %place.1 = (f32[120,2048]{1,0:T(8,128)S(1)}, f32[120,1024]{1,0:T(8,128)S(1)}) custom-call(f32[16,112,128]{2,1,0:T(8,128)S(1)} %all_to_all.10.recv_ref, s32[1,2048]{1,0:T(1,128)S(1)} %get-tuple-element.13.cell_ref), custom_call_target="tpu_custom_call" | custom-call | flops 2013265920 | bytes 1966080 | tf_op jit(solution)/shard_map/place/pallas_call | solution.py:615
  44.7 0.0 collective-permute-done.first_ref
  44.7 1.6 %collective-permute-done.1.second_ref = f32[112,512]{1,0:T(8,128)S(1)} collective-permute-done((f32[112,512]{1,0:T(8,128)S(1)}, f32[112,512]{1,0:T(8,128)S(1)}, u32[]{:S(2)}, u32[]{:S(2)}) %collective-permute-start.1) | collective-permute-done | bytes 229408 | tf_op jit(solution)/shard_map/ppermute | solution.py:614
  46.2 3.8 %step.1 = f32[16,27,4,128]{3,2,1,0:T(4,128)S(1)} custom-call(f32[120,2048]{1,0:T(8,128)S(1)} %get-tuple-element.14.field_ref, f32[120,1024]{1,0:T(8,128)S(1)} %get-tuple-element.15.inner_ref, f32[112,512]{1,0:T(8,128)S(1)} %collective-permute-done.first_ref, f32[112,512]{1,0:T(8,128)S(1)} %collective-permute-done.1.second_ref, ...), custom_call_target="tpu_custom_call" | custom-call | tf_op jit(solution)/shard_map/step/pallas_call | solution.py:627
  50.0 0.0 copy-start
  50.0 26.5 %all_to_all.11.recv_ref = f32[16,27,4,128]{3,2,1,0:T(4,128)S(1)} all-to-all(f32[16,27,4,128]{3,2,1,0:T(4,128)S(1)} %step.1), channel_id=1, replica_groups=mesh['groups'=2,'blk'=16] {'blk'}, dimensions={0} | all-to-all | bytes 1769472 | tf_op jit(solution)/shard_map/all_to_all | solution.py:550
  76.6 0.0 copy-done
  76.6 3.0 %pick.1 = f32[3,36,2048]{2,1,0:T(8,128)} custom-call(f32[16,27,4,128]{3,2,1,0:T(4,128)S(1)} %all_to_all.11.recv_ref, s32[1,2048]{1,0:T(1,128)S(1)} %copy-done), custom_call_target="tpu_custom_call" | custom-call | tf_op jit(solution)/shard_map/pick/pallas_call | solution.py:643
Async XLA Ops:
  38.8 5.8 %collective-permute-start = (f32[112,512]{1,0:T(8,128)S(1)}, f32[112,512]{1,0:T(8,128)S(1)}, u32[]{:S(2)}, u32[]{:S(2)}) collective-permute-start(f32[112,512]{1,0:T(8,128)S(1)} %get-tuple-element.16), channel_id=1, source_target_pairs={{0,1},{1,0},{2,3},{3,2},{6,7},{7,6},{4,5},{5,4},{8,9},{9,8},{10,11... | collective-permute-start | bytes 688136 | tf_op jit(solution)/shard_map/ppermute | solution.py:614
  38.9 7.3 %collective-permute-start.1 = (f32[112,512]{1,0:T(8,128)S(1)}, f32[112,512]{1,0:T(8,128)S(1)}, u32[]{:S(2)}, u32[]{:S(2)}) collective-permute-start(f32[112,512]{1,0:T(8,128)S(1)} %get-tuple-element.17), channel_id=1, source_target_pairs={{1,2},{2,1},{3,6},{6,3},{7,4},{4,7},{5,8},{8,5},{9,10},{10,9},{11,... | collective-permute-start | bytes 688136 | tf_op jit(solution)/shard_map/ppermute | solution.py:614
  50.0 26.5 %copy-start = (s32[1,2048]{1,0:T(1,128)S(1)}, s32[1,2048]{1,0:T(1,128)}, u32[]{:S(2)}) copy-start(s32[1,2048]{1,0:T(1,128)} %get-tuple-element.18.pos_ref) | copy-start | bytes 24580

commit v5 on v4

--- a/solution.py
+++ b/solution.py
@@ -217,73 +217,62 @@
         lhs[rows : 2 * rows, c * LANES : (c + 1) * LANES] = low
 
 
-def edge_kernel(
-    freqs, dirs, blocks, recv_ref, first_ref, second_ref, cell_ref, south_lhs, north_lhs, wide
-):
+def edge_kernel(freqs, dirs, blocks, recv_ref, first_ref, second_ref, cell_ref, lhs, fold_ref, out_ref):
     points = cell_ref.shape[1]
     label = freqs * dirs
     half = dirs // 2
-    rows = south_lhs.shape[0] // 2
+    rows = lhs.shape[0] // 4
     near_rows = freqs * (half + 1) + 1
+    edge = 2 * NLON
     fill = jnp.ones((rows - freqs * (half + 1), LANES), F32)
     for c in range(points // LANES):
         where = slice(c * LANES, (c + 1) * LANES)
         own = recv_ref[c, label : label + 1, :].astype(jnp.int32) - 1
         cell_ref[:, where] = own
-        wide[where, :] = jnp.broadcast_to(own, (LANES, LANES)).T.astype(jnp.int16)
+        upper = own >= points - edge
+        lower = (own >= 0) & (own < edge)
+        fold_ref[:, where] = jnp.where(upper, own - (points - edge), jnp.where(lower, own, -1))
         x = recv_ref[c]
-        for lhs, start, other in ((south_lhs, 0, half), (north_lhs, half, 0)):
+        for side, start, other, mine in ((0, 0, half, upper), (1, half, 0, lower)):
             pieces = []
             for f in range(freqs):
                 base = f * dirs
                 pieces.append(x[base + start : base + start + half])
                 pieces.append(x[base + other : base + other + 1])
-            high, low = split(jnp.concatenate(pieces + [fill], axis=0))
-            lhs[0:rows, where] = high
-            lhs[rows : 2 * rows, where] = low
-    ids = lax.broadcasted_iota(jnp.int32, (1, LANES), 1)
-
-    def side(out_ref, lhs, row, near):
-        for t in range(NLON // TILE):
-            start = row * NLON + t * TILE
-            table = jnp.concatenate(
-                [
-                    jnp.where(
-                        wide[...] == (ids + (start + h * LANES)).astype(jnp.int16),
-                        jnp.ones((), BF16),
-                        jnp.zeros((), BF16),
-                    )
-                    for h in range(TILE // LANES)
-                ],
-                axis=1,
-            )
-            both = jnp.dot(lhs[...], table, preferred_element_type=F32)
-            out = both[0:rows] + both[rows : 2 * rows]
-            where = slice(t * TILE, (t + 1) * TILE)
-            if near:
-                out_ref[0:near_rows, where] = out[0:near_rows]
-                continue
-            for f in range(freqs):
-                at = near_rows + f * (half - 1)
-                low = f * (half + 1) + 1
-                out_ref[at : at + half - 1, where] = out[low : low + half - 1]
-
-    top = points // NLON - 1
+            high, low = split(jnp.where(mine, jnp.concatenate(pieces + [fill], axis=0), 0.0))
+            lhs[side * rows : (side + 1) * rows, where] = high
+            lhs[(2 + side) * rows : (3 + side) * rows, where] = low
+    cells = fold_ref[...]
     even = lax.rem(snake(lax.axis_index("blk"), blocks), 2) == 0
 
-    def sides(up_ref, down_ref):
-        side(up_ref, south_lhs, top, True)
-        side(up_ref, south_lhs, top - 1, False)
-        side(down_ref, north_lhs, 0, True)
-        side(down_ref, north_lhs, 1, False)
+    def keep(edge_ref, out, t, near):
+        where = slice(t * TILE % NLON, t * TILE % NLON + TILE)
+        if near:
+            edge_ref[0:near_rows, where] = out[0:near_rows]
+            return
+        for f in range(freqs):
+            at = near_rows + f * (half - 1)
+            low = f * (half + 1) + 1
+            edge_ref[at : at + half - 1, where] = out[low : low + half - 1]
+
+    for t in range(edge // TILE):
+        both = matmul_nt(lhs[...], one_hot(cells, t * TILE, points))
+        out_ref[:, t * TILE : (t + 1) * TILE] = both[0 : 2 * rows] + both[2 * rows : 4 * rows]
+
+    def store(up_ref, down_ref):
+        for t in range(edge // TILE):
+            out = out_ref[:, t * TILE : (t + 1) * TILE]
+            second_row = t * TILE >= NLON
+            keep(up_ref, out[0:rows], t, second_row)
+            keep(down_ref, out[rows : 2 * rows], t, not second_row)
 
     @pl.when(even)
     def _():
-        sides(first_ref, second_ref)
+        store(first_ref, second_ref)
 
     @pl.when(jnp.logical_not(even))
     def _():
-        sides(second_ref, first_ref)
+        store(second_ref, first_ref)
 
 
 def lanes(row):
@@ -603,9 +592,9 @@
         in_specs=[vmem],
         out_specs=(vmem,) * 3,
         scratch_shapes=[
-            pltpu.VMEM((2 * edge_lhs, points), BF16),
-            pltpu.VMEM((2 * edge_lhs, points), BF16),
-            pltpu.VMEM((points, LANES), jnp.int16),
+            pltpu.VMEM((4 * edge_lhs, points), BF16),
+            pltpu.VMEM((1, points), jnp.int32),
+            pltpu.VMEM((2 * edge_lhs, 2 * NLON), F32),
         ],
         compiler_params=params,
         name="edges",

time: 80.1 us -> 78.8 us (0.984)
  Pallas kernels: 17.3 us -> 16.3 us
    pallas_call x1, Pallas kernels: 2.28 us -> 1.38 us  [per_device(): pl.pallas_call(functools.partial(edge_kernel, freqs, dirs, blocks), out_s...]
where the time goes in v5:
time: 78.8 us; the launch traced here: 78.5 us
  blocking collectives  56.8 us (72%)
  Pallas kernels  16.3 us (21%)
  starting transfers between devices  3.16 us (4%)
  waiting for transfers between devices  1.57 us (2%)
    all_to_all x2, blocking collectives, exchange(): return lax.all_to_all(x, 'blk', split_axis=0, concat_axis=0, tiled=True)  56.8 us
    pallas_call x1, Pallas kernels, per_device(): pl.pallas_call(functools.partial(source_kernel, blocks, cap), out_shape=(...  5.6 us
    pallas_call x1, Pallas kernels, per_device(): pl.pallas_call(functools.partial(step_kernel, freqs, dirs, blocks), out_s...  3.61 us
    ppermute x1, starting transfers between devices, per_device(): lax.ppermute(second, 'blk', outer)  3.09 us
    pallas_call x1, Pallas kernels, per_device(): pl.pallas_call(functools.partial(pick_kernel, freqs, dirs), out_shape=arr...  3.01 us
    pallas_call x1, Pallas kernels, per_device(): pl.pallas_call(functools.partial(place_kernel, freqs, dirs, blocks), out_...  2.65 us
  transfers between devices with their start and end apart: 2, of which 1 were waited for; matrix products, arithmetic and copies ran while one was open for 0% of the time, Pallas kernels for 3%

profile of v5, /device:TPU:1, one launch (start us, length us, event | category | flops | bytes accessed | tf_op | source)
XLA Modules:
  0.0 78.5 jit_solution(5674262298511070849)
XLA Ops:
  0.7 5.6 %source.1 = (f32[16,112,128]{2,1,0:T(8,128)}, s32[1,2048]{1,0:T(1,128)}) custom-call(s32[2]{0:T(128)} %shift_in.1, s32[1]{0:T(128)S(6)} %copy.6.count_in, f32[3,36,2048]{2,1,0:T(8,128)} %spec_in.1, f32[2,2048]{1,0:T(2,128)} %wind_in.1, s32[1,2048]{1,0:T(1,128)} %bitcast.1), custom_call_target="tpu_custom_call" | custom-call | tf_op jit(solution)/shard_map/source/pallas_call | solution.py:566
  6.3 30.3 %all_to_all.10.recv_ref = f32[16,112,128]{2,1,0:T(8,128)S(1)} all-to-all(f32[16,112,128]{2,1,0:T(8,128)} %get-tuple-element.12), channel_id=1, replica_groups=mesh['groups'=2,'blk'=16] {'blk'}, dimensions={0} | all-to-all | bytes 1835008 | tf_op jit(solution)/shard_map/all_to_all | solution.py:539
  36.5 1.4 %edges.1 = (f32[112,512]{1,0:T(8,128)S(1)}, f32[112,512]{1,0:T(8,128)S(1)}, s32[1,2048]{1,0:T(1,128)S(1)}) custom-call(f32[16,112,128]{2,1,0:T(8,128)S(1)} %all_to_all.10.recv_ref), custom_call_target="tpu_custom_call" | custom-call | tf_op jit(solution)/shard_map/edges/pallas_call | solution.py:585
  37.9 0.1 collective-permute-start
  38.0 3.1 %collective-permute-start.1 = (f32[112,512]{1,0:T(8,128)S(1)}, f32[112,512]{1,0:T(8,128)S(1)}, u32[]{:S(2)}, u32[]{:S(2)}) collective-permute-start(f32[112,512]{1,0:T(8,128)S(1)} %get-tuple-element.17), channel_id=1, source_target_pairs={{1,2},{2,1},{3,6},{6,3},{7,4},{4,7},{5,8},{8,5},{9,10},{10,9},{11,... | collective-permute-start | bytes 688136 | tf_op jit(solution)/shard_map/ppermute | solution.py:603
  41.1 2.7 %place.1 = (f32[120,2048]{1,0:T(8,128)S(1)}, f32[120,1024]{1,0:T(8,128)S(1)}) custom-call(f32[16,112,128]{2,1,0:T(8,128)S(1)} %all_to_all.10.recv_ref, s32[1,2048]{1,0:T(1,128)S(1)} %get-tuple-element.13.cell_ref), custom_call_target="tpu_custom_call" | custom-call | flops 2013265920 | bytes 1966080 | tf_op jit(solution)/shard_map/place/pallas_call | solution.py:604
  43.7 0.0 collective-permute-done.first_ref
  43.7 1.6 %collective-permute-done.1.second_ref = f32[112,512]{1,0:T(8,128)S(1)} collective-permute-done((f32[112,512]{1,0:T(8,128)S(1)}, f32[112,512]{1,0:T(8,128)S(1)}, u32[]{:S(2)}, u32[]{:S(2)}) %collective-permute-start.1) | collective-permute-done | bytes 229408 | tf_op jit(solution)/shard_map/ppermute | solution.py:603
  45.3 3.6 %step.1 = f32[16,27,4,128]{3,2,1,0:T(4,128)S(1)} custom-call(f32[120,2048]{1,0:T(8,128)S(1)} %get-tuple-element.14.field_ref, f32[120,1024]{1,0:T(8,128)S(1)} %get-tuple-element.15.inner_ref, f32[112,512]{1,0:T(8,128)S(1)} %collective-permute-done.first_ref, f32[112,512]{1,0:T(8,128)S(1)} %collective-permute-done.1.second_ref, ...), custom_call_target="tpu_custom_call" | custom-call | tf_op jit(solution)/shard_map/step/pallas_call | solution.py:616
  48.9 0.0 copy-start
  48.9 26.5 %all_to_all.11.recv_ref = f32[16,27,4,128]{3,2,1,0:T(4,128)S(1)} all-to-all(f32[16,27,4,128]{3,2,1,0:T(4,128)S(1)} %step.1), channel_id=1, replica_groups=mesh['groups'=2,'blk'=16] {'blk'}, dimensions={0} | all-to-all | bytes 1769472 | tf_op jit(solution)/shard_map/all_to_all | solution.py:539
  75.5 0.0 copy-done
  75.5 3.0 %pick.1 = f32[3,36,2048]{2,1,0:T(8,128)} custom-call(f32[16,27,4,128]{3,2,1,0:T(4,128)S(1)} %all_to_all.11.recv_ref, s32[1,2048]{1,0:T(1,128)S(1)} %copy-done), custom_call_target="tpu_custom_call" | custom-call | tf_op jit(solution)/shard_map/pick/pallas_call | solution.py:632
Async XLA Ops:
  37.9 5.8 %collective-permute-start = (f32[112,512]{1,0:T(8,128)S(1)}, f32[112,512]{1,0:T(8,128)S(1)}, u32[]{:S(2)}, u32[]{:S(2)}) collective-permute-start(f32[112,512]{1,0:T(8,128)S(1)} %get-tuple-element.16), channel_id=1, source_target_pairs={{0,1},{1,0},{2,3},{3,2},{6,7},{7,6},{4,5},{5,4},{8,9},{9,8},{10,11... | collective-permute-start | bytes 688136 | tf_op jit(solution)/shard_map/ppermute | solution.py:603
  38.0 7.3 %collective-permute-start.1 = (f32[112,512]{1,0:T(8,128)S(1)}, f32[112,512]{1,0:T(8,128)S(1)}, u32[]{:S(2)}, u32[]{:S(2)}) collective-permute-start(f32[112,512]{1,0:T(8,128)S(1)} %get-tuple-element.17), channel_id=1, source_target_pairs={{1,2},{2,1},{3,6},{6,3},{7,4},{4,7},{5,8},{8,5},{9,10},{10,9},{11,... | collective-permute-start | bytes 688136 | tf_op jit(solution)/shard_map/ppermute | solution.py:603
  48.9 26.5 %copy-start = (s32[1,2048]{1,0:T(1,128)S(1)}, s32[1,2048]{1,0:T(1,128)}, u32[]{:S(2)}) copy-start(s32[1,2048]{1,0:T(1,128)} %get-tuple-element.18.pos_ref) | copy-start | bytes 24580

commit v6 on v5

--- a/solution.py
+++ b/solution.py
@@ -343,11 +343,23 @@
         meridional = by_tile(low, high, norths, from_south, rows_of(row - 1), rows_of(row + 1))
         zonal = by_tile(low, high, cosines, from_west, turned_by(1), turned_by(-1))
         adv = (x - cy * (x - meridional) - cx * (x - zonal)) * sea
+        return turned(adv, ct, from_lower[part]) * sea
+
+    def turned(adv, ct, from_lower):
         lower = pltpu.roll(adv, 1, 0)
-        upper = pltpu.roll(adv, high - low - 1, 0)
-        return (adv - ct * (adv - jnp.where(from_lower[part], lower, upper))) * sea
-
-    return advance
+        upper = pltpu.roll(adv, adv.shape[0] - 1, 0)
+        return adv - ct * (adv - jnp.where(from_lower, lower, upper))
+
+    def answer(x, row, f, sea, low, high, valid):
+        part = slice(low, high)
+        _, ct, from_lower = latitude(row)
+        speed = 1.0 / (1.0 + 0.25 * f)
+        adv = jnp.where(valid[part], (speed * cy_base)[part, 0:1] * x, 0.0) * sea
+        return turned(adv, (speed * ct)[part], from_lower[part]) * sea
+
+    south_side = from_south
+    north_side = jnp.logical_not(from_south) & (at <= dirs)[:, 0:1]
+    return advance, answer, south_side, north_side
 
 
 def repeat_ends(out, dirs):
@@ -356,7 +368,24 @@
     )
 
 
-def place_kernel(freqs, dirs, blocks, recv_ref, cell_ref, field_ref, inner_ref, lhs):
+def blank(row, piece):
+    return jnp.zeros((piece.stop - piece.start, NLON), F32)
+
+
+def pick_rows(lhs, cells, first, count, where):
+    table = jnp.concatenate(
+        [
+            one_hot(cells[:, where], first * NLON + k * TILE, TILE)
+            for k in range(count * NLON // TILE)
+        ],
+        axis=0,
+    )
+    both = jnp.dot(lhs[...], table, preferred_element_type=F32)
+    half = lhs.shape[0] // 2
+    return both[0:half] + both[half : 2 * half]
+
+
+def place_kernel(freqs, dirs, blocks, recv_ref, cell_ref, field_ref, mid_ref, pre_ref, lhs, lhs2):
     points = cell_ref.shape[1]
     rows = freqs * STRIDE
     row_count = points // NLON
@@ -365,12 +394,30 @@
     for t in range(points // TILE):
         both = matmul_nt(lhs[...], one_hot(cells, t * TILE, points))
         field_ref[:, t * TILE : (t + 1) * TILE] = both[0:rows] + both[rows : 2 * rows]
-    advance = stepper(freqs, dirs, blocks, row_count)
+    advance = stepper(freqs, dirs, blocks, row_count)[0]
+
+    def sea_of(row):
+        return field_ref[dirs + 1 : dirs + 2, lanes(row)]
+
+    def before(row, piece):
+        if row < 0 or row >= row_count:
+            return blank(row, piece)
+        return field_ref[piece, lanes(row)]
+
+    for row in range(row_count):
+        for f in range(freqs):
+            out = advance(before, row, f, sea_of(row))
+            mid_ref[f * STRIDE : (f + 1) * STRIDE, lanes(row)] = repeat_ends(out, dirs)
     for row in range(1, row_count - 1):
-        sea = field_ref[dirs + 1 : dirs + 2, lanes(row)]
-        for f in range(freqs):
-            out = advance(lambda r, piece: field_ref[piece, lanes(r)], row, f, sea)
-            inner_ref[f * STRIDE : (f + 1) * STRIDE, lanes(row - 1)] = repeat_ends(out, dirs)
+        for f in range(freqs):
+            out = advance(lambda r, piece: mid_ref[piece, lanes(r)], row, f, sea_of(row))
+            high, low = split(out)
+            base = f * STRIDE
+            lhs2[base : base + STRIDE, lanes(row - 1)] = high
+            lhs2[rows + base : rows + base + STRIDE, lanes(row - 1)] = low
+    for t in range(points // TILE):
+        where = slice(t * TILE, (t + 1) * TILE)
+        pre_ref[:, where] = pick_rows(lhs2, cell_ref, 1, row_count - 2, where)
 
 
 def step_kernel(
@@ -378,7 +425,8 @@
     dirs,
     blocks,
     field_ref,
-    inner_ref,
+    mid_ref,
+    pre_ref,
     first_ref,
     second_ref,
     cell_ref,
@@ -386,8 +434,10 @@
     south,
     north,
     outer,
-    acc,
+    cross,
     lhs,
+    lhs_low,
+    lhs_high,
 ):
     points = field_ref.shape[1]
     rows = freqs * STRIDE
@@ -441,63 +491,118 @@
     def between(row, piece):
         if row in places:
             return outer[piece, lanes(places[row])]
-        return inner_ref[piece, lanes(row - 1)]
-
-    advance = stepper(freqs, dirs, blocks, row_count)
-    south_high = -(-(half + 1) // 8) * 8
-    north_low = half // 8 * 8
-
-    def first_step(row, f):
+        return mid_ref[piece, lanes(row)]
+
+    advance, answer, south_side, north_side = stepper(freqs, dirs, blocks, row_count)
+    high = -(-(half + 1) // 8) * 8
+    low = half // 8 * 8
+    wide = STRIDE - low
+
+    def first_step(f):
         base = f * STRIDE
-        where = lanes(places[row])
-        if row < 0:
-            out = advance(before, row, f, sea_of(row), 0, south_high)
-            outer[base : base + south_high, where] = out
-        elif row > top:
-            out = advance(before, row, f, sea_of(row), north_low, STRIDE)
-            outer[base + north_low : base + STRIDE, where] = out
-            spot = dirs - 1 - north_low
-            outer[base + STRIDE - 1 : base + STRIDE, where] = out[spot : spot + 1]
-        else:
-            out = advance(before, row, f, sea_of(row))
-            outer[base : base + STRIDE, where] = repeat_ends(out, dirs)
-
-    def second_step(row, f):
-        high, low = split(advance(between, row, f, sea_of(row)))
-        lhs[f * STRIDE : (f + 1) * STRIDE, lanes(row)] = high
-        lhs[rows + f * STRIDE : rows + (f + 1) * STRIDE, lanes(row)] = low
-
-    def pick(t, row):
+        out = advance(before, -1, f, sea_of(-1), 0, high)
+        outer[base : base + high, lanes(places[-1])] = out
+        out = advance(before, top + 1, f, sea_of(top + 1), low, STRIDE)
+        outer[base + low : base + STRIDE, lanes(places[top + 1])] = out
+        spot = dirs - 1 - low
+        outer[base + STRIDE - 1 : base + STRIDE, lanes(places[top + 1])] = out[spot : spot + 1]
+        more = answer(
+            south[base : base + high, lanes(0)], 0, f, sea_of(0), 0, high, south_side
+        )
+        cross[f * high : (f + 1) * high, :] = more
+        old = mid_ref[base : base + STRIDE, lanes(0)]
+        outer[base : base + STRIDE, lanes(places[0])] = jnp.concatenate(
+            [
+                old[0:high] + more,
+                old[high:dirs],
+                old[dirs : dirs + 1] + more[0:1],
+                old[dirs + 1 : STRIDE],
+            ],
+            axis=0,
+        )
+        more = answer(
+            north[base + low : base + STRIDE, lanes(0)], top, f, sea_of(top), low, STRIDE, north_side
+        )
+        at = freqs * high + f * wide
+        cross[at : at + wide, :] = more
+        old = mid_ref[base : base + STRIDE, lanes(top)]
+        zero, last = more[dirs - low : dirs - low + 1], more[dirs - 1 - low : dirs - low]
+        outer[base : base + STRIDE, lanes(places[top])] = jnp.concatenate(
+            [
+                old[0:1] + zero,
+                old[1:low],
+                old[low:dirs] + more[0 : dirs - low],
+                old[dirs : dirs + 1] + zero,
+                old[dirs + 1 : STRIDE - 1],
+                old[STRIDE - 1 : STRIDE] + last,
+            ],
+            axis=0,
+        )
+
+    def second_step(f):
+        base = f * STRIDE
+        for row, out_lhs in ((0, lhs_low), (top, lhs_high)):
+            upper, lower = split(advance(between, row, f, sea_of(row)))
+            out_lhs[base : base + STRIDE, :] = upper
+            out_lhs[rows + base : rows + base + STRIDE, :] = lower
+        total = freqs * (high + wide)
+        at = f * high
+        upper, lower = split(
+            answer(cross[at : at + high, :], 1, f, sea_of(1), 0, high, south_side)
+        )
+        lhs[at : at + high, :] = upper
+        lhs[total + at : total + at + high, :] = lower
+        at = freqs * high + f * wide
+        upper, lower = split(
+            answer(cross[at : at + wide, :], top - 1, f, sea_of(top - 1), low, STRIDE, north_side)
+        )
+        lhs[at : at + wide, :] = upper
+        lhs[total + at : total + at + wide, :] = lower
+
+    def pick(t):
         where = slice(t * TILE, (t + 1) * TILE)
         cells = cell_ref[:, where]
+        out = pre_ref[:, where]
+        out = out + pick_rows(lhs_low, cell_ref, 0, 1, where)
+        out = out + pick_rows(lhs_high, cell_ref, top, 1, where)
+        row = lax.shift_right_arithmetic(cells, NLON.bit_length() - 1)
+        inside = jnp.where(
+            row == 1, cells - NLON, jnp.where(row == top - 1, cells - (top - 1) * NLON, -1)
+        )
         table = jnp.concatenate(
-            [one_hot(cells, row * NLON + k * TILE, TILE) for k in range(NLON // TILE)], axis=0
-        )
-        both = jnp.dot(lhs[:, lanes(row)], table, preferred_element_type=F32)
-        out = both[0:rows] + both[rows : 2 * rows]
-        if row:
-            out = acc[:, where] + out
-        if row < top:
-            acc[:, where] = out
-            return
-        for h in range(TILE // LANES):
-            for q in range(freqs * dirs // 4):
-                low = q // (dirs // 4) * STRIDE + q % (dirs // 4) * 4
-                back_ref[t * (TILE // LANES) + h, q] = out[
-                    low : low + 4, h * LANES : (h + 1) * LANES
-                ]
-
-    steps = points // TILE
-    for row in places:
-        for f in range(freqs):
-            first_step(row, f)
-    for row in range(row_count + 1):
-        for f in range(freqs):
-            if row < row_count:
-                second_step(row, f)
-            if row:
-                for t in range(f * steps // freqs, (f + 1) * steps // freqs):
-                    pick(t, row - 1)
+            [one_hot(inside, k * TILE, TILE) for k in range(NLON // TILE)], axis=0
+        )
+        both = jnp.dot(lhs[...], table, preferred_element_type=F32)
+        total = freqs * (high + wide)
+        both = both[0:total] + both[total : 2 * total]
+        from_below = jnp.where(row == 1, both[0 : freqs * high], 0.0)
+        from_above = jnp.where(row == top - 1, both[freqs * high : total], 0.0)
+        for f in range(freqs):
+            base = f * STRIDE
+            below = from_below[f * high : (f + 1) * high]
+            above = from_above[f * wide : (f + 1) * wide]
+            sums = jnp.concatenate(
+                [
+                    out[base : base + low] + below[0:low],
+                    out[base + low : base + high] + below[low:high] + above[0 : high - low],
+                    out[base + high : base + STRIDE] + above[high - low : wide],
+                ],
+                axis=0,
+            )
+            first = sums[0:1] + above[dirs - low : dirs - low + 1]
+            sums = jnp.concatenate([first, sums[1:dirs]], axis=0)
+            for h in range(TILE // LANES):
+                for q in range(dirs // 4):
+                    back_ref[t * (TILE // LANES) + h, f * (dirs // 4) + q] = sums[
+                        4 * q : 4 * q + 4, h * LANES : (h + 1) * LANES
+                    ]
+
+    for f in range(freqs):
+        first_step(f)
+    for f in range(freqs):
+        second_step(f)
+    for t in range(points // TILE):
+        pick(t)
 
 
 def pick_kernel(freqs, dirs, recv_ref, pos_ref, out_ref, result, lhs, sems):
@@ -601,33 +706,40 @@
     )(arrived)
     inner, outer = halo_swaps(blocks)
     mine, theirs = lax.ppermute(first, "blk", inner), lax.ppermute(second, "blk", outer)
-    field, middle = pl.pallas_call(
+    field, middle, inner_part = pl.pallas_call(
         functools.partial(place_kernel, freqs, dirs, blocks),
-        out_shape=(arr((rows, points)), arr((rows, points - 2 * NLON))),
+        out_shape=(arr((rows, points)),) * 3,
         in_specs=[vmem] * 2,
-        out_specs=(vmem,) * 2,
-        scratch_shapes=[pltpu.VMEM((2 * rows, points), BF16)],
+        out_specs=(vmem,) * 3,
+        scratch_shapes=[
+            pltpu.VMEM((2 * rows, points), BF16),
+            pltpu.VMEM((2 * rows, points - 2 * NLON), BF16),
+        ],
         compiler_params=params,
         cost_estimate=pl.CostEstimate(
-            flops=4 * rows * points * points, bytes_accessed=8 * rows * points, transcendentals=0
+            flops=6 * rows * points * points, bytes_accessed=8 * rows * points, transcendentals=0
         ),
         name="place",
     )(arrived, cells)
+    half = dirs // 2
+    cross_rows = freqs * (-(-(half + 1) // 8) * 8 + STRIDE - half // 8 * 8)
     back = pl.pallas_call(
         functools.partial(step_kernel, freqs, dirs, blocks),
         out_shape=arr((pieces, freqs * dirs // 4, 4, LANES)),
-        in_specs=[vmem] * 5,
+        in_specs=[vmem] * 6,
         out_specs=vmem,
         scratch_shapes=[
             pltpu.VMEM((rows + 8, 2 * NLON), F32),
             pltpu.VMEM((rows + 8, 2 * NLON), F32),
             pltpu.VMEM((rows, 4 * NLON), F32),
-            pltpu.VMEM((rows, points), F32),
-            pltpu.VMEM((2 * rows, points), BF16),
+            pltpu.VMEM((cross_rows, NLON), F32),
+            pltpu.VMEM((2 * cross_rows, NLON), BF16),
+            pltpu.VMEM((2 * rows, NLON), BF16),
+            pltpu.VMEM((2 * rows, NLON), BF16),
         ],
         compiler_params=params,
         name="step",
-    )(field, middle, mine, theirs, cells)
+    )(field, middle, inner_part, mine, theirs, cells)
     returned = exchange(back, blocks, cap)
     return pl.pallas_call(
         functools.partial(pick_kernel, freqs, dirs),

time: 78.8 us -> 78.1 us (level)
  waiting for transfers between devices: 1.57 us -> 0.01 us
  Pallas kernels: 16.3 us -> 17.3 us
    pallas_call x1, Pallas kernels: 2.65 us -> 4.38 us  [per_device(): pl.pallas_call(functools.partial(place_kernel, freqs, dirs, blocks), out_...]
    ppermute x1, waiting for transfers between devices: 1.57 us -> 0.01 us  [per_device(): lax.ppermute(second, 'blk', outer)]
  transfers between devices with their start and end apart: 2 -> 2, of which waited for: 1 -> 0; matrix products, arithmetic and copies ran while one was open for 0% -> 0% of each run, Pallas kernels for 3% -> 6%
where the time goes in v6:
time: 78.1 us; the launch traced here: 77.8 us
  blocking collectives  56.6 us (72%)
  Pallas kernels  17.3 us (22%)
  starting transfers between devices  3.16 us (4%)
    all_to_all x2, blocking collectives, exchange(): return lax.all_to_all(x, 'blk', split_axis=0, concat_axis=0, tiled=True)  56.6 us
    pallas_call x1, Pallas kernels, per_device(): pl.pallas_call(functools.partial(source_kernel, blocks, cap), out_shape=(...  5.6 us
    pallas_call x1, Pallas kernels, per_device(): pl.pallas_call(functools.partial(place_kernel, freqs, dirs, blocks), out_...  4.38 us
    ppermute x1, starting transfers between devices, per_device(): lax.ppermute(second, 'blk', outer)  3.09 us
    pallas_call x1, Pallas kernels, per_device(): pl.pallas_call(functools.partial(pick_kernel, freqs, dirs), out_shape=arr...  3.01 us
    pallas_call x1, Pallas kernels, per_device(): pl.pallas_call(functools.partial(step_kernel, freqs, dirs, blocks), out_s...  2.96 us
  transfers between devices with their start and end apart: 2, of which 0 were waited for; matrix products, arithmetic and copies ran while one was open for 0% of the time, Pallas kernels for 6%

profile of v6, /device:TPU:1, one launch (start us, length us, event | category | flops | bytes accessed | tf_op | source)
XLA Modules:
  0.0 77.8 jit_solution(14986130080419599503)
XLA Ops:
  0.7 5.6 %source.1 = (f32[16,112,128]{2,1,0:T(8,128)}, s32[1,2048]{1,0:T(1,128)}) custom-call(s32[2]{0:T(128)} %shift_in.1, s32[1]{0:T(128)S(6)} %copy.6.count_in, f32[3,36,2048]{2,1,0:T(8,128)} %spec_in.1, f32[2,2048]{1,0:T(2,128)} %wind_in.1, s32[1,2048]{1,0:T(1,128)} %bitcast.1), custom_call_target="tpu_custom_call" | custom-call | tf_op jit(solution)/shard_map/source/pallas_call | solution.py:671
  6.3 30.3 %all_to_all.10.recv_ref = f32[16,112,128]{2,1,0:T(8,128)S(1)} all-to-all(f32[16,112,128]{2,1,0:T(8,128)} %get-tuple-element.13), channel_id=1, replica_groups=mesh['groups'=2,'blk'=16] {'blk'}, dimensions={0} | all-to-all | bytes 1835008 | tf_op jit(solution)/shard_map/all_to_all | solution.py:644
  36.5 1.4 %edges.1 = (f32[112,512]{1,0:T(8,128)S(1)}, f32[112,512]{1,0:T(8,128)S(1)}, s32[1,2048]{1,0:T(1,128)S(1)}) custom-call(f32[16,112,128]{2,1,0:T(8,128)S(1)} %all_to_all.10.recv_ref), custom_call_target="tpu_custom_call" | custom-call | tf_op jit(solution)/shard_map/edges/pallas_call | solution.py:690
  37.9 0.1 collective-permute-start
  38.0 3.1 %collective-permute-start.1 = (f32[112,512]{1,0:T(8,128)S(1)}, f32[112,512]{1,0:T(8,128)S(1)}, u32[]{:S(2)}, u32[]{:S(2)}) collective-permute-start(f32[112,512]{1,0:T(8,128)S(1)} %get-tuple-element.19), channel_id=1, source_target_pairs={{1,2},{2,1},{3,6},{6,3},{7,4},{4,7},{5,8},{8,5},{9,10},{10,9},{11,... | collective-permute-start | bytes 688136 | tf_op jit(solution)/shard_map/ppermute | solution.py:708
  41.1 4.4 %place.1 = (f32[120,2048]{1,0:T(8,128)S(1)}, f32[120,2048]{1,0:T(8,128)S(1)}, f32[120,2048]{1,0:T(8,128)S(1)}) custom-call(f32[16,112,128]{2,1,0:T(8,128)S(1)} %all_to_all.10.recv_ref, s32[1,2048]{1,0:T(1,128)S(1)} %get-tuple-element.14.cell_ref), custom_call_target="tpu_custom_call" | custom-call | flops 3019898880 | bytes 1966080 | tf_op jit(solution)/shard_map/place/pallas_call | solution.py:709
  45.5 0.0 collective-permute-done.first_ref
  45.5 0.0 collective-permute-done.1.second_ref
  45.5 3.0 %step.1 = f32[16,27,4,128]{3,2,1,0:T(4,128)S(1)} custom-call(f32[120,2048]{1,0:T(8,128)S(1)} %get-tuple-element.15.field_ref, f32[120,2048]{1,0:T(8,128)S(1)} %get-tuple-element.16.mid_ref, f32[120,2048]{1,0:T(8,128)S(1)} %get-tuple-element.17.pre_ref, f32[112,512]{1,0:T(8,128)S(1)} %collective-permute-done.first_ref, ...), custom_call_target="tpu_custom_call" | custom-call | tf_op jit(solution)/shard_map/step/pallas_call | solution.py:726
  48.5 0.0 copy-start
  48.5 26.3 %all_to_all.11.recv_ref = f32[16,27,4,128]{3,2,1,0:T(4,128)S(1)} all-to-all(f32[16,27,4,128]{3,2,1,0:T(4,128)S(1)} %step.1), channel_id=1, replica_groups=mesh['groups'=2,'blk'=16] {'blk'}, dimensions={0} | all-to-all | bytes 1769472 | tf_op jit(solution)/shard_map/all_to_all | solution.py:644
  74.8 0.0 copy-done
  74.8 3.0 %pick.1 = f32[3,36,2048]{2,1,0:T(8,128)} custom-call(f32[16,27,4,128]{3,2,1,0:T(4,128)S(1)} %all_to_all.11.recv_ref, s32[1,2048]{1,0:T(1,128)S(1)} %copy-done), custom_call_target="tpu_custom_call" | custom-call | tf_op jit(solution)/shard_map/pick/pallas_call | solution.py:744
Async XLA Ops:
  37.9 7.6 %collective-permute-start = (f32[112,512]{1,0:T(8,128)S(1)}, f32[112,512]{1,0:T(8,128)S(1)}, u32[]{:S(2)}, u32[]{:S(2)}) collective-permute-start(f32[112,512]{1,0:T(8,128)S(1)} %get-tuple-element.18), channel_id=1, source_target_pairs={{0,1},{1,0},{2,3},{3,2},{6,7},{7,6},{4,5},{5,4},{8,9},{9,8},{10,11... | collective-permute-start | bytes 688136 | tf_op jit(solution)/shard_map/ppermute | solution.py:708
  38.0 7.5 %collective-permute-start.1 = (f32[112,512]{1,0:T(8,128)S(1)}, f32[112,512]{1,0:T(8,128)S(1)}, u32[]{:S(2)}, u32[]{:S(2)}) collective-permute-start(f32[112,512]{1,0:T(8,128)S(1)} %get-tuple-element.19), channel_id=1, source_target_pairs={{1,2},{2,1},{3,6},{6,3},{7,4},{4,7},{5,8},{8,5},{9,10},{10,9},{11,... | collective-permute-start | bytes 688136 | tf_op jit(solution)/shard_map/ppermute | solution.py:708
  48.5 26.4 %copy-start = (s32[1,2048]{1,0:T(1,128)S(1)}, s32[1,2048]{1,0:T(1,128)}, u32[]{:S(2)}) copy-start(s32[1,2048]{1,0:T(1,128)} %get-tuple-element.20.pos_ref) | copy-start | bytes 24580

commit v7 on v6

--- a/solution.py
+++ b/solution.py
@@ -111,6 +111,7 @@
     dest_ref,
     dbl,
     lhs,
+    acc,
     sems,
 ):
     freqs, dirs, points = spec_ref.shape
@@ -180,6 +181,7 @@
         lhs[rows : 2 * rows, where] = low
 
     per_step = TILE // LANES
+    send_rows = freqs * dirs + 1
 
     def place(t, g):
         where = slice(g * GROUP, (g + 1) * GROUP)
@@ -187,9 +189,13 @@
         out = both[0:rows] + both[rows : 2 * rows]
         for h in range(per_step):
             piece = out[:, h * LANES : (h + 1) * LANES]
+            k = t * per_step + h
             if g:
-                piece = send_ref[t * per_step + h] + piece
-            send_ref[t * per_step + h] = piece
+                piece = acc[k] + piece
+            if g < groups - 1:
+                acc[k] = piece
+            else:
+                send_ref[k * send_rows : (k + 1) * send_rows, :] = piece[0:send_rows]
 
     groups = points // GROUP
     chunks = GROUP // LANES
@@ -227,12 +233,12 @@
     fill = jnp.ones((rows - freqs * (half + 1), LANES), F32)
     for c in range(points // LANES):
         where = slice(c * LANES, (c + 1) * LANES)
-        own = recv_ref[c, label : label + 1, :].astype(jnp.int32) - 1
+        x = recv_ref[c * (label + 1) : (c + 1) * (label + 1), :]
+        own = x[label : label + 1].astype(jnp.int32) - 1
         cell_ref[:, where] = own
         upper = own >= points - edge
         lower = (own >= 0) & (own < edge)
         fold_ref[:, where] = jnp.where(upper, own - (points - edge), jnp.where(lower, own, -1))
-        x = recv_ref[c]
         for side, start, other, mine in ((0, 0, half, upper), (1, half, 0, lower)):
             pieces = []
             for f in range(freqs):
@@ -389,7 +395,10 @@
     points = cell_ref.shape[1]
     rows = freqs * STRIDE
     row_count = points // NLON
-    spread_rows(lambda c: recv_ref[c], freqs, dirs, points, lhs)
+    count = freqs * dirs
+    spread_rows(
+        lambda c: recv_ref[c * (count + 1) : c * (count + 1) + count, :], freqs, dirs, points, lhs
+    )
     cells = cell_ref[...]
     for t in range(points // TILE):
         both = matmul_nt(lhs[...], one_hot(cells, t * TILE, points))
@@ -592,10 +601,8 @@
             first = sums[0:1] + above[dirs - low : dirs - low + 1]
             sums = jnp.concatenate([first, sums[1:dirs]], axis=0)
             for h in range(TILE // LANES):
-                for q in range(dirs // 4):
-                    back_ref[t * (TILE // LANES) + h, f * (dirs // 4) + q] = sums[
-                        4 * q : 4 * q + 4, h * LANES : (h + 1) * LANES
-                    ]
+                at = ((t * (TILE // LANES) + h) * freqs + f) * dirs
+                back_ref[at : at + dirs, :] = sums[:, h * LANES : (h + 1) * LANES]
 
     for f in range(freqs):
         first_step(f)
@@ -608,12 +615,9 @@
 def pick_kernel(freqs, dirs, recv_ref, pos_ref, out_ref, result, lhs, sems):
     points = pos_ref.shape[1]
     rows = freqs * STRIDE
+    count = freqs * dirs
     spread_rows(
-        lambda c: jnp.concatenate([recv_ref[c, q] for q in range(freqs * dirs // 4)], axis=0),
-        freqs,
-        dirs,
-        points,
-        lhs,
+        lambda c: recv_ref[c * count : (c + 1) * count, :], freqs, dirs, points, lhs
     )
     parts = []
 
@@ -640,14 +644,15 @@
 
 
 def exchange(x, blocks, cap):
+    pieces = blocks * cap // LANES
+    rows = x.shape[0] // pieces
     if cap == LANES:
-        return lax.all_to_all(x, "blk", split_axis=0, concat_axis=0, tiled=True)
-    pieces, lanes = x.shape[0], x.shape[-1]
-    inner = x.shape[1:-1]
-    x = jnp.moveaxis(x, 0, -2).reshape(*inner, blocks, cap)
-    dim = len(inner)
-    x = lax.all_to_all(x, "blk", split_axis=dim, concat_axis=dim, tiled=True)
-    return jnp.moveaxis(x.reshape(*inner, pieces, lanes), -2, 0)
+        parts = x.reshape(blocks, rows, 1, LANES)
+        parts = lax.all_to_all(parts, "blk", split_axis=0, concat_axis=0, tiled=True)
+        return parts.reshape(x.shape)
+    parts = jnp.moveaxis(x.reshape(pieces, rows, LANES), 1, 0).reshape(rows, blocks, cap)
+    parts = lax.all_to_all(parts, "blk", split_axis=1, concat_axis=1, tiled=True)
+    return jnp.moveaxis(parts.reshape(rows, pieces, LANES), 0, 1).reshape(x.shape)
 
 
 def per_device(spectrum, wind_vector, dest_cell, counts, sea_mask, dia_shift):
@@ -656,7 +661,7 @@
     cap = points // blocks
     pieces = points // LANES
     rows = freqs * STRIDE
-    send_rows = -(-(freqs * dirs + 1) // 8) * 8
+    lhs_rows = -(-(freqs * dirs + 1) // 8) * 8
     near_rows = freqs * (dirs // 2 + 1) + 1
     far_rows = freqs * (dirs // 2 - 1)
     edge_rows = -(-(near_rows + far_rows) // 8) * 8
@@ -670,7 +675,7 @@
 
     send, position = pl.pallas_call(
         functools.partial(source_kernel, blocks, cap),
-        out_shape=(arr((pieces, send_rows, LANES)), arr((1, points), jnp.int32)),
+        out_shape=(arr((pieces * (freqs * dirs + 1), LANES)), arr((1, points), jnp.int32)),
         in_specs=[hbm] * 5,
         out_specs=(vmem, vmem),
         scratch_shapes=[
@@ -680,7 +685,8 @@
             pltpu.VMEM(wind_vector.shape, F32),
             pltpu.VMEM((1, points), jnp.int32),
             pltpu.VMEM((freqs, 2 * dirs, points), F32),
-            pltpu.VMEM((2 * send_rows, points), BF16),
+            pltpu.VMEM((2 * lhs_rows, points), BF16),
+            pltpu.VMEM((pieces, lhs_rows, LANES), F32),
             pltpu.SemaphoreType.DMA((5,)),
         ],
         compiler_params=pltpu.CompilerParams(vmem_limit_bytes=SOURCE_LIMIT),
@@ -725,7 +731,7 @@
     cross_rows = freqs * (-(-(half + 1) // 8) * 8 + STRIDE - half // 8 * 8)
     back = pl.pallas_call(
         functools.partial(step_kernel, freqs, dirs, blocks),
-        out_shape=arr((pieces, freqs * dirs // 4, 4, LANES)),
+        out_shape=arr((pieces * freqs * dirs, LANES)),
         in_specs=[vmem] * 6,
         out_specs=vmem,
         scratch_shapes=[

time: 78.1 us -> 77.5 us (level)
  no operation moved by 1% of the time
where the time goes in v7:
time: 77.5 us; the launch traced here: 77.2 us
  blocking collectives  56.2 us (73%)
  Pallas kernels  17.2 us (22%)
  starting transfers between devices  3.12 us (4%)
    all_to_all x2, blocking collectives, exchange(): lax.all_to_all(parts, 'blk', split_axis=0, concat_axis=0, tiled=True)  56.2 us
    pallas_call x1, Pallas kernels, per_device(): pl.pallas_call(functools.partial(source_kernel, blocks, cap), out_shape=(...  5.58 us
    pallas_call x1, Pallas kernels, per_device(): pl.pallas_call(functools.partial(place_kernel, freqs, dirs, blocks), out_...  4.34 us
    ppermute x1, starting transfers between devices, per_device(): lax.ppermute(second, 'blk', outer)  3.05 us
    pallas_call x1, Pallas kernels, per_device(): pl.pallas_call(functools.partial(pick_kernel, freqs, dirs), out_shape=arr...  2.98 us
    pallas_call x1, Pallas kernels, per_device(): pl.pallas_call(functools.partial(step_kernel, freqs, dirs, blocks), out_s...  2.93 us
  transfers between devices with their start and end apart: 2, of which 0 were waited for; matrix products, arithmetic and copies ran while one was open for 0% of the time, Pallas kernels for 6%

profile of v7, /device:TPU:1, one launch (start us, length us, event | category | flops | bytes accessed | tf_op | source)
XLA Modules:
  0.0 77.2 jit_solution(7222125416262857878)
XLA Ops:
  0.7 5.6 %source.1 = (f32[1744,128]{1,0:T(8,128)}, s32[1,2048]{1,0:T(1,128)}) custom-call(s32[2]{0:T(128)} %shift_in.1, s32[1]{0:T(128)S(6)} %copy.8.count_in, f32[3,36,2048]{2,1,0:T(8,128)} %spec_in.1, f32[2,2048]{1,0:T(2,128)} %wind_in.1, s32[1,2048]{1,0:T(1,128)} %bitcast.10), custom_call_target="tpu_custom_call" | custom-call | tf_op jit(solution)/shard_map/source/pallas_call | solution.py:676
  6.2 29.8 %all_to_all.10 = f32[16,109,1,128]{3,2,1,0:T(1,128)S(1)} all-to-all(f32[16,109,1,128]{3,2,1,0:T(1,128)} %bitcast.9), channel_id=1, replica_groups=mesh['groups'=2,'blk'=16] {'blk'}, dimensions={0} | all-to-all | bytes 1785856 | tf_op jit(solution)/shard_map/all_to_all | solution.py:651
  36.1 1.4 %edges.1 = (f32[112,512]{1,0:T(8,128)S(1)}, f32[112,512]{1,0:T(8,128)S(1)}, s32[1,2048]{1,0:T(1,128)S(1)}) custom-call(f32[1744,128]{1,0:T(8,128)S(1)} %bitcast.5), custom_call_target="tpu_custom_call" | custom-call | tf_op jit(solution)/shard_map/edges/pallas_call | solution.py:696
  37.5 0.1 collective-permute-start
  37.5 3.1 %collective-permute-start.1 = (f32[112,512]{1,0:T(8,128)S(1)}, f32[112,512]{1,0:T(8,128)S(1)}, u32[]{:S(2)}, u32[]{:S(2)}) collective-permute-start(f32[112,512]{1,0:T(8,128)S(1)} %get-tuple-element.19), channel_id=1, source_target_pairs={{1,2},{2,1},{3,6},{6,3},{7,4},{4,7},{5,8},{8,5},{9,10},{10,9},{11,... | collective-permute-start | bytes 688136 | tf_op jit(solution)/shard_map/ppermute | solution.py:714
  40.6 4.3 %place.1 = (f32[120,2048]{1,0:T(8,128)S(1)}, f32[120,2048]{1,0:T(8,128)S(1)}, f32[120,2048]{1,0:T(8,128)S(1)}) custom-call(f32[1744,128]{1,0:T(8,128)S(1)} %bitcast.6, s32[1,2048]{1,0:T(1,128)S(1)} %get-tuple-element.14.cell_ref), custom_call_target="tpu_custom_call" | custom-call | flops 3019898880 | bytes 1966080 | tf_op jit(solution)/shard_map/place/pallas_call | solution.py:715
  44.9 0.0 collective-permute-done.first_ref
  45.0 0.0 collective-permute-done.1.second_ref
  45.0 2.9 %step.1 = f32[1728,128]{1,0:T(8,128)S(1)} custom-call(f32[120,2048]{1,0:T(8,128)S(1)} %get-tuple-element.15.field_ref, f32[120,2048]{1,0:T(8,128)S(1)} %get-tuple-element.16.mid_ref, f32[120,2048]{1,0:T(8,128)S(1)} %get-tuple-element.17.pre_ref, f32[112,512]{1,0:T(8,128)S(1)} %collective-permute-done.first_ref, ...), custom_call_target="tpu_custom_call" | custom-call | tf_op jit(solution)/shard_map/step/pallas_call | solution.py:732
  47.9 0.0 copy-start
  47.9 26.3 %all_to_all.11 = f32[16,108,1,128]{3,2,1,0:T(1,128)S(1)} all-to-all(f32[16,108,1,128]{3,2,1,0:T(1,128)S(1)} %bitcast.8), channel_id=1, replica_groups=mesh['groups'=2,'blk'=16] {'blk'}, dimensions={0} | all-to-all | bytes 1769472 | tf_op jit(solution)/shard_map/all_to_all | solution.py:651
  74.2 0.0 copy-done
  74.2 3.0 %pick.1 = f32[3,36,2048]{2,1,0:T(8,128)} custom-call(f32[1728,128]{1,0:T(8,128)S(1)} %bitcast.7, s32[1,2048]{1,0:T(1,128)S(1)} %copy-done), custom_call_target="tpu_custom_call" | custom-call | tf_op jit(solution)/shard_map/pick/pallas_call | solution.py:750
Async XLA Ops:
  37.5 7.5 %collective-permute-start = (f32[112,512]{1,0:T(8,128)S(1)}, f32[112,512]{1,0:T(8,128)S(1)}, u32[]{:S(2)}, u32[]{:S(2)}) collective-permute-start(f32[112,512]{1,0:T(8,128)S(1)} %get-tuple-element.18), channel_id=1, source_target_pairs={{0,1},{1,0},{2,3},{3,2},{6,7},{7,6},{4,5},{5,4},{8,9},{9,8},{10,11... | collective-permute-start | bytes 688136 | tf_op jit(solution)/shard_map/ppermute | solution.py:714
  37.5 7.4 %collective-permute-start.1 = (f32[112,512]{1,0:T(8,128)S(1)}, f32[112,512]{1,0:T(8,128)S(1)}, u32[]{:S(2)}, u32[]{:S(2)}) collective-permute-start(f32[112,512]{1,0:T(8,128)S(1)} %get-tuple-element.19), channel_id=1, source_target_pairs={{1,2},{2,1},{3,6},{6,3},{7,4},{4,7},{5,8},{8,5},{9,10},{10,9},{11,... | collective-permute-start | bytes 688136 | tf_op jit(solution)/shard_map/ppermute | solution.py:714
  47.9 26.3 %copy-start = (s32[1,2048]{1,0:T(1,128)S(1)}, s32[1,2048]{1,0:T(1,128)}, u32[]{:S(2)}) copy-start(s32[1,2048]{1,0:T(1,128)} %get-tuple-element.20.pos_ref) | copy-start | bytes 24580

commit v8 on v7

--- a/solution.py
+++ b/solution.py
@@ -457,7 +457,7 @@
     top = row_count - 1
 
     def fill(ghost, in_ref, start):
-        ghost[0:rows, lanes(1)] = jnp.zeros((rows, NLON), F32)
+        ghost[...] = jnp.zeros(ghost.shape, F32)
         for f in range(freqs):
             base = f * STRIDE + start
             at = f * (half + 1)
@@ -614,11 +614,14 @@
 
 def pick_kernel(freqs, dirs, recv_ref, pos_ref, out_ref, result, lhs, sems):
     points = pos_ref.shape[1]
-    rows = freqs * STRIDE
+    rows = lhs.shape[0] // 2
     count = freqs * dirs
-    spread_rows(
-        lambda c: recv_ref[c * count : (c + 1) * count, :], freqs, dirs, points, lhs
-    )
+    fill = jnp.zeros((rows - count, LANES), F32)
+    for c in range(points // LANES):
+        x = jnp.concatenate([recv_ref[c * count : (c + 1) * count, :], fill], axis=0)
+        high, low = split(x)
+        lhs[0:rows, c * LANES : (c + 1) * LANES] = high
+        lhs[rows : 2 * rows, c * LANES : (c + 1) * LANES] = low
     parts = []
 
     def body(t):
@@ -630,7 +633,7 @@
         both = jnp.dot(lhs[...], table, preferred_element_type=F32)
         out = both[0:rows] + both[rows : 2 * rows]
         for f in range(freqs):
-            result[f, :, where] = out[f * STRIDE : f * STRIDE + dirs]
+            result[f, :, where] = out[f * dirs : (f + 1) * dirs]
         part = pltpu.make_async_copy(
             result.at[:, :, where], out_ref.at[:, :, where], sems.at[t]
         )
@@ -754,7 +757,7 @@
         out_specs=hbm,
         scratch_shapes=[
             pltpu.VMEM((freqs, dirs, points), F32),
-            pltpu.VMEM((2 * rows, points), BF16),
+            pltpu.VMEM((2 * lhs_rows, points), BF16),
             pltpu.SemaphoreType.DMA((points // TILE,)),
         ],
         compiler_params=params,

time: 77.5 us -> 77.4 us (level)
  no operation moved by 1% of the time
where the time goes in v8:
time: 77.4 us; the launch traced here: 77.1 us
  blocking collectives  56.2 us (73%)
  Pallas kernels  17.1 us (22%)
  starting transfers between devices  3.12 us (4%)
    all_to_all x2, blocking collectives, exchange(): lax.all_to_all(parts, 'blk', split_axis=0, concat_axis=0, tiled=True)  56.2 us
    pallas_call x1, Pallas kernels, per_device(): pl.pallas_call(functools.partial(source_kernel, blocks, cap), out_shape=(...  5.58 us
    pallas_call x1, Pallas kernels, per_device(): pl.pallas_call(functools.partial(place_kernel, freqs, dirs, blocks), out_...  4.34 us
    ppermute x1, starting transfers between devices, per_device(): lax.ppermute(second, 'blk', outer)  3.05 us
    pallas_call x1, Pallas kernels, per_device(): pl.pallas_call(functools.partial(step_kernel, freqs, dirs, blocks), out_s...  2.94 us
    pallas_call x1, Pallas kernels, per_device(): pl.pallas_call(functools.partial(pick_kernel, freqs, dirs), out_shape=arr...  2.88 us
  transfers between devices with their start and end apart: 2, of which 0 were waited for; matrix products, arithmetic and copies ran while one was open for 0% of the time, Pallas kernels for 6%

profile of v8, /device:TPU:1, one launch (start us, length us, event | category | flops | bytes accessed | tf_op | source)
XLA Modules:
  0.0 77.1 jit_solution(2815358533103878323)
XLA Ops:
  0.7 5.6 %source.1 = (f32[1744,128]{1,0:T(8,128)}, s32[1,2048]{1,0:T(1,128)}) custom-call(s32[2]{0:T(128)} %shift_in.1, s32[1]{0:T(128)S(6)} %copy.8.count_in, f32[3,36,2048]{2,1,0:T(8,128)} %spec_in.1, f32[2,2048]{1,0:T(2,128)} %wind_in.1, s32[1,2048]{1,0:T(1,128)} %bitcast.10), custom_call_target="tpu_custom_call" | custom-call | tf_op jit(solution)/shard_map/source/pallas_call | solution.py:679
  6.2 29.8 %all_to_all.10 = f32[16,109,1,128]{3,2,1,0:T(1,128)S(1)} all-to-all(f32[16,109,1,128]{3,2,1,0:T(1,128)} %bitcast.9), channel_id=1, replica_groups=mesh['groups'=2,'blk'=16] {'blk'}, dimensions={0} | all-to-all | bytes 1785856 | tf_op jit(solution)/shard_map/all_to_all | solution.py:654
  36.1 1.4 %edges.1 = (f32[112,512]{1,0:T(8,128)S(1)}, f32[112,512]{1,0:T(8,128)S(1)}, s32[1,2048]{1,0:T(1,128)S(1)}) custom-call(f32[1744,128]{1,0:T(8,128)S(1)} %bitcast.5), custom_call_target="tpu_custom_call" | custom-call | tf_op jit(solution)/shard_map/edges/pallas_call | solution.py:699
  37.5 0.1 collective-permute-start
  37.5 3.1 %collective-permute-start.1 = (f32[112,512]{1,0:T(8,128)S(1)}, f32[112,512]{1,0:T(8,128)S(1)}, u32[]{:S(2)}, u32[]{:S(2)}) collective-permute-start(f32[112,512]{1,0:T(8,128)S(1)} %get-tuple-element.19), channel_id=1, source_target_pairs={{1,2},{2,1},{3,6},{6,3},{7,4},{4,7},{5,8},{8,5},{9,10},{10,9},{11,... | collective-permute-start | bytes 688136 | tf_op jit(solution)/shard_map/ppermute | solution.py:717
  40.6 4.3 %place.1 = (f32[120,2048]{1,0:T(8,128)S(1)}, f32[120,2048]{1,0:T(8,128)S(1)}, f32[120,2048]{1,0:T(8,128)S(1)}) custom-call(f32[1744,128]{1,0:T(8,128)S(1)} %bitcast.6, s32[1,2048]{1,0:T(1,128)S(1)} %get-tuple-element.14.cell_ref), custom_call_target="tpu_custom_call" | custom-call | flops 3019898880 | bytes 1966080 | tf_op jit(solution)/shard_map/place/pallas_call | solution.py:718
  44.9 0.0 collective-permute-done.first_ref
  45.0 0.0 collective-permute-done.1.second_ref
  45.0 2.9 %step.1 = f32[1728,128]{1,0:T(8,128)S(1)} custom-call(f32[120,2048]{1,0:T(8,128)S(1)} %get-tuple-element.15.field_ref, f32[120,2048]{1,0:T(8,128)S(1)} %get-tuple-element.16.mid_ref, f32[120,2048]{1,0:T(8,128)S(1)} %get-tuple-element.17.pre_ref, f32[112,512]{1,0:T(8,128)S(1)} %collective-permute-done.first_ref, ...), custom_call_target="tpu_custom_call" | custom-call | tf_op jit(solution)/shard_map/step/pallas_call | solution.py:735
  47.9 0.0 copy-start
  47.9 26.3 %all_to_all.11 = f32[16,108,1,128]{3,2,1,0:T(1,128)S(1)} all-to-all(f32[16,108,1,128]{3,2,1,0:T(1,128)S(1)} %bitcast.8), channel_id=1, replica_groups=mesh['groups'=2,'blk'=16] {'blk'}, dimensions={0} | all-to-all | bytes 1769472 | tf_op jit(solution)/shard_map/all_to_all | solution.py:654
  74.2 0.0 copy-done
  74.2 2.9 %pick.1 = f32[3,36,2048]{2,1,0:T(8,128)} custom-call(f32[1728,128]{1,0:T(8,128)S(1)} %bitcast.7, s32[1,2048]{1,0:T(1,128)S(1)} %copy-done), custom_call_target="tpu_custom_call" | custom-call | tf_op jit(solution)/shard_map/pick/pallas_call | solution.py:753
Async XLA Ops:
  37.5 7.5 %collective-permute-start = (f32[112,512]{1,0:T(8,128)S(1)}, f32[112,512]{1,0:T(8,128)S(1)}, u32[]{:S(2)}, u32[]{:S(2)}) collective-permute-start(f32[112,512]{1,0:T(8,128)S(1)} %get-tuple-element.18), channel_id=1, source_target_pairs={{0,1},{1,0},{2,3},{3,2},{6,7},{7,6},{4,5},{5,4},{8,9},{9,8},{10,11... | collective-permute-start | bytes 688136 | tf_op jit(solution)/shard_map/ppermute | solution.py:717
  37.5 7.4 %collective-permute-start.1 = (f32[112,512]{1,0:T(8,128)S(1)}, f32[112,512]{1,0:T(8,128)S(1)}, u32[]{:S(2)}, u32[]{:S(2)}) collective-permute-start(f32[112,512]{1,0:T(8,128)S(1)} %get-tuple-element.19), channel_id=1, source_target_pairs={{1,2},{2,1},{3,6},{6,3},{7,4},{4,7},{5,8},{8,5},{9,10},{10,9},{11,... | collective-permute-start | bytes 688136 | tf_op jit(solution)/shard_map/ppermute | solution.py:717
  47.9 26.3 %copy-start = (s32[1,2048]{1,0:T(1,128)S(1)}, s32[1,2048]{1,0:T(1,128)}, u32[]{:S(2)}) copy-start(s32[1,2048]{1,0:T(1,128)} %get-tuple-element.20.pos_ref) | copy-start | bytes 24580

commit v9 on v8

--- a/solution.py
+++ b/solution.py
@@ -12,7 +12,7 @@
 SUBSTEPS = 2
 LANES = 128
 TILE = 256
-GROUP = 512
+GROUP = 2048
 STRIDE = 40
 F32 = jnp.float32
 BF16 = jnp.bfloat16

time: 77.4 us -> 77.5 us (level)
  no operation moved by 1% of the time
where the time goes in v9:
time: 77.5 us; the launch traced here: 77.2 us
  blocking collectives  56.1 us (72%)
  Pallas kernels  17.2 us (22%)
  starting transfers between devices  3.14 us (4%)
    all_to_all x2, blocking collectives, exchange(): lax.all_to_all(parts, 'blk', split_axis=0, concat_axis=0, tiled=True)  56.1 us
    pallas_call x1, Pallas kernels, per_device(): pl.pallas_call(functools.partial(source_kernel, blocks, cap), out_shape=(...  5.7 us
    pallas_call x1, Pallas kernels, per_device(): pl.pallas_call(functools.partial(place_kernel, freqs, dirs, blocks), out_...  4.35 us
    ppermute x1, starting transfers between devices, per_device(): lax.ppermute(second, 'blk', outer)  3.07 us
    pallas_call x1, Pallas kernels, per_device(): pl.pallas_call(functools.partial(step_kernel, freqs, dirs, blocks), out_s...  2.94 us
    pallas_call x1, Pallas kernels, per_device(): pl.pallas_call(functools.partial(pick_kernel, freqs, dirs), out_shape=arr...  2.88 us
  transfers between devices with their start and end apart: 2, of which 0 were waited for; matrix products, arithmetic and copies ran while one was open for 0% of the time, Pallas kernels for 6%

profile of v9, /device:TPU:1, one launch (start us, length us, event | category | flops | bytes accessed | tf_op | source)
XLA Modules:
  0.0 77.2 jit_solution(10140470237209336206)
XLA Ops:
  0.7 5.7 %source.1 = (f32[1744,128]{1,0:T(8,128)}, s32[1,2048]{1,0:T(1,128)}) custom-call(s32[2]{0:T(128)} %shift_in.1, s32[1]{0:T(128)S(6)} %copy.8.count_in, f32[3,36,2048]{2,1,0:T(8,128)} %spec_in.1, f32[2,2048]{1,0:T(2,128)} %wind_in.1, s32[1,2048]{1,0:T(1,128)} %bitcast.10), custom_call_target="tpu_custom_call" | custom-call | tf_op jit(solution)/shard_map/source/pallas_call | solution.py:679
  6.4 29.8 %all_to_all.10 = f32[16,109,1,128]{3,2,1,0:T(1,128)S(1)} all-to-all(f32[16,109,1,128]{3,2,1,0:T(1,128)} %bitcast.9), channel_id=1, replica_groups=mesh['groups'=2,'blk'=16] {'blk'}, dimensions={0} | all-to-all | bytes 1785856 | tf_op jit(solution)/shard_map/all_to_all | solution.py:654
  36.2 1.4 %edges.1 = (f32[112,512]{1,0:T(8,128)S(1)}, f32[112,512]{1,0:T(8,128)S(1)}, s32[1,2048]{1,0:T(1,128)S(1)}) custom-call(f32[1744,128]{1,0:T(8,128)S(1)} %bitcast.5), custom_call_target="tpu_custom_call" | custom-call | tf_op jit(solution)/shard_map/edges/pallas_call | solution.py:699
  37.6 0.1 collective-permute-start
  37.6 3.1 %collective-permute-start.1 = (f32[112,512]{1,0:T(8,128)S(1)}, f32[112,512]{1,0:T(8,128)S(1)}, u32[]{:S(2)}, u32[]{:S(2)}) collective-permute-start(f32[112,512]{1,0:T(8,128)S(1)} %get-tuple-element.19), channel_id=1, source_target_pairs={{1,2},{2,1},{3,6},{6,3},{7,4},{4,7},{5,8},{8,5},{9,10},{10,9},{11,... | collective-permute-start | bytes 688136 | tf_op jit(solution)/shard_map/ppermute | solution.py:717
  40.7 4.3 %place.1 = (f32[120,2048]{1,0:T(8,128)S(1)}, f32[120,2048]{1,0:T(8,128)S(1)}, f32[120,2048]{1,0:T(8,128)S(1)}) custom-call(f32[1744,128]{1,0:T(8,128)S(1)} %bitcast.6, s32[1,2048]{1,0:T(1,128)S(1)} %get-tuple-element.14.cell_ref), custom_call_target="tpu_custom_call" | custom-call | flops 3019898880 | bytes 1966080 | tf_op jit(solution)/shard_map/place/pallas_call | solution.py:718
  45.1 0.0 collective-permute-done.first_ref
  45.1 0.0 collective-permute-done.1.second_ref
  45.1 2.9 %step.1 = f32[1728,128]{1,0:T(8,128)S(1)} custom-call(f32[120,2048]{1,0:T(8,128)S(1)} %get-tuple-element.15.field_ref, f32[120,2048]{1,0:T(8,128)S(1)} %get-tuple-element.16.mid_ref, f32[120,2048]{1,0:T(8,128)S(1)} %get-tuple-element.17.pre_ref, f32[112,512]{1,0:T(8,128)S(1)} %collective-permute-done.first_ref, ...), custom_call_target="tpu_custom_call" | custom-call | tf_op jit(solution)/shard_map/step/pallas_call | solution.py:735
  48.0 0.0 copy-start
  48.0 26.3 %all_to_all.11 = f32[16,108,1,128]{3,2,1,0:T(1,128)S(1)} all-to-all(f32[16,108,1,128]{3,2,1,0:T(1,128)S(1)} %bitcast.8), channel_id=1, replica_groups=mesh['groups'=2,'blk'=16] {'blk'}, dimensions={0} | all-to-all | bytes 1769472 | tf_op jit(solution)/shard_map/all_to_all | solution.py:654
  74.4 0.0 copy-done
  74.4 2.9 %pick.1 = f32[3,36,2048]{2,1,0:T(8,128)} custom-call(f32[1728,128]{1,0:T(8,128)S(1)} %bitcast.7, s32[1,2048]{1,0:T(1,128)S(1)} %copy-done), custom_call_target="tpu_custom_call" | custom-call | tf_op jit(solution)/shard_map/pick/pallas_call | solution.py:753
Async XLA Ops:
  37.6 7.5 %collective-permute-start = (f32[112,512]{1,0:T(8,128)S(1)}, f32[112,512]{1,0:T(8,128)S(1)}, u32[]{:S(2)}, u32[]{:S(2)}) collective-permute-start(f32[112,512]{1,0:T(8,128)S(1)} %get-tuple-element.18), channel_id=1, source_target_pairs={{0,1},{1,0},{2,3},{3,2},{6,7},{7,6},{4,5},{5,4},{8,9},{9,8},{10,11... | collective-permute-start | bytes 688136 | tf_op jit(solution)/shard_map/ppermute | solution.py:717
  37.6 7.4 %collective-permute-start.1 = (f32[112,512]{1,0:T(8,128)S(1)}, f32[112,512]{1,0:T(8,128)S(1)}, u32[]{:S(2)}, u32[]{:S(2)}) collective-permute-start(f32[112,512]{1,0:T(8,128)S(1)} %get-tuple-element.19), channel_id=1, source_target_pairs={{1,2},{2,1},{3,6},{6,3},{7,4},{4,7},{5,8},{8,5},{9,10},{10,9},{11,... | collective-permute-start | bytes 688136 | tf_op jit(solution)/shard_map/ppermute | solution.py:717
  48.0 26.3 %copy-start = (s32[1,2048]{1,0:T(1,128)S(1)}, s32[1,2048]{1,0:T(1,128)}, u32[]{:S(2)}) copy-start(s32[1,2048]{1,0:T(1,128)} %get-tuple-element.20.pos_ref) | copy-start | bytes 24580
